TPU v7x, 32 devices: a whole 2x2x4 slice. The times are simulated.
32 devices in a mesh: subtree: 4 (over z), forest: 8 (over y, x, core).
Axes of the slice: x: 2, y: 2, z: 4, core: 2. Of those that a mesh axis runs over, the one named last changes fastest.
Arguments:
- panels: bfloat16 [4, 8, 1024, 2048], P('subtree', 'forest'), may hold values from -0.75 to 0.75
- pattern: int32 [4, 8, 8, 8], P('subtree', 'forest'), may hold values from 0 to 1, as said below
- child_map: int32 [4, 8, 8], P('subtree', 'forest'), may hold values from 0 to 7, each once within a row
- ancestor_map: int32 [4, 8, 8], P('subtree', 'forest'), may hold values from 0 to 23, as said below
Outputs:
- ancestors: float32 [4, 24, 256, 128], P('subtree', 'forest')
Inputs may be any that keep to these rules, and one draw needn't show every extreme that they name: pattern[s, f, i, j] = pattern[s, f, i, i] * pattern[s, f, j, j], so each pattern is symmetric; every panel has at least one occupied and at least one empty block row. No two entries of ancestor_map[s, f, :] have the same value of entry // 3.
All inputs are finite; a program needn't handle non-finite values.
Results may differ from a plain program's by a relative error of at most 0.0003.
Values sent between devices are 32-bit elements; how exact they have to be, the bound alone decides.
No kernel may reach another device: no remote copies, remote signals or barrier semaphores. Data moves between devices by JAX's collectives and lax.ppermute only.
A program may use at most 64 MiB of HBM per device.

v0:
```python
import jax
import jax.numpy as jnp
from jax import lax
from jax.sharding import PartitionSpec as P

ANC_DEV = 3


def swapped(shard, axis, apart):
    return lax.ppermute(shard, axis, [(i, i ^ 1 << apart) for i in range(lax.axis_size(axis))])


def per_device(panels, pattern, child_map, ancestor_map):
    row_total = panels.shape[2]
    pivot_width = panels.shape[3]
    block_count = child_map.shape[2]
    block_rows = row_total // block_count
    blocks = panels[0, 0].reshape(block_count, block_rows, pivot_width)
    one_hot = child_map[0, 0][:, None] == jnp.arange(block_count, dtype=jnp.int32)[None, :]
    reordered = jnp.einsum(
        "im,ipk->mpk", one_hot.astype(jnp.bfloat16), blocks, preferred_element_type=jnp.float32
    ).astype(jnp.bfloat16)
    flat_rows = reordered.reshape(row_total, pivot_width)
    hot_float = one_hot.astype(jnp.float32)
    moved_pattern = jnp.dot(
        jnp.dot(hot_float.T, pattern[0, 0].astype(jnp.float32), precision=lax.Precision.HIGHEST),
        hot_float,
        precision=lax.Precision.HIGHEST,
    )
    update = lax.dot_general(
        flat_rows, flat_rows, (((1,), (1,)), ((), ())), preferred_element_type=jnp.float32
    )
    update = (
        update.reshape(block_count, block_rows, block_count, block_rows)
        * moved_pattern[:, None, :, None]
    ).reshape(row_total, row_total)
    sub_count = lax.axis_size("subtree")
    depth = sub_count.bit_length() - 1
    my_index = lax.axis_index("subtree")
    holding = update
    for depth_step in range(depth):
        bit_number = depth - 1 - depth_step
        half_rows = holding.shape[0] // 2
        low_half = holding[:half_rows]
        high_half = holding[half_rows:]
        high_side = my_index >> bit_number & 1 == 1
        kept_half = jnp.where(high_side, high_half, low_half)
        sent_half = jnp.where(high_side, low_half, high_half)
        holding = kept_half + swapped(sent_half, "subtree", bit_number)
    piece_rows = holding.shape[0]
    column_blocks = holding.reshape(piece_rows, block_count, block_rows).transpose(1, 0, 2)
    slot_values = ancestor_map[0, 0]
    tree_count = lax.axis_size("forest")
    every_slot = lax.all_gather(slot_values, "forest", axis=0, tiled=True)
    owner_of = slot_values // ANC_DEV
    owner_hot = (owner_of[:, None] == jnp.arange(tree_count, dtype=jnp.int32)[None, :]).astype(
        jnp.float32
    )
    outgoing = jnp.einsum("co,cpq->opq", owner_hot, column_blocks, precision=lax.Precision.HIGHEST)
    incoming = lax.all_to_all(outgoing, "forest", split_axis=0, concat_axis=0, tiled=True)
    forest_index = lax.axis_index("forest")
    every_slot = every_slot.reshape(tree_count, block_count)
    mine_mask = every_slot // ANC_DEV == forest_index
    local_slot = every_slot % ANC_DEV
    source_hot = jnp.sum(
        jnp.where(
            mine_mask[:, :, None],
            (local_slot[:, :, None] == jnp.arange(ANC_DEV, dtype=jnp.int32)[None, None, :]).astype(
                jnp.float32
            ),
            0.0,
        ),
        axis=1,
    )
    summed = jnp.einsum("sk,spq->kpq", source_hot, incoming, precision=lax.Precision.HIGHEST)
    return summed[None]


def solution(mesh):
    in_specs = (
        P("subtree", "forest", None, None),
        P("subtree", "forest", None, None),
        P("subtree", "forest", None),
        P("subtree", "forest", None),
    )
    out_specs = P("subtree", "forest", None, None)
    return jax.shard_map(
        per_device, mesh=mesh, in_specs=in_specs, out_specs=out_specs, check_vma=False
    )
```

profile of v0, /device:TPU:0, one launch (start us, length us, event | category | flops | bytes accessed | tf_op | source)
XLA Modules:
  0.0 180.3 jit_solution(6584591107351705309)
XLA Ops:
  0.0 0.8 fusion.18
  0.8 0.8 fusion.21
  1.6 7.0 %fusion.6 = bf16[8,128,2048]{2,0,1:T(8,128)(2,1)} fusion(bf16[8,128,2048]{2,1,0:T(8,128)(2,1)} %bitcast.48, s32[8]{0:T(128)} %bitcast.52), kind=kOutput, calls=%fused_computation.6 | convolution fusion | flops 35651648 | bytes 8388640 | tf_op jit(solution)/shard_map/im,ipk->mpk/dot_general | solution.py:20
  8.6 20.1 %fusion.9 = f32[8,128,8,128]{3,1,2,0:T(8,128)S(1)} fusion(bf16[8,128,2048]{2,0,1:T(8,128)(2,1)} %fusion.6, bf16[8,128,2048,1]{2,0,1,3:T(8,128)(2,1)} %bitcast.49, f32[8,8]{1,0:T(8,128)S(1)} %fusion.21), kind=kOutput, calls=%fused_computation.7 | convolution fusion | flops 4296015872 | bytes 12583168 | tf_op jit(solution)/shard_map/dot_general | solution.py:30
  28.8 0.3 slice_select_fusion.1
  29.1 1.2 copy.21
  30.3 1.8 copy.49
  32.1 4.0 %collective-permute-start = (f32[512,1024]{1,0:T(8,128)}, f32[512,1024]{1,0:T(8,128)S(1)}, u32[]{:S(2)}, u32[]{:S(2)}) collective-permute-start(f32[512,1024]{1,0:T(8,128)} %bitcast.44), channel_id=1, source_target_pairs={{0,16},{8,24},{16,0},{24,8},{1,17},{9,25},{17,1},{25,9},{2,18},{10... | collective-permute-start | bytes 6291464 | tf_op jit(solution)/shard_map/ppermute | solution.py:10
  36.1 2.5 %copy.20 = f32[4,128,8,128]{3,2,1,0:T(8,128)} copy(f32[4,128,8,128]{3,1,2,0:T(8,128)S(1)} %get-tuple-element.5) | data formatting | bytes 4194304 | tf_op jit(solution)/shard_map/jit(_where)/select_n | solution.py:47
  38.7 88.2 %collective-permute-done = f32[512,1024]{1,0:T(8,128)S(1)} collective-permute-done((f32[512,1024]{1,0:T(8,128)}, f32[512,1024]{1,0:T(8,128)S(1)}, u32[]{:S(2)}, u32[]{:S(2)}) %collective-permute-start) | collective-permute-done | bytes 2097184 | tf_op jit(solution)/shard_map/ppermute | solution.py:10
  126.9 1.3 copy-done
  128.2 3.0 %bitcast_add_fusion = f32[512,1024]{1,0:T(8,128)S(1)} fusion(f32[512,1024]{1,0:T(8,128)} %copy-done, f32[64,8,8,128]{3,2,1,0:T(8,128)} %bitcast.45), kind=kLoop, calls=%fused_computation.9 | loop fusion | flops 524288 | bytes 6291456 | tf_op jit(solution)/shard_map/add | solution.py:49
  131.2 1.1 slice_select_fusion.2
  132.3 0.8 collective-permute-start.1
  133.1 0.0 copy-done.2
  133.1 0.6 dynamic-slice
  134.4 0.0 copy-done.1
  134.4 0.1 bitcast_dynamic-update-slice_fusion
  134.5 8.0 %all-reduce = s32[64]{0:T(128)S(1)} all-reduce(s32[64]{0:T(128)S(1)} %get-tuple-element.9), channel_id=2, replica_groups=mesh['subtree'=4,'forest'=8] {'forest'}, use_global_device_ids=true, to_apply=%add | all-reduce | flops 64 | bytes 512
  142.5 14.4 %collective-permute-done.1 = f32[256,1024]{1,0:T(8,128)S(1)} collective-permute-done((f32[256,1024]{1,0:T(8,128)}, f32[256,1024]{1,0:T(8,128)S(1)}, u32[]{:S(2)}, u32[]{:S(2)}) %collective-permute-start.1) | collective-permute-done | bytes 1048608 | tf_op jit(solution)/shard_map/ppermute | solution.py:10
  156.9 0.3 add_bitcast_fusion
  157.1 0.2 copy.30
  157.4 0.6 fusion.14
  158.0 1.2 copy.22
  159.1 3.6 %all-to-all-start = ((f32[8,256,128]{2,1,0:T(8,128)}), f32[8,256,128]{2,1,0:T(8,128)S(1)}, u32[]{:S(2)}, u32[]{:S(2)}) async-start(f32[8,256,128]{2,1,0:T(8,128)} %copy.22), calls=%async_computation | async-start | bytes 2097152 | tf_op jit(solution)/shard_map/all_to_all | solution.py:60
  162.7 0.1 rem.38
  162.8 0.1 div.24
  162.9 0.1 ne.62
  163.0 0.1 select_reduce_fusion
  163.1 15.0 %all-to-all-done = f32[8,256,128]{2,1,0:T(8,128)S(1)} async-done(((f32[8,256,128]{2,1,0:T(8,128)}), f32[8,256,128]{2,1,0:T(8,128)S(1)}, u32[]{:S(2)}, u32[]{:S(2)}) %all-to-all-start) | async-done | bytes 1048608 | tf_op jit(solution)/shard_map/all_to_all | solution.py:60
  178.1 1.5 convolution_bitcast_fusion
  179.6 0.8 copy.24
  (8 shorter events, 0.0 us)
Async XLA Ops:
  32.1 94.8 %collective-permute-start = (f32[512,1024]{1,0:T(8,128)}, f32[512,1024]{1,0:T(8,128)S(1)}, u32[]{:S(2)}, u32[]{:S(2)}) collective-permute-start(f32[512,1024]{1,0:T(8,128)} %bitcast.44), channel_id=1, source_target_pairs={{0,16},{8,24},{16,0},{24,8},{1,17},{9,25},{17,1},{25,9},{2,18},{10... | collective-permute-start | bytes 6291464 | tf_op jit(solution)/shard_map/ppermute | solution.py:10
  126.9 1.3 copy-start
  128.2 4.9 %copy-start.2 = (u32[32]{0:T(128)S(1)}, u32[32]{0:T(128)}, u32[]{:S(2)}) copy-start(u32[32]{0:T(128)} %constant.43) | copy-start | bytes 388
  128.2 6.2 %copy-start.1 = (s32[1,1,8]{2,1,0:T(1,128)S(1)}, s32[1,1,8]{2,1,0:T(1,128)}, u32[]{:S(2)}) copy-start(s32[1,1,8]{2,1,0:T(1,128)} %param.7) | copy-start | bytes 100
  132.3 24.6 %collective-permute-start.1 = (f32[256,1024]{1,0:T(8,128)}, f32[256,1024]{1,0:T(8,128)S(1)}, u32[]{:S(2)}, u32[]{:S(2)}) collective-permute-start(f32[256,1024]{1,0:T(8,128)} %slice_select_fusion.2), channel_id=1, source_target_pairs={{0,8},{8,0},{16,24},{24,16},{1,9},{9,1},{17,25},{25,17},{2,10},{10... | collective-permute-start | bytes 3145736 | tf_op jit(solution)/shard_map/ppermute | solution.py:10
  159.1 19.0 %all-to-all-start = ((f32[8,256,128]{2,1,0:T(8,128)}), f32[8,256,128]{2,1,0:T(8,128)S(1)}, u32[]{:S(2)}, u32[]{:S(2)}) async-start(f32[8,256,128]{2,1,0:T(8,128)} %copy.22), calls=%async_computation | async-start | bytes 2097152 | tf_op jit(solution)/shard_map/all_to_all | solution.py:60
where the time goes:
time: 181 us; the launch traced here: 180 us
  waiting for transfers between devices  118 us (65%)
  matrix products  30.8 us (17%)
  local copies, waits for them, and re-layouts  9.8 us (5%)
  starting transfers between devices  8.43 us (5%)
  blocking collectives  8.01 us (4%)
  other arithmetic  4.89 us (3%)
    ppermute x2, waiting for transfers between devices, swapped(): lax.ppermute(shard, axis, [(i, i ^ 1 << apart) for i in range(lax.axis_si...  103 us
    dot_general x1, matrix products, per_device(): lax.dot_general(flat_rows, flat_rows, (((1,), (1,)), ((), ())), preferred...  20.1 us
    all_to_all x1, waiting for transfers between devices, per_device(): lax.all_to_all(outgoing, 'forest', split_axis=0, concat_axis=0, tiled=True)  15 us
    unnamed x1, blocking collectives  8.01 us
    dot_general x1, matrix products, per_device(): jnp.einsum('im,ipk->mpk', one_hot.astype(jnp.bfloat16), blocks, preferred...  7.03 us
    ppermute x2, starting transfers between devices, swapped(): lax.ppermute(shard, axis, [(i, i ^ 1 << apart) for i in range(lax.axis_si...  4.87 us
    unnamed x10, local copies, waits for them, and re-layouts  3.87 us
  transfers between devices with their start and end apart: 3, of which 3 were waited for; matrix products, arithmetic and copies ran while one was open for 2% of the time, Pallas kernels for 0%

commit v1 on v0

--- a/solution.py
+++ b/solution.py
@@ -1,16 +1,232 @@
+import functools
+
 import jax
 import jax.numpy as jnp
 from jax import lax
+from jax.experimental import pallas as pl
+from jax.experimental.pallas import tpu as pltpu
 from jax.sharding import PartitionSpec as P
 
 ANC_DEV = 3
+META = 8
+CUT = 16
+CHUNK_PARTS = (3, 3, 2)
+VMEM_LIMIT = 44 * 1024 * 1024
 
 
 def swapped(shard, axis, apart):
-    return lax.ppermute(shard, axis, [(i, i ^ 1 << apart) for i in range(lax.axis_size(axis))])
-
-
-def per_device(panels, pattern, child_map, ancestor_map):
+    return lax.ppermute(shard, axis, [(i, i ^ apart) for i in range(lax.axis_size(axis))])
+
+
+def smem_spec():
+    return pl.BlockSpec(memory_space=pltpu.SMEM)
+
+
+def vmem_spec():
+    return pl.BlockSpec(memory_space=pltpu.VMEM)
+
+
+def first_empty(nb, per_piece, my_sub, child_ref, pattern_ref, inverse):
+    for i in range(nb):
+        inverse[child_ref[0, 0, i]] = i
+    empty = jnp.int32(nb - 1)
+    for place in range(nb - 1, -1, -1):
+        i = inverse[position_of(place, per_piece, my_sub)]
+        empty = jnp.where(pattern_ref[0, 0, i, i] == 0, jnp.int32(place), empty)
+    return empty
+
+
+def position_of(place, per_piece, my_sub):
+    return ((place // per_piece) ^ my_sub) * per_piece + place % per_piece
+
+
+def multiply_kernel(nb, per_piece, chunk_rows, child_ref, pattern_ref, panel_ref, *refs):
+    out_refs = refs[: len(chunk_rows)]
+    left, inverse = refs[len(chunk_rows) :]
+    block = panel_ref.shape[0] // nb
+    my_sub = lax.axis_index("subtree")
+    empty = first_empty(nb, per_piece, my_sub, child_ref, pattern_ref, inverse)
+    rows = []
+    for k in range(nb - 1):
+        place = k + (empty <= k).astype(jnp.int32)
+        rows.append(inverse[position_of(place, per_piece, my_sub)])
+    start = 0
+    at = 0
+    for count in chunk_rows:
+        for k in range(nb - 1):
+            source = pl.multiple_of(rows[k] * block + start, CUT)
+            left[pl.ds(at, count), :] = panel_ref[pl.ds(source, count), :]
+            at += count
+        start += count
+    wide = 2 * block if nb % 2 == 0 else block
+    for n in range(nb * block // wide):
+        product = lax.dot_general(
+            left[...],
+            panel_ref[pl.ds(n * wide, wide), :],
+            (((1,), (1,)), ((), ())),
+            preferred_element_type=jnp.float32,
+        )
+        at = 0
+        for out_ref, count in zip(out_refs, chunk_rows):
+            for k in range(nb - 1):
+                for part in range(wide // block):
+                    j = n * (wide // block) + part
+                    scale = pattern_ref[0, 0, rows[k], j].astype(jnp.float32)
+                    out_ref[k, :, pl.ds(j * block, block)] = (
+                        product[at : at + count, part * block : (part + 1) * block] * scale
+                    )
+                at += count
+
+
+def route_kernel(nb, per_piece, subs, child_ref, pattern_ref, *refs):
+    slot_refs = refs[:subs]
+    update_ref, same_ref, other_ref, inverse, goal = refs[subs:]
+    count = update_ref.shape[1]
+    block = same_ref.shape[2]
+    my_sub = lax.axis_index("subtree")
+    my_tree = lax.axis_index("forest")
+    empty = first_empty(nb, per_piece, my_sub, child_ref, pattern_ref, inverse)
+    tail = (nb - 1) * count
+    same_ref[:, pl.ds(tail, META), :] = jnp.zeros((same_ref.shape[0], META, block), jnp.float32)
+    other_ref[:, pl.ds(tail, META), :] = jnp.zeros((same_ref.shape[0], META, block), jnp.float32)
+    mark = jnp.full((same_ref.shape[0], 1, block), empty.astype(jnp.float32), jnp.float32)
+    same_ref[:, pl.ds(tail, 1), :] = mark
+    other_ref[:, pl.ds(tail, 1), :] = mark
+    for apart in range(subs):
+        for j in range(nb):
+            entry = slot_refs[apart][0, 0, child_ref[0, 0, j]]
+            owner = lax.div(entry, ANC_DEV)
+            to = owner ^ my_tree
+            goal[apart, j] = to
+            slot = (entry - owner * ANC_DEV).astype(jnp.float32)
+            row = jnp.full((1, block), slot, jnp.float32)
+
+            @pl.when(to & 1 == 0)
+            def _():
+                same_ref[to >> 1, pl.ds(tail + 1 + apart, 1), :] = row
+
+            @pl.when(to & 1 == 1)
+            def _():
+                other_ref[to >> 1, pl.ds(tail + 1 + apart, 1), :] = row
+
+    for k in range(nb - 1):
+        place = k + (empty <= k).astype(jnp.int32)
+        apart = place // per_piece
+        for j in range(nb):
+            to = goal[apart, j]
+
+            @pl.when(to & 1 == 0)
+            def _():
+                same_ref[to >> 1, pl.ds(k * count, count), :] = update_ref[k, :, pl.ds(j * block, block)]
+
+            @pl.when(to & 1 == 1)
+            def _():
+                other_ref[to >> 1, pl.ds(k * count, count), :] = update_ref[k, :, pl.ds(j * block, block)]
+
+
+def gather_kernel(nb, per_piece, count, *refs):
+    subs = nb // per_piece
+    in_refs, out_refs = refs[:-subs], refs[-subs:]
+    tail = (nb - 1) * count
+    block = in_refs[0].shape[-1]
+    sources = []
+    for ref in in_refs:
+        for index in range(ref.shape[0]):
+            sources.append(ref.at[index])
+    for apart in range(subs):
+        for part in range(per_piece):
+            place = apart * per_piece + part
+            sums = [jnp.zeros((count, block), jnp.float32) for _ in range(ANC_DEV)]
+            for source in sources:
+                empty = source[pl.ds(tail, 1), :]
+                slot = source[pl.ds(tail + 1 + apart, 1), :]
+                low = source[pl.ds(min(place, nb - 2) * count, count), :]
+                high = source[pl.ds(max(place - 1, 0) * count, count), :]
+                value = jnp.where(empty > place, low, jnp.where(empty < place, high, 0.0))
+                for index in range(ANC_DEV):
+                    sums[index] += jnp.where(slot == index, value, 0.0)
+            for index in range(ANC_DEV):
+                out_refs[apart][index, part] = sums[index]
+
+
+def finish_kernel(subs, chunk_rows, *refs):
+    out_ref = refs[-1]
+    start = 0
+    for c, count in enumerate(chunk_rows):
+        parts = refs[c * subs : (c + 1) * subs]
+        total = parts[0][...]
+        for part in parts[1:]:
+            total += part[...]
+        out_ref[0, :, :, pl.ds(start, count), :] = total
+        start += count
+
+
+def per_device_blocks(panels, pattern, child_map, ancestor_map):
+    row_total, pivot_width = panels.shape[2:]
+    nb = child_map.shape[2]
+    block = row_total // nb
+    subs = lax.axis_size("subtree")
+    trees = lax.axis_size("forest")
+    per_piece = nb // subs
+    units = block // CUT
+    chunk_rows = []
+    for index, share in enumerate(CHUNK_PARTS):
+        chunk_rows.append(units * share // sum(CHUNK_PARTS) * CUT)
+    chunk_rows[-1] += block - sum(chunk_rows)
+    chips = trees // 2
+    params = pltpu.CompilerParams(vmem_limit_bytes=VMEM_LIMIT)
+
+    slots = [ancestor_map] + [swapped(ancestor_map, "subtree", apart) for apart in range(1, subs)]
+    updates = pl.pallas_call(
+        functools.partial(multiply_kernel, nb, per_piece, chunk_rows),
+        out_shape=[jax.ShapeDtypeStruct((nb - 1, count, row_total), jnp.float32) for count in chunk_rows],
+        in_specs=[smem_spec(), smem_spec(), vmem_spec()],
+        out_specs=[vmem_spec()] * len(chunk_rows),
+        scratch_shapes=[
+            pltpu.VMEM(((nb - 1) * block, pivot_width), jnp.bfloat16),
+            pltpu.SMEM((nb,), jnp.int32),
+        ],
+        compiler_params=params,
+    )(child_map, pattern, panels.reshape(row_total, pivot_width))
+
+    pieces = []
+    for count, update in zip(chunk_rows, updates):
+        rows = (nb - 1) * count + META
+        same, other = pl.pallas_call(
+            functools.partial(route_kernel, nb, per_piece, subs),
+            out_shape=[jax.ShapeDtypeStruct((chips, rows, block), jnp.float32)] * 2,
+            in_specs=[smem_spec()] * (2 + subs) + [vmem_spec()],
+            out_specs=[vmem_spec()] * 2,
+            scratch_shapes=[pltpu.SMEM((nb,), jnp.int32), pltpu.SMEM((subs, nb), jnp.int32)],
+            compiler_params=params,
+        )(child_map, pattern, *slots, update)
+        crossed = swapped(other, "forest", 1)
+        arrived = [same[:1], crossed[:1]]
+        for chip in range(1, chips):
+            both = jnp.stack([same[chip], crossed[chip]])
+            arrived.append(swapped(both, "forest", 2 * chip))
+        piece_shape = jax.ShapeDtypeStruct((ANC_DEV, per_piece, count, block), jnp.float32)
+        sums = pl.pallas_call(
+            functools.partial(gather_kernel, nb, per_piece, count),
+            out_shape=[piece_shape] * subs,
+            in_specs=[vmem_spec()] * len(arrived),
+            out_specs=[vmem_spec()] * subs,
+            compiler_params=params,
+        )(*arrived)
+        pieces.append(sums[0])
+        for apart in range(1, subs):
+            pieces.append(swapped(sums[apart], "subtree", apart))
+    out = pl.pallas_call(
+        functools.partial(finish_kernel, subs, chunk_rows),
+        out_shape=jax.ShapeDtypeStruct((1, ANC_DEV, per_piece, block, block), jnp.float32),
+        in_specs=[vmem_spec()] * len(pieces),
+        out_specs=vmem_spec(),
+        compiler_params=params,
+    )(*pieces)
+    return out.reshape(1, ANC_DEV, per_piece * block, block)
+
+
+def per_device_halving(panels, pattern, child_map, ancestor_map):
     row_total = panels.shape[2]
     pivot_width = panels.shape[3]
     block_count = child_map.shape[2]
@@ -46,7 +262,7 @@
         high_side = my_index >> bit_number & 1 == 1
         kept_half = jnp.where(high_side, high_half, low_half)
         sent_half = jnp.where(high_side, low_half, high_half)
-        holding = kept_half + swapped(sent_half, "subtree", bit_number)
+        holding = kept_half + swapped(sent_half, "subtree", 1 << bit_number)
     piece_rows = holding.shape[0]
     column_blocks = holding.reshape(piece_rows, block_count, block_rows).transpose(1, 0, 2)
     slot_values = ancestor_map[0, 0]
@@ -84,6 +300,14 @@
         P("subtree", "forest", None),
     )
     out_specs = P("subtree", "forest", None, None)
+
+    def per_device(panels, pattern, child_map, ancestor_map):
+        nb = child_map.shape[2]
+        subs, trees = mesh.shape["subtree"], mesh.shape["forest"]
+        if nb == trees and nb % subs == 0 and subs < META and trees % 2 == 0:
+            return per_device_blocks(panels, pattern, child_map, ancestor_map)
+        return per_device_halving(panels, pattern, child_map, ancestor_map)
+
     return jax.shard_map(
         per_device, mesh=mesh, in_specs=in_specs, out_specs=out_specs, check_vma=False
     )

time: 181 us -> 106 us (0.59)
  waiting for transfers between devices: 118 us -> 52 us
  matrix products: 30.8 us -> 0 us
  starting transfers between devices: 8.43 us -> 35.3 us
  Pallas kernels: 0 us -> 13.9 us
  blocking collectives: 8.01 us -> 0 us
  local copies, waits for them, and re-layouts: 9.8 us -> 3.79 us
  other arithmetic: 4.89 us -> 0.23 us
    ppermute x2 -> x24, waiting for transfers between devices: 103 us -> 52 us  [swapped(): lax.ppermute(shard, axis, [(i, i ^ apart) for i in range(lax.axis_size(ax...]
    dot_general x6 -> x0, matrix products: 30.8 us -> none  [the longest x1 20.1 us: per_device(): lax.dot_general(flat_rows, flat_rows, (((1,), (1,)), ((), ())), preferred...]
    ppermute x2 -> x24, starting transfers between devices: 4.87 us -> 35.3 us  [swapped(): lax.ppermute(shard, axis, [(i, i ^ apart) for i in range(lax.axis_size(ax...]
    all_to_all x1 -> x0, waiting for transfers between devices: 15 us -> none  [per_device(): lax.all_to_all(outgoing, 'forest', split_axis=0, concat_axis=0, tiled=True)]
    pallas_call x0 -> x8, Pallas kernels: none -> 13.9 us  [the longest x3 6.58 us: per_device_blocks(): pl.pallas_call(functools.partial(route_kernel, nb, per_piece, subs), out_...]
    unnamed x1 -> x0, blocking collectives: 8.01 us -> none
    select_n x2 -> x0, local copies, waits for them, and re-layouts: 3.76 us -> none  [the longest x1 2.54 us: per_device(): kept_half = jnp.where(high_side, high_half, low_half)]
    all_to_all x1 -> x0, starting transfers between devices: 3.56 us -> none  [per_device(): lax.all_to_all(outgoing, 'forest', split_axis=0, concat_axis=0, tiled=True)]
  transfers between devices with their start and end apart: 3 -> 24, of which waited for: 3 -> 8; matrix products, arithmetic and copies ran while one was open for 2% -> 0% of each run, Pallas kernels for 0% -> 10%
where the time goes in v1:
time: 106 us; the launch traced here: 105 us
  waiting for transfers between devices  52 us (49%)
  starting transfers between devices  35.3 us (33%)
  Pallas kernels  13.9 us (13%)
  local copies, waits for them, and re-layouts  3.79 us (4%)
    ppermute x24, waiting for transfers between devices, swapped(): lax.ppermute(shard, axis, [(i, i ^ apart) for i in range(lax.axis_size(ax...  52 us
    ppermute x24, starting transfers between devices, swapped(): lax.ppermute(shard, axis, [(i, i ^ apart) for i in range(lax.axis_size(ax...  35.3 us
    pallas_call x3, Pallas kernels, per_device_blocks(): pl.pallas_call(functools.partial(route_kernel, nb, per_piece, subs), out_...  6.58 us
    pallas_call x1, Pallas kernels, per_device_blocks(): pl.pallas_call(functools.partial(multiply_kernel, nb, per_piece, chunk_ro...  4.59 us
    unnamed x8, local copies, waits for them, and re-layouts  3.53 us
  transfers between devices with their start and end apart: 24, of which 8 were waited for; matrix products, arithmetic and copies ran while one was open for 0% of the time, Pallas kernels for 10%

profile of v1, /device:TPU:0, one launch (start us, length us, event | category | flops | bytes accessed | tf_op | source)
XLA Modules:
  0.0 105.4 jit_solution(5504811451493265131)
XLA Ops:
  0.0 3.0 %collective-permute-start = (s32[1,1,8]{2,1,0:T(1,128)}, s32[1,1,8]{2,1,0:T(1,128)S(1)}, u32[]{:S(2)}, u32[]{:S(2)}) collective-permute-start(s32[1,1,8]{2,1,0:T(1,128)} %refs_0_.5), channel_id=1, source_target_pairs={{0,8},{8,0},{16,24},{24,16},{1,9},{9,1},{17,25},{25,17},{2,10},{10... | collective-permute-start | bytes 104 | tf_op jit(solution)/shard_map/ppermute | solution.py:18
  3.0 2.6 %collective-permute-start.1 = (s32[1,1,8]{2,1,0:T(1,128)}, s32[1,1,8]{2,1,0:T(1,128)S(1)}, u32[]{:S(2)}, u32[]{:S(2)}) collective-permute-start(s32[1,1,8]{2,1,0:T(1,128)} %refs_0_.5), channel_id=1, source_target_pairs={{0,16},{8,24},{16,0},{24,8},{1,17},{9,25},{17,1},{25,9},{2,18},{10... | collective-permute-start | bytes 104 | tf_op jit(solution)/shard_map/ppermute | solution.py:18
  5.6 2.2 %copy-done = bf16[1,1,1024,2048]{3,2,1,0:T(8,128)(2,1)S(1)} copy-done((bf16[1,1,1024,2048]{3,2,1,0:T(8,128)(2,1)S(1)}, bf16[1,1,1024,2048]{3,2,1,0:T(8,128)(2,1)}, u32[]{:S(2)}) %copy-start) | copy-done | bytes 4194328
  7.8 0.7 copy-done.1
  8.5 0.7 copy-done.2
  9.2 4.6 %shard_map.46 = (f32[7,48,1024]{2,1,0:T(8,128)S(1)}, f32[7,48,1024]{2,1,0:T(8,128)S(1)}, f32[7,32,1024]{2,1,0:T(8,128)S(1)}) custom-call(s32[1,1,8]{2,1,0:T(1,128)S(1)} %copy-done.2, s32[1,1,8,8]{3,2,1,0:T(8,128)S(1)} %copy-done.1, bf16[1024,2048]{1,0:T(8,128)(2,1)S(1)} %bitcast.2), custom_call_target="tpu_custom_call" | custom-call | tf_op jit(solution)/shard_map/pallas_call | solution.py:180
  13.8 2.2 %shard_map.51 = (f32[4,232,128]{2,1,0:T(8,128)S(1)}, f32[4,232,128]{2,1,0:T(8,128)S(1)}) custom-call(s32[1,1,8]{2,1,0:T(1,128)S(1)} %copy-done.2, s32[1,1,8,8]{3,2,1,0:T(8,128)S(1)} %copy-done.1, s32[1,1,8]{2,1,0:T(1,128)S(1)} %copy-done.3, s32[1,1,8]{2,1,0:T(1,128)S(1)} %collective-permute-done.refs_1_, s32[1,1,8]{2,1,0:T(1,128)S(1)} %collective-permute-done.1.refs_2_, ...), custom_call_target="tpu_custom_call" | custom-call | tf_op jit(solution)/shard_map/pallas_call | solution.py:195
  16.1 2.2 %shard_map.49 = (f32[4,344,128]{2,1,0:T(8,128)S(1)}, f32[4,344,128]{2,1,0:T(8,128)S(1)}) custom-call(s32[1,1,8]{2,1,0:T(1,128)S(1)} %copy-done.2, s32[1,1,8,8]{3,2,1,0:T(8,128)S(1)} %copy-done.1, s32[1,1,8]{2,1,0:T(1,128)S(1)} %copy-done.3, s32[1,1,8]{2,1,0:T(1,128)S(1)} %collective-permute-done.refs_1_, s32[1,1,8]{2,1,0:T(1,128)S(1)} %collective-permute-done.1.refs_2_, ...), custom_call_target="tpu_custom_call" | custom-call | tf_op jit(solution)/shard_map/pallas_call | solution.py:195
  18.9 2.2 %shard_map.47 = (f32[4,344,128]{2,1,0:T(8,128)S(1)}, f32[4,344,128]{2,1,0:T(8,128)S(1)}) custom-call(s32[1,1,8]{2,1,0:T(1,128)S(1)} %copy-done.2, s32[1,1,8,8]{3,2,1,0:T(8,128)S(1)} %copy-done.1, s32[1,1,8]{2,1,0:T(1,128)S(1)} %copy-done.3, s32[1,1,8]{2,1,0:T(1,128)S(1)} %collective-permute-done.refs_1_, s32[1,1,8]{2,1,0:T(1,128)S(1)} %collective-permute-done.1.refs_2_, ...), custom_call_target="tpu_custom_call" | custom-call | tf_op jit(solution)/shard_map/pallas_call | solution.py:195
  21.3 1.8 %collective-permute-start.18 = (f32[2,232,128]{2,1,0:T(8,128)S(1)}, f32[2,232,128]{2,1,0:T(8,128)S(1)}, u32[]{:S(2)}, u32[]{:S(2)}) collective-permute-start(f32[2,232,128]{2,1,0:T(8,128)S(1)} %pad_maximum_fusion.6), channel_id=1, source_target_pairs={{0,2},{1,3},{2,0},{3,1},{4,6},{5,7},{6,4},{7,5},{8,10},{9,11},{10,... | collective-permute-start | bytes 712712 | tf_op jit(solution)/shard_map/ppermute | solution.py:18
  23.1 1.6 %collective-permute-start.19 = (f32[2,232,128]{2,1,0:T(8,128)S(1)}, f32[2,232,128]{2,1,0:T(8,128)S(1)}, u32[]{:S(2)}, u32[]{:S(2)}) collective-permute-start(f32[2,232,128]{2,1,0:T(8,128)S(1)} %pad_maximum_fusion.7), channel_id=1, source_target_pairs={{0,4},{1,5},{2,6},{3,7},{4,0},{5,1},{6,2},{7,3},{8,12},{9,13},{10,... | collective-permute-start | bytes 712712 | tf_op jit(solution)/shard_map/ppermute | solution.py:18
  25.8 2.7 %collective-permute-start.13 = (f32[2,344,128]{2,1,0:T(8,128)S(1)}, f32[2,344,128]{2,1,0:T(8,128)S(1)}, u32[]{:S(2)}, u32[]{:S(2)}) collective-permute-start(f32[2,344,128]{2,1,0:T(8,128)S(1)} %pad_maximum_fusion.5), channel_id=1, source_target_pairs={{0,6},{1,7},{2,4},{3,5},{4,2},{5,3},{6,0},{7,1},{8,14},{9,15},{10,... | collective-permute-start | bytes 1056776 | tf_op jit(solution)/shard_map/ppermute | solution.py:18
  28.7 1.3 %collective-permute-done.18.refs_2_ = f32[2,232,128]{2,1,0:T(8,128)S(1)} collective-permute-done((f32[2,232,128]{2,1,0:T(8,128)S(1)}, f32[2,232,128]{2,1,0:T(8,128)S(1)}, u32[]{:S(2)}, u32[]{:S(2)}) %collective-permute-start.18) | collective-permute-done | bytes 237600 | tf_op jit(solution)/shard_map/ppermute | solution.py:18
  30.0 2.7 %collective-permute-start.6 = (f32[2,344,128]{2,1,0:T(8,128)S(1)}, f32[2,344,128]{2,1,0:T(8,128)S(1)}, u32[]{:S(2)}, u32[]{:S(2)}) collective-permute-start(f32[2,344,128]{2,1,0:T(8,128)S(1)} %pad_maximum_fusion.2), channel_id=1, source_target_pairs={{0,6},{1,7},{2,4},{3,5},{4,2},{5,3},{6,0},{7,1},{8,14},{9,15},{10,... | collective-permute-start | bytes 1056776 | tf_op jit(solution)/shard_map/ppermute | solution.py:18
  32.6 4.9 %collective-permute-done.11.refs_2_ = f32[2,344,128]{2,1,0:T(8,128)S(1)} collective-permute-done((f32[2,344,128]{2,1,0:T(8,128)S(1)}, f32[2,344,128]{2,1,0:T(8,128)S(1)}, u32[]{:S(2)}, u32[]{:S(2)}) %collective-permute-start.11) | collective-permute-done | bytes 352288 | tf_op jit(solution)/shard_map/ppermute | solution.py:18
  37.5 1.7 %collective-permute-start.5 = (f32[2,344,128]{2,1,0:T(8,128)S(1)}, f32[2,344,128]{2,1,0:T(8,128)S(1)}, u32[]{:S(2)}, u32[]{:S(2)}) collective-permute-start(f32[2,344,128]{2,1,0:T(8,128)S(1)} %pad_maximum_fusion.1), channel_id=1, source_target_pairs={{0,4},{1,5},{2,6},{3,7},{4,0},{5,1},{6,2},{7,3},{8,12},{9,13},{10,... | collective-permute-start | bytes 1056776 | tf_op jit(solution)/shard_map/ppermute | solution.py:18
  39.3 14.6 %collective-permute-done.12.refs_3_ = f32[2,344,128]{2,1,0:T(8,128)S(1)} collective-permute-done((f32[2,344,128]{2,1,0:T(8,128)S(1)}, f32[2,344,128]{2,1,0:T(8,128)S(1)}, u32[]{:S(2)}, u32[]{:S(2)}) %collective-permute-start.12) | collective-permute-done | bytes 352288 | tf_op jit(solution)/shard_map/ppermute | solution.py:18
  53.9 3.6 %collective-permute-start.20 = (f32[2,232,128]{2,1,0:T(8,128)S(1)}, f32[2,232,128]{2,1,0:T(8,128)S(1)}, u32[]{:S(2)}, u32[]{:S(2)}) collective-permute-start(f32[2,232,128]{2,1,0:T(8,128)S(1)} %pad_maximum_fusion.8), channel_id=1, source_target_pairs={{0,6},{1,7},{2,4},{3,5},{4,2},{5,3},{6,0},{7,1},{8,14},{9,15},{10,... | collective-permute-start | bytes 712712 | tf_op jit(solution)/shard_map/ppermute | solution.py:18
  57.5 0.7 shard_map.50
  58.2 0.7 collective-permute-start.14
  59.0 10.3 %collective-permute-done.20.refs_4_ = f32[2,232,128]{2,1,0:T(8,128)S(1)} collective-permute-done((f32[2,232,128]{2,1,0:T(8,128)S(1)}, f32[2,232,128]{2,1,0:T(8,128)S(1)}, u32[]{:S(2)}, u32[]{:S(2)}) %collective-permute-start.20) | collective-permute-done | bytes 237600 | tf_op jit(solution)/shard_map/ppermute | solution.py:18
  69.8 0.7 collective-permute-start.21
  70.6 3.5 %collective-permute-start.22 = (f32[3,2,32,128]{3,2,1,0:T(8,128)S(1)}, f32[3,2,32,128]{3,2,1,0:T(8,128)S(1)}, u32[]{:S(2)}, u32[]{:S(2)}) collective-permute-start(f32[3,2,32,128]{3,2,1,0:T(8,128)S(1)} %get-tuple-element.45), channel_id=1, source_target_pairs={{0,16},{8,24},{16,0},{24,8},{1,17},{9,25},{17,1},{25,9},{2,18},{10... | collective-permute-start | bytes 294920 | tf_op jit(solution)/shard_map/ppermute | solution.py:18
  74.3 1.3 %collective-permute-start.15 = (f32[3,2,48,128]{3,2,1,0:T(8,128)S(1)}, f32[3,2,48,128]{3,2,1,0:T(8,128)S(1)}, u32[]{:S(2)}, u32[]{:S(2)}) collective-permute-start(f32[3,2,48,128]{3,2,1,0:T(8,128)S(1)} %get-tuple-element.38), channel_id=1, source_target_pairs={{0,16},{8,24},{16,0},{24,8},{1,17},{9,25},{17,1},{25,9},{2,18},{10... | collective-permute-start | bytes 442376 | tf_op jit(solution)/shard_map/ppermute | solution.py:18
  75.6 0.7 shard_map.48
  76.3 2.3 %collective-permute-start.16 = (f32[3,2,48,128]{3,2,1,0:T(8,128)S(1)}, f32[3,2,48,128]{3,2,1,0:T(8,128)S(1)}, u32[]{:S(2)}, u32[]{:S(2)}) collective-permute-start(f32[3,2,48,128]{3,2,1,0:T(8,128)S(1)} %get-tuple-element.39), channel_id=1, source_target_pairs={{0,24},{8,16},{16,8},{24,0},{1,25},{9,17},{17,9},{25,1},{2,26},{10... | collective-permute-start | bytes 442376 | tf_op jit(solution)/shard_map/ppermute | solution.py:18
  78.6 11.8 %collective-permute-done.22.refs_10_ = f32[3,2,32,128]{3,2,1,0:T(8,128)S(1)} collective-permute-done((f32[3,2,32,128]{3,2,1,0:T(8,128)S(1)}, f32[3,2,32,128]{3,2,1,0:T(8,128)S(1)}, u32[]{:S(2)}, u32[]{:S(2)}) %collective-permute-start.22) | collective-permute-done | bytes 98336 | tf_op jit(solution)/shard_map/ppermute | solution.py:18
  90.4 3.6 %collective-permute-start.8 = (f32[3,2,48,128]{3,2,1,0:T(8,128)S(1)}, f32[3,2,48,128]{3,2,1,0:T(8,128)S(1)}, u32[]{:S(2)}, u32[]{:S(2)}) collective-permute-start(f32[3,2,48,128]{3,2,1,0:T(8,128)S(1)} %get-tuple-element.31), channel_id=1, source_target_pairs={{0,16},{8,24},{16,0},{24,8},{1,17},{9,25},{17,1},{25,9},{2,18},{10... | collective-permute-start | bytes 442376 | tf_op jit(solution)/shard_map/ppermute | solution.py:18
  94.0 1.4 %collective-permute-start.9 = (f32[3,2,48,128]{3,2,1,0:T(8,128)S(1)}, f32[3,2,48,128]{3,2,1,0:T(8,128)S(1)}, u32[]{:S(2)}, u32[]{:S(2)}) collective-permute-start(f32[3,2,48,128]{3,2,1,0:T(8,128)S(1)} %get-tuple-element.32), channel_id=1, source_target_pairs={{0,24},{8,16},{16,8},{24,0},{1,25},{9,17},{17,9},{25,1},{2,26},{10... | collective-permute-start | bytes 442376 | tf_op jit(solution)/shard_map/ppermute | solution.py:18
  95.8 2.0 %collective-permute-done.7.refs_1_ = f32[3,2,48,128]{3,2,1,0:T(8,128)S(1)} collective-permute-done((f32[3,2,48,128]{3,2,1,0:T(8,128)S(1)}, f32[3,2,48,128]{3,2,1,0:T(8,128)S(1)}, u32[]{:S(2)}, u32[]{:S(2)}) %collective-permute-start.7) | collective-permute-done | bytes 147488 | tf_op jit(solution)/shard_map/ppermute | solution.py:18
  97.7 6.8 %collective-permute-done.8.refs_2_ = f32[3,2,48,128]{3,2,1,0:T(8,128)S(1)} collective-permute-done((f32[3,2,48,128]{3,2,1,0:T(8,128)S(1)}, f32[3,2,48,128]{3,2,1,0:T(8,128)S(1)}, u32[]{:S(2)}, u32[]{:S(2)}) %collective-permute-start.8) | collective-permute-done | bytes 147488 | tf_op jit(solution)/shard_map/ppermute | solution.py:18
  104.5 0.8 shard_map.53
  (47 shorter events, 3.3 us)
Async XLA Ops:
  0.0 13.7 %collective-permute-start = (s32[1,1,8]{2,1,0:T(1,128)}, s32[1,1,8]{2,1,0:T(1,128)S(1)}, u32[]{:S(2)}, u32[]{:S(2)}) collective-permute-start(s32[1,1,8]{2,1,0:T(1,128)} %refs_0_.5), channel_id=1, source_target_pairs={{0,8},{8,0},{16,24},{24,16},{1,9},{9,1},{17,25},{25,17},{2,10},{10... | collective-permute-start | bytes 104 | tf_op jit(solution)/shard_map/ppermute | solution.py:18
  3.0 10.7 %collective-permute-start.1 = (s32[1,1,8]{2,1,0:T(1,128)}, s32[1,1,8]{2,1,0:T(1,128)S(1)}, u32[]{:S(2)}, u32[]{:S(2)}) collective-permute-start(s32[1,1,8]{2,1,0:T(1,128)} %refs_0_.5), channel_id=1, source_target_pairs={{0,16},{8,24},{16,0},{24,8},{1,17},{9,25},{17,1},{25,9},{2,18},{10... | collective-permute-start | bytes 104 | tf_op jit(solution)/shard_map/ppermute | solution.py:18
  5.6 8.2 %collective-permute-start.2 = (s32[1,1,8]{2,1,0:T(1,128)}, s32[1,1,8]{2,1,0:T(1,128)S(1)}, u32[]{:S(2)}, u32[]{:S(2)}) collective-permute-start(s32[1,1,8]{2,1,0:T(1,128)} %refs_0_.5), channel_id=1, source_target_pairs={{0,24},{8,16},{16,8},{24,0},{1,25},{9,17},{17,9},{25,1},{2,26},{10... | collective-permute-start | bytes 104 | tf_op jit(solution)/shard_map/ppermute | solution.py:18
  5.6 2.2 %copy-start = (bf16[1,1,1024,2048]{3,2,1,0:T(8,128)(2,1)S(1)}, bf16[1,1,1024,2048]{3,2,1,0:T(8,128)(2,1)}, u32[]{:S(2)}) copy-start(bf16[1,1,1024,2048]{3,2,1,0:T(8,128)(2,1)} %param.4) | copy-start | bytes 12582916
  7.8 0.7 copy-start.1
  8.5 0.7 copy-start.2
  9.1 4.6 %copy-start.3 = (s32[1,1,8]{2,1,0:T(1,128)S(1)}, s32[1,1,8]{2,1,0:T(1,128)}, u32[]{:S(2)}) copy-start(s32[1,1,8]{2,1,0:T(1,128)} %refs_0_.5) | copy-start | bytes 100
  16.0 5.3 %collective-permute-start.17 = (f32[4,232,128]{2,1,0:T(8,128)S(1)}, f32[4,232,128]{2,1,0:T(8,128)S(1)}, u32[]{:S(2)}, u32[]{:S(2)}) collective-permute-start(f32[4,232,128]{2,1,0:T(8,128)S(1)} %get-tuple-element.42), channel_id=1, source_target_pairs={{0,1},{1,0},{2,3},{3,2},{4,5},{5,4},{6,7},{7,6},{8,9},{9,8},{10,11... | collective-permute-start | bytes 1425416 | tf_op jit(solution)/shard_map/ppermute | solution.py:18
  18.3 6.4 %collective-permute-start.10 = (f32[4,344,128]{2,1,0:T(8,128)S(1)}, f32[4,344,128]{2,1,0:T(8,128)S(1)}, u32[]{:S(2)}, u32[]{:S(2)}) collective-permute-start(f32[4,344,128]{2,1,0:T(8,128)S(1)} %get-tuple-element.35), channel_id=1, source_target_pairs={{0,1},{1,0},{2,3},{3,2},{4,5},{5,4},{6,7},{7,6},{8,9},{9,8},{10,11... | collective-permute-start | bytes 2113544 | tf_op jit(solution)/shard_map/ppermute | solution.py:18
  21.1 4.7 %collective-permute-start.3 = (f32[4,344,128]{2,1,0:T(8,128)S(1)}, f32[4,344,128]{2,1,0:T(8,128)S(1)}, u32[]{:S(2)}, u32[]{:S(2)}) collective-permute-start(f32[4,344,128]{2,1,0:T(8,128)S(1)} %get-tuple-element.28), channel_id=1, source_target_pairs={{0,1},{1,0},{2,3},{3,2},{4,5},{5,4},{6,7},{7,6},{8,9},{9,8},{10,11... | collective-permute-start | bytes 2113544 | tf_op jit(solution)/shard_map/ppermute | solution.py:18
  21.3 8.6 %collective-permute-start.18 = (f32[2,232,128]{2,1,0:T(8,128)S(1)}, f32[2,232,128]{2,1,0:T(8,128)S(1)}, u32[]{:S(2)}, u32[]{:S(2)}) collective-permute-start(f32[2,232,128]{2,1,0:T(8,128)S(1)} %pad_maximum_fusion.6), channel_id=1, source_target_pairs={{0,2},{1,3},{2,0},{3,1},{4,6},{5,7},{6,4},{7,5},{8,10},{9,11},{10,... | collective-permute-start | bytes 712712 | tf_op jit(solution)/shard_map/ppermute | solution.py:18
  23.1 35.1 %collective-permute-start.19 = (f32[2,232,128]{2,1,0:T(8,128)S(1)}, f32[2,232,128]{2,1,0:T(8,128)S(1)}, u32[]{:S(2)}, u32[]{:S(2)}) collective-permute-start(f32[2,232,128]{2,1,0:T(8,128)S(1)} %pad_maximum_fusion.7), channel_id=1, source_target_pairs={{0,4},{1,5},{2,6},{3,7},{4,0},{5,1},{6,2},{7,3},{8,12},{9,13},{10,... | collective-permute-start | bytes 712712 | tf_op jit(solution)/shard_map/ppermute | solution.py:18
  24.8 12.7 %collective-permute-start.11 = (f32[2,344,128]{2,1,0:T(8,128)S(1)}, f32[2,344,128]{2,1,0:T(8,128)S(1)}, u32[]{:S(2)}, u32[]{:S(2)}) collective-permute-start(f32[2,344,128]{2,1,0:T(8,128)S(1)} %pad_maximum_fusion.3), channel_id=1, source_target_pairs={{0,2},{1,3},{2,0},{3,1},{4,6},{5,7},{6,4},{7,5},{8,10},{9,11},{10,... | collective-permute-start | bytes 1056776 | tf_op jit(solution)/shard_map/ppermute | solution.py:18
  25.4 28.5 %collective-permute-start.12 = (f32[2,344,128]{2,1,0:T(8,128)S(1)}, f32[2,344,128]{2,1,0:T(8,128)S(1)}, u32[]{:S(2)}, u32[]{:S(2)}) collective-permute-start(f32[2,344,128]{2,1,0:T(8,128)S(1)} %pad_maximum_fusion.4), channel_id=1, source_target_pairs={{0,4},{1,5},{2,6},{3,7},{4,0},{5,1},{6,2},{7,3},{8,12},{9,13},{10,... | collective-permute-start | bytes 1056776 | tf_op jit(solution)/shard_map/ppermute | solution.py:18
  25.8 28.1 %collective-permute-start.13 = (f32[2,344,128]{2,1,0:T(8,128)S(1)}, f32[2,344,128]{2,1,0:T(8,128)S(1)}, u32[]{:S(2)}, u32[]{:S(2)}) collective-permute-start(f32[2,344,128]{2,1,0:T(8,128)S(1)} %pad_maximum_fusion.5), channel_id=1, source_target_pairs={{0,6},{1,7},{2,4},{3,5},{4,2},{5,3},{6,0},{7,1},{8,14},{9,15},{10,... | collective-permute-start | bytes 1056776 | tf_op jit(solution)/shard_map/ppermute | solution.py:18
  30.0 40.6 %collective-permute-start.6 = (f32[2,344,128]{2,1,0:T(8,128)S(1)}, f32[2,344,128]{2,1,0:T(8,128)S(1)}, u32[]{:S(2)}, u32[]{:S(2)}) collective-permute-start(f32[2,344,128]{2,1,0:T(8,128)S(1)} %pad_maximum_fusion.2), channel_id=1, source_target_pairs={{0,6},{1,7},{2,4},{3,5},{4,2},{5,3},{6,0},{7,1},{8,14},{9,15},{10,... | collective-permute-start | bytes 1056776 | tf_op jit(solution)/shard_map/ppermute | solution.py:18
  37.5 36.5 %collective-permute-start.5 = (f32[2,344,128]{2,1,0:T(8,128)S(1)}, f32[2,344,128]{2,1,0:T(8,128)S(1)}, u32[]{:S(2)}, u32[]{:S(2)}) collective-permute-start(f32[2,344,128]{2,1,0:T(8,128)S(1)} %pad_maximum_fusion.1), channel_id=1, source_target_pairs={{0,4},{1,5},{2,6},{3,7},{4,0},{5,1},{6,2},{7,3},{8,12},{9,13},{10,... | collective-permute-start | bytes 1056776 | tf_op jit(solution)/shard_map/ppermute | solution.py:18
  53.9 20.4 %collective-permute-start.4 = (f32[2,344,128]{2,1,0:T(8,128)S(1)}, f32[2,344,128]{2,1,0:T(8,128)S(1)}, u32[]{:S(2)}, u32[]{:S(2)}) collective-permute-start(f32[2,344,128]{2,1,0:T(8,128)S(1)} %pad_maximum_fusion), channel_id=1, source_target_pairs={{0,2},{1,3},{2,0},{3,1},{4,6},{5,7},{6,4},{7,5},{8,10},{9,11},{10,... | collective-permute-start | bytes 1056776 | tf_op jit(solution)/shard_map/ppermute | solution.py:18
  53.9 15.4 %collective-permute-start.20 = (f32[2,232,128]{2,1,0:T(8,128)S(1)}, f32[2,232,128]{2,1,0:T(8,128)S(1)}, u32[]{:S(2)}, u32[]{:S(2)}) collective-permute-start(f32[2,232,128]{2,1,0:T(8,128)S(1)} %pad_maximum_fusion.8), channel_id=1, source_target_pairs={{0,6},{1,7},{2,4},{3,5},{4,2},{5,3},{6,0},{7,1},{8,14},{9,15},{10,... | collective-permute-start | bytes 712712 | tf_op jit(solution)/shard_map/ppermute | solution.py:18
  58.2 35.8 %collective-permute-start.14 = (f32[3,2,48,128]{3,2,1,0:T(8,128)S(1)}, f32[3,2,48,128]{3,2,1,0:T(8,128)S(1)}, u32[]{:S(2)}, u32[]{:S(2)}) collective-permute-start(f32[3,2,48,128]{3,2,1,0:T(8,128)S(1)} %get-tuple-element.37), channel_id=1, source_target_pairs={{0,8},{8,0},{16,24},{24,16},{1,9},{9,1},{17,25},{25,17},{2,10},{10... | collective-permute-start | bytes 442376 | tf_op jit(solution)/shard_map/ppermute | solution.py:18
  69.8 6.5 %collective-permute-start.21 = (f32[3,2,32,128]{3,2,1,0:T(8,128)S(1)}, f32[3,2,32,128]{3,2,1,0:T(8,128)S(1)}, u32[]{:S(2)}, u32[]{:S(2)}) collective-permute-start(f32[3,2,32,128]{3,2,1,0:T(8,128)S(1)} %get-tuple-element.44), channel_id=1, source_target_pairs={{0,8},{8,0},{16,24},{24,16},{1,9},{9,1},{17,25},{25,17},{2,10},{10... | collective-permute-start | bytes 294920 | tf_op jit(solution)/shard_map/ppermute | solution.py:18
  70.6 19.8 %collective-permute-start.22 = (f32[3,2,32,128]{3,2,1,0:T(8,128)S(1)}, f32[3,2,32,128]{3,2,1,0:T(8,128)S(1)}, u32[]{:S(2)}, u32[]{:S(2)}) collective-permute-start(f32[3,2,32,128]{3,2,1,0:T(8,128)S(1)} %get-tuple-element.45), channel_id=1, source_target_pairs={{0,16},{8,24},{16,0},{24,8},{1,17},{9,25},{17,1},{25,9},{2,18},{10... | collective-permute-start | bytes 294920 | tf_op jit(solution)/shard_map/ppermute | solution.py:18
  74.1 16.4 %collective-permute-start.23 = (f32[3,2,32,128]{3,2,1,0:T(8,128)S(1)}, f32[3,2,32,128]{3,2,1,0:T(8,128)S(1)}, u32[]{:S(2)}, u32[]{:S(2)}) collective-permute-start(f32[3,2,32,128]{3,2,1,0:T(8,128)S(1)} %get-tuple-element.46), channel_id=1, source_target_pairs={{0,24},{8,16},{16,8},{24,0},{1,25},{9,17},{17,9},{25,1},{2,26},{10... | collective-permute-start | bytes 294920 | tf_op jit(solution)/shard_map/ppermute | solution.py:18
  74.3 21.5 %collective-permute-start.15 = (f32[3,2,48,128]{3,2,1,0:T(8,128)S(1)}, f32[3,2,48,128]{3,2,1,0:T(8,128)S(1)}, u32[]{:S(2)}, u32[]{:S(2)}) collective-permute-start(f32[3,2,48,128]{3,2,1,0:T(8,128)S(1)} %get-tuple-element.38), channel_id=1, source_target_pairs={{0,16},{8,24},{16,0},{24,8},{1,17},{9,25},{17,1},{25,9},{2,18},{10... | collective-permute-start | bytes 442376 | tf_op jit(solution)/shard_map/ppermute | solution.py:18
  76.3 19.5 %collective-permute-start.16 = (f32[3,2,48,128]{3,2,1,0:T(8,128)S(1)}, f32[3,2,48,128]{3,2,1,0:T(8,128)S(1)}, u32[]{:S(2)}, u32[]{:S(2)}) collective-permute-start(f32[3,2,48,128]{3,2,1,0:T(8,128)S(1)} %get-tuple-element.39), channel_id=1, source_target_pairs={{0,24},{8,16},{16,8},{24,0},{1,25},{9,17},{17,9},{25,1},{2,26},{10... | collective-permute-start | bytes 442376 | tf_op jit(solution)/shard_map/ppermute | solution.py:18
  90.4 7.3 %collective-permute-start.7 = (f32[3,2,48,128]{3,2,1,0:T(8,128)S(1)}, f32[3,2,48,128]{3,2,1,0:T(8,128)S(1)}, u32[]{:S(2)}, u32[]{:S(2)}) collective-permute-start(f32[3,2,48,128]{3,2,1,0:T(8,128)S(1)} %get-tuple-element.30), channel_id=1, source_target_pairs={{0,8},{8,0},{16,24},{24,16},{1,9},{9,1},{17,25},{25,17},{2,10},{10... | collective-permute-start | bytes 442376 | tf_op jit(solution)/shard_map/ppermute | solution.py:18
  90.4 14.1 %collective-permute-start.8 = (f32[3,2,48,128]{3,2,1,0:T(8,128)S(1)}, f32[3,2,48,128]{3,2,1,0:T(8,128)S(1)}, u32[]{:S(2)}, u32[]{:S(2)}) collective-permute-start(f32[3,2,48,128]{3,2,1,0:T(8,128)S(1)} %get-tuple-element.31), channel_id=1, source_target_pairs={{0,16},{8,24},{16,0},{24,8},{1,17},{9,25},{17,1},{25,9},{2,18},{10... | collective-permute-start | bytes 442376 | tf_op jit(solution)/shard_map/ppermute | solution.py:18
  94.0 10.5 %collective-permute-start.9 = (f32[3,2,48,128]{3,2,1,0:T(8,128)S(1)}, f32[3,2,48,128]{3,2,1,0:T(8,128)S(1)}, u32[]{:S(2)}, u32[]{:S(2)}) collective-permute-start(f32[3,2,48,128]{3,2,1,0:T(8,128)S(1)} %get-tuple-element.32), channel_id=1, source_target_pairs={{0,24},{8,16},{16,8},{24,0},{1,25},{9,17},{17,9},{25,1},{2,26},{10... | collective-permute-start | bytes 442376 | tf_op jit(solution)/shard_map/ppermute | solution.py:18

commit v2 on v0

--- a/solution.py
+++ b/solution.py
@@ -1,16 +1,331 @@
+import functools
+
 import jax
 import jax.numpy as jnp
 from jax import lax
+from jax.experimental import pallas as pl
+from jax.experimental.pallas import tpu as pltpu
 from jax.sharding import PartitionSpec as P
 
 ANC_DEV = 3
+META = 8
+CUT = 16
+CHUNK_PARTS = (2, 2, 2, 2)
+DEPS = ((1,), (1,), (2,))
+ZWAIT = 2
+ZDEP = 2
+GATHER_COST = 128 * 1024 * 1024
+VMEM_LIMIT = 44 * 1024 * 1024
 
 
 def swapped(shard, axis, apart):
-    return lax.ppermute(shard, axis, [(i, i ^ 1 << apart) for i in range(lax.axis_size(axis))])
-
-
-def per_device(panels, pattern, child_map, ancestor_map):
+    return lax.ppermute(shard, axis, [(i, i ^ apart) for i in range(lax.axis_size(axis))])
+
+
+def smem_spec():
+    return pl.BlockSpec(memory_space=pltpu.SMEM)
+
+
+def vmem_spec():
+    return pl.BlockSpec(memory_space=pltpu.VMEM)
+
+
+def place_of(position, per_piece, my_sub):
+    return ((position // per_piece) ^ my_sub) * per_piece + position % per_piece
+
+
+def multiply_kernel(nb, per_piece, spans, child_any, pattern_any, map_any, panel_any, *refs):
+    out_refs = refs[: len(spans)]
+    plan_ref, panel_ref, child_ref, pattern_ref, map_ref, sems = refs[len(spans) :]
+    block = panel_any.shape[0] // nb
+    small = [
+        pltpu.make_async_copy(child_any, child_ref, sems.at[nb]),
+        pltpu.make_async_copy(pattern_any, pattern_ref, sems.at[nb + 1]),
+        pltpu.make_async_copy(map_any, map_ref, sems.at[nb + 2]),
+    ]
+    for copy in small:
+        copy.start()
+    large = []
+    for i in range(nb):
+        rows = pl.ds(i * block, block)
+        large.append(pltpu.make_async_copy(panel_any.at[rows, :], panel_ref.at[rows, :], sems.at[i]))
+        large[-1].start()
+    for copy in small:
+        copy.wait()
+    my_sub = lax.axis_index("subtree")
+    columns = [child_ref[0, 0, i] for i in range(nb)]
+    places = [place_of(column, per_piece, my_sub) for column in columns]
+    empty = jnp.int32(nb)
+    for i in range(nb):
+        empty = jnp.where((pattern_ref[0, 0, i, i] == 0) & (places[i] < empty), places[i], empty)
+    kept = []
+    for i in range(nb):
+        kept.append(jnp.where(places[i] == empty, nb - 1, places[i] - (places[i] > empty).astype(jnp.int32)))
+        plan_ref[0, i] = map_ref[0, 0, i]
+        plan_ref[1, i] = empty
+
+    def put(i, j, value):
+        for out_ref, (start, count) in zip(out_refs, spans):
+            out_ref[columns[j], pl.ds(pl.multiple_of(kept[i] * count, CUT), count), :] = value[start : start + count]
+
+    for copy in large:
+        copy.wait()
+    for first in range(nb - 2, -1, -2):
+        product = lax.dot_general(
+            panel_ref[pl.ds(first * block, (nb - first) * block), :],
+            panel_ref[pl.ds(first * block, 2 * block), :],
+            (((1,), (1,)), ((), ())),
+            preferred_element_type=jnp.float32,
+        )
+        for i in range(first, nb):
+            for j in (first, first + 1):
+                scale = pattern_ref[0, 0, i, j].astype(jnp.float32)
+                value = (
+                    product[(i - first) * block : (i - first + 1) * block, (j - first) * block : (j - first + 1) * block]
+                    * scale
+                )
+                put(i, j, value)
+                if i > first + 1:
+                    put(j, i, value.T)
+
+
+def route_kernel(nb, per_piece, subs, counts, extra, plan_ref, *refs):
+    slot_refs = refs[: subs - 1]
+    update_refs = refs[subs - 1 : subs - 1 + len(counts)]
+    out_ref, goal = refs[subs - 1 + len(counts) + extra :]
+    block = out_ref.shape[2]
+    my_tree = lax.axis_index("forest")
+    half = out_ref.shape[0] // 2
+    empty = plan_ref[1, 0]
+    tails = []
+    at = 0
+    for count in counts:
+        tails.append(at + (nb - 1) * count)
+        at = tails[-1] + META
+    for tail in tails:
+        out_ref[:, pl.ds(tail, META), :] = jnp.full((out_ref.shape[0], META, block), empty.astype(jnp.float32))
+    for apart in range(subs):
+        for c in range(nb):
+            entry = plan_ref[0, c] if apart == 0 else slot_refs[apart - 1][0, 0, c]
+            owner = lax.div(entry, ANC_DEV)
+            to = owner ^ my_tree
+            to = (to & 1) * half + (to >> 1)
+            goal[apart, c] = to
+            slot = (entry - owner * ANC_DEV).astype(jnp.float32)
+            for tail in tails:
+                out_ref[to, pl.ds(tail + 1 + apart, 1), :] = jnp.full((1, block), slot, jnp.float32)
+    for k in range(nb - 1):
+        place = k + (empty <= k).astype(jnp.int32)
+        apart = place // per_piece
+        for c in range(nb):
+            to = goal[apart, c]
+            for tail, count, update_ref in zip(tails, counts, update_refs):
+                out_ref[to, pl.ds(tail - (nb - 1 - k) * count, count), :] = update_ref[c, pl.ds(k * count, count), :]
+
+
+def gather_kernel(nb, per_piece, count, extra, *refs):
+    subs = nb // per_piece
+    in_refs, out_refs = refs[: len(refs) - subs - extra], refs[-subs:]
+    tail = (nb - 1) * count
+    block = in_refs[0].shape[-1]
+    sources = []
+    for ref in in_refs:
+        for index in range(ref.shape[0]):
+            sources.append(ref.at[index])
+    for apart in range(subs):
+        for part in range(per_piece):
+            place = apart * per_piece + part
+            sums = [jnp.zeros((count, block), jnp.float32) for _ in range(ANC_DEV)]
+            for source in sources:
+                empty = source[pl.ds(tail, 1), :]
+                slot = source[pl.ds(tail + 1 + apart, 1), :]
+                low = source[pl.ds(min(place, nb - 2) * count, count), :]
+                high = source[pl.ds(max(place - 1, 0) * count, count), :]
+                value = jnp.where(empty > place, low, jnp.where(empty < place, high, 0.0))
+                for index in range(ANC_DEV):
+                    sums[index] += jnp.where(slot == index, value, 0.0)
+            for index in range(ANC_DEV):
+                out_refs[apart][index, part] = sums[index]
+
+
+def pack_kernel(chip, same_ref, crossed_ref, *refs):
+    refs[-1][0] = same_ref[chip]
+    refs[-1][1] = crossed_ref[chip]
+
+
+def pack(params, chip, same, crossed, *earlier):
+    return pl.pallas_call(
+        functools.partial(pack_kernel, chip),
+        out_shape=jax.ShapeDtypeStruct((2, *same.shape[1:]), jnp.float32),
+        in_specs=[vmem_spec()] * 2 + [pl.BlockSpec(memory_space=pl.ANY)] * len(earlier),
+        out_specs=vmem_spec(),
+        compiler_params=params,
+    )(same, crossed, *earlier)
+
+
+def gather(params, nb, per_piece, count, arrived, earlier):
+    subs = nb // per_piece
+    block = arrived[0].shape[-1]
+    return pl.pallas_call(
+        functools.partial(gather_kernel, nb, per_piece, count, len(earlier)),
+        out_shape=[jax.ShapeDtypeStruct((ANC_DEV, per_piece, count, block), jnp.float32)] * subs,
+        in_specs=[vmem_spec()] * len(arrived) + [pl.BlockSpec(memory_space=pl.ANY)] * len(earlier),
+        out_specs=[vmem_spec()] * subs,
+        compiler_params=params,
+        cost_estimate=pl.CostEstimate(flops=0, bytes_accessed=GATHER_COST, transcendentals=0),
+    )(*arrived, *earlier)
+
+
+def add_kernel(places, *refs):
+    came_ref, out_refs = refs[len(places)], refs[-len(places) :]
+    for held_ref, place, out_ref in zip(refs, places, out_refs):
+        out_ref[...] = held_ref[...] + came_ref[place]
+
+
+def send(held, apart):
+    going = [index for index in held if index & apart]
+    return going, swapped(jnp.stack([held[index] for index in going]), "subtree", apart)
+
+
+def settle(params, held, parts, apart, going, came, earlier):
+    parts.append(came[going.index(apart)])
+    for index in going:
+        del held[index]
+    kept = [index ^ apart for index in going if index != apart]
+    if kept:
+        sums = pl.pallas_call(
+            functools.partial(add_kernel, [going.index(index ^ apart) for index in kept]),
+            out_shape=[jax.ShapeDtypeStruct(came.shape[1:], came.dtype)] * len(kept),
+            in_specs=[vmem_spec()] * (len(kept) + 1) + [pl.BlockSpec(memory_space=pl.ANY)] * len(earlier),
+            out_specs=[vmem_spec()] * len(kept),
+            compiler_params=params,
+        )(*[held[index] for index in kept], came, *earlier)
+        held.update(zip(kept, sums))
+
+
+def finish_kernel(chunk_rows, shares, *refs):
+    out_ref = refs[-1]
+    start = at = 0
+    for count, share in zip(chunk_rows, shares):
+        total = refs[at][...]
+        for part in refs[at + 1 : at + share]:
+            total += part[...]
+        out_ref[0, :, :, pl.ds(start, count), :] = total
+        start += count
+        at += share
+
+
+def per_device_blocks(panels, pattern, child_map, ancestor_map):
+    row_total, pivot_width = panels.shape[2:]
+    nb = child_map.shape[2]
+    block = row_total // nb
+    subs = lax.axis_size("subtree")
+    trees = lax.axis_size("forest")
+    per_piece = nb // subs
+    units = block // CUT
+    chunk_rows = []
+    for index, share in enumerate(CHUNK_PARTS):
+        chunk_rows.append(units * share // sum(CHUNK_PARTS) * CUT)
+    chunk_rows[-1] += block - sum(chunk_rows)
+    chips = trees // 2
+    params = pltpu.CompilerParams(vmem_limit_bytes=VMEM_LIMIT)
+
+    panel = panels.reshape(row_total, pivot_width)
+    spans = []
+    for count in chunk_rows:
+        spans.append((sum(chunk_rows[: len(spans)]), count))
+    slots = [swapped(ancestor_map, "subtree", apart) for apart in range(1, subs)]
+    updates = pl.pallas_call(
+        functools.partial(multiply_kernel, nb, per_piece, spans),
+        out_shape=[jax.ShapeDtypeStruct((nb, nb * count, block), jnp.float32) for count in chunk_rows]
+        + [jax.ShapeDtypeStruct((2, nb), jnp.int32)],
+        in_specs=[pl.BlockSpec(memory_space=pltpu.HBM)] * 4,
+        out_specs=[vmem_spec()] * len(spans) + [smem_spec()],
+        scratch_shapes=[
+            pltpu.VMEM((row_total, pivot_width), jnp.bfloat16),
+            pltpu.SMEM(child_map.shape, jnp.int32),
+            pltpu.SMEM(pattern.shape, jnp.int32),
+            pltpu.SMEM(ancestor_map.shape, jnp.int32),
+            pltpu.SemaphoreType.DMA((nb + 3,)),
+        ],
+        compiler_params=params,
+        cost_estimate=pl.CostEstimate(
+            flops=2 * nb * block * row_total * pivot_width,
+            bytes_accessed=2 * row_total * pivot_width,
+            transcendentals=0,
+        ),
+    )(*[pltpu.with_memory_space_constraint(array, pltpu.HBM) for array in (child_map, pattern, ancestor_map, panel)])
+    plan = updates[-1]
+    laid = []
+    earlier = []
+    for first, end in ((0, 1), (1, len(spans))):
+        counts = chunk_rows[first:end]
+        blocks = pl.pallas_call(
+            functools.partial(route_kernel, nb, per_piece, subs, counts, len(earlier)),
+            out_shape=jax.ShapeDtypeStruct(
+                (trees, (nb - 1) * sum(counts) + META * len(counts), block), jnp.float32
+            ),
+            in_specs=[smem_spec()] * subs
+            + [vmem_spec()] * len(counts)
+            + [pl.BlockSpec(memory_space=pl.ANY)] * len(earlier),
+            out_specs=vmem_spec(),
+            scratch_shapes=[pltpu.SMEM((subs, nb), jnp.int32)],
+            compiler_params=params,
+        )(plan, *slots, *updates[first:end], *earlier)
+        same, crossed = blocks[:chips], swapped(blocks[chips:], "forest", 1)
+        at = 0
+        for count in counts:
+            rows = (nb - 1) * count + META
+            laid.append((same[:, at : at + rows], crossed[:, at : at + rows]))
+            at += rows
+        if first == 0:
+            going_out = [pack(params, chip, *laid[0]) for chip in range(1, chips)]
+            earlier = going_out
+
+    pieces = []
+    arrivals = []
+    open_sums = None
+    for c, count in enumerate(chunk_rows):
+        arrived = [laid[c][0][:1], laid[c][1][:1]]
+        for chip in range(1, chips):
+            arrived.append(swapped(going_out[chip - 1], "forest", 2 * chip))
+        arrivals.append(arrived)
+        waits = []
+        if c < len(chunk_rows) - 1:
+            going_out = []
+            for chip in range(1, chips):
+                earlier = [arrived[index + 1] for index in DEPS[chip - 1]]
+                if chip == 2 and c > 1 and ZDEP:
+                    earlier.append(pieces[c - 2][-1])
+                going_out.append(pack(params, chip, *laid[c + 1], *earlier))
+            waits = list(going_out)
+        if open_sums is not None:
+            held, apart = open_sums[0], 1
+            settle(params, held, pieces[-1], apart, *open_sums[1:], waits[:ZWAIT])
+            while 2 * apart < subs:
+                apart *= 2
+                settle(params, held, pieces[-1], apart, *send(held, apart), [])
+        sums = gather(params, nb, per_piece, count, arrived, waits)
+        parts = [sums[0]]
+        open_sums = None
+        if c == len(chunk_rows) - 1:
+            for apart in range(1, subs):
+                parts.append(swapped(sums[apart], "subtree", apart))
+        else:
+            held = dict(enumerate(sums))
+            open_sums = (held, *send(held, 1))
+        pieces.append(parts)
+    out = pl.pallas_call(
+        functools.partial(finish_kernel, chunk_rows, [len(parts) for parts in pieces]),
+        out_shape=jax.ShapeDtypeStruct((1, ANC_DEV, per_piece, block, block), jnp.float32),
+        in_specs=[vmem_spec()] * sum(len(parts) for parts in pieces),
+        out_specs=vmem_spec(),
+        compiler_params=params,
+    )(*[part for parts in pieces for part in parts])
+    return out.reshape(1, ANC_DEV, per_piece * block, block)
+
+
+def per_device_halving(panels, pattern, child_map, ancestor_map):
     row_total = panels.shape[2]
     pivot_width = panels.shape[3]
     block_count = child_map.shape[2]
@@ -46,7 +361,7 @@
         high_side = my_index >> bit_number & 1 == 1
         kept_half = jnp.where(high_side, high_half, low_half)
         sent_half = jnp.where(high_side, low_half, high_half)
-        holding = kept_half + swapped(sent_half, "subtree", bit_number)
+        holding = kept_half + swapped(sent_half, "subtree", 1 << bit_number)
     piece_rows = holding.shape[0]
     column_blocks = holding.reshape(piece_rows, block_count, block_rows).transpose(1, 0, 2)
     slot_values = ancestor_map[0, 0]
@@ -84,6 +399,14 @@
         P("subtree", "forest", None),
     )
     out_specs = P("subtree", "forest", None, None)
+
+    def per_device(panels, pattern, child_map, ancestor_map):
+        nb = child_map.shape[2]
+        subs, trees = mesh.shape["subtree"], mesh.shape["forest"]
+        if nb == trees and nb % subs == 0 and subs < META and trees % 2 == 0:
+            return per_device_blocks(panels, pattern, child_map, ancestor_map)
+        return per_device_halving(panels, pattern, child_map, ancestor_map)
+
     return jax.shard_map(
         per_device, mesh=mesh, in_specs=in_specs, out_specs=out_specs, check_vma=False
     )

time: 181 us -> 74.7 us (0.41)
  waiting for transfers between devices: 118 us -> 23.6 us
  starting transfers between devices: 8.43 us -> 39.5 us
  matrix products: 30.8 us -> 0 us
  Pallas kernels: 0 us -> 10.7 us
  local copies, waits for them, and re-layouts: 9.8 us -> 0.44 us
  blocking collectives: 8.01 us -> 0 us
  other arithmetic: 4.89 us -> 0.05 us
    ppermute x2 -> x26, waiting for transfers between devices: 103 us -> 23.6 us  [swapped(): lax.ppermute(shard, axis, [(i, i ^ apart) for i in range(lax.axis_size(ax...]
    ppermute x2 -> x26, starting transfers between devices: 4.87 us -> 39.5 us  [swapped(): lax.ppermute(shard, axis, [(i, i ^ apart) for i in range(lax.axis_size(ax...]
    dot_general x6 -> x0, matrix products: 30.8 us -> none  [the longest x1 20.1 us: per_device(): lax.dot_general(flat_rows, flat_rows, (((1,), (1,)), ((), ())), preferred...]
    all_to_all x1 -> x0, waiting for transfers between devices: 15 us -> none  [per_device(): lax.all_to_all(outgoing, 'forest', split_axis=0, concat_axis=0, tiled=True)]
    pallas_call x0 -> x23, Pallas kernels: none -> 10.7 us  [the longest x1 5.76 us: per_device_blocks(): pl.pallas_call(functools.partial(multiply_kernel, nb, per_piece, spans),...]
    unnamed x1 -> x0, blocking collectives: 8.01 us -> none
    unnamed x10 -> x0, local copies, waits for them, and re-layouts: 3.87 us -> none
    select_n x2 -> x0, local copies, waits for them, and re-layouts: 3.76 us -> none  [the longest x1 2.54 us: per_device(): kept_half = jnp.where(high_side, high_half, low_half)]
  transfers between devices with their start and end apart: 3 -> 26, of which waited for: 3 -> 10; matrix products, arithmetic and copies ran while one was open for 2% -> 0% of each run, Pallas kernels for 0% -> 11%
where the time goes in v2:
time: 74.7 us; the launch traced here: 74.6 us
  starting transfers between devices  39.5 us (53%)
  waiting for transfers between devices  23.6 us (32%)
  Pallas kernels  10.7 us (14%)
    ppermute x26, starting transfers between devices, swapped(): lax.ppermute(shard, axis, [(i, i ^ apart) for i in range(lax.axis_size(ax...  39.5 us
    ppermute x26, waiting for transfers between devices, swapped(): lax.ppermute(shard, axis, [(i, i ^ apart) for i in range(lax.axis_size(ax...  23.6 us
    pallas_call x1, Pallas kernels, per_device_blocks(): pl.pallas_call(functools.partial(multiply_kernel, nb, per_piece, spans),...  5.76 us
    pallas_call x4, Pallas kernels, gather(): pl.pallas_call(functools.partial(gather_kernel, nb, per_piece, count, len...  1.97 us
    pallas_call x2, Pallas kernels, per_device_blocks(): pl.pallas_call(functools.partial(route_kernel, nb, per_piece, subs, count...  1.93 us
  transfers between devices with their start and end apart: 26, of which 10 were waited for; matrix products, arithmetic and copies ran while one was open for 0% of the time, Pallas kernels for 11%

profile of v2, /device:TPU:0, one launch (start us, length us, event | category | flops | bytes accessed | tf_op | source)
XLA Modules:
  0.0 74.6 jit_solution(15269204221588249412)
XLA Ops:
  0.0 3.0 %collective-permute-start = (s32[1,1,8]{2,1,0:T(1,128)}, s32[1,1,8]{2,1,0:T(1,128)S(1)}, u32[]{:S(2)}, u32[]{:S(2)}) collective-permute-start(s32[1,1,8]{2,1,0:T(1,128)} %map_any.1), channel_id=1, source_target_pairs={{0,8},{8,0},{16,24},{24,16},{1,9},{9,1},{17,25},{25,17},{2,10},{10... | collective-permute-start | bytes 104 | tf_op jit(solution)/shard_map/ppermute | solution.py:22
  3.0 2.5 %collective-permute-start.2 = (s32[1,1,8]{2,1,0:T(1,128)}, s32[1,1,8]{2,1,0:T(1,128)S(1)}, u32[]{:S(2)}, u32[]{:S(2)}) collective-permute-start(s32[1,1,8]{2,1,0:T(1,128)} %map_any.1), channel_id=1, source_target_pairs={{0,24},{8,16},{16,8},{24,0},{1,25},{9,17},{17,9},{25,1},{2,26},{10... | collective-permute-start | bytes 104 | tf_op jit(solution)/shard_map/ppermute | solution.py:22
  5.6 5.8 %shard_map.46 = (f32[8,256,128]{2,1,0:T(8,128)S(1)}, f32[8,256,128]{2,1,0:T(8,128)S(1)}, f32[8,256,128]{2,1,0:T(8,128)S(1)}, f32[8,256,128]{2,1,0:T(8,128)S(1)}, s32[2,8]{1,0:T(2,128)S(1)}) custom-call(s32[1,1,8]{2,1,0:T(1,128)} %child_any.1, s32[1,1,8,8]{3,2,1,0:T(8,128)} %pattern_any.1, s32[1,1,8]{2,1,0:T(1,128)} %map_any.1, bf16[1024,2048]{1,0:T(8,128)(2,1)} %bitcast.33), custom_call_target="tpu_custom_call" | custom-call | flops 4294967296 | bytes 4194304 | tf_op jit(solution)/shard_map/pallas_call | solution.py:238
  11.4 0.9 %shard_map.47 = f32[8,232,128]{2,1,0:T(8,128)S(1)} custom-call(s32[2,8]{1,0:T(2,128)S(1)} %get-tuple-element.26.plan_ref, s32[1,1,8]{2,1,0:T(1,128)S(1)} %collective-permute-done.refs_0_, s32[1,1,8]{2,1,0:T(1,128)S(1)} %collective-permute-done.1.refs_1_, s32[1,1,8]{2,1,0:T(1,128)S(1)} %collective-permute-done.2.refs_2_, ...), custom_call_target="tpu_custom_call" | custom-call | tf_op jit(solution)/shard_map/pallas_call | solution.py:263
  12.5 1.8 %collective-permute-done.3.crossed_ref = f32[4,232,128]{2,1,0:T(8,128)S(1)} collective-permute-done((f32[4,232,128]{2,1,0:T(8,128)S(1)}, f32[4,232,128]{2,1,0:T(8,128)S(1)}, u32[]{:S(2)}, u32[]{:S(2)}) %collective-permute-start.3) | collective-permute-done | bytes 475168 | tf_op jit(solution)/shard_map/ppermute | solution.py:22
  14.4 1.0 %shard_map.51 = f32[8,696,128]{2,1,0:T(8,128)S(1)} custom-call(s32[2,8]{1,0:T(2,128)S(1)} %get-tuple-element.26.plan_ref, s32[1,1,8]{2,1,0:T(1,128)S(1)} %collective-permute-done.refs_0_, s32[1,1,8]{2,1,0:T(1,128)S(1)} %collective-permute-done.1.refs_1_, s32[1,1,8]{2,1,0:T(1,128)S(1)} %collective-permute-done.2.refs_2_, ...), custom_call_target="tpu_custom_call" | custom-call | tf_op jit(solution)/shard_map/pallas_call | solution.py:263
  15.7 1.6 %collective-permute-start.4 = (f32[2,232,128]{2,1,0:T(8,128)S(1)}, f32[2,232,128]{2,1,0:T(8,128)S(1)}, u32[]{:S(2)}, u32[]{:S(2)}) collective-permute-start(f32[2,232,128]{2,1,0:T(8,128)S(1)} %shard_map.48.refs_6_), channel_id=1, source_target_pairs={{0,2},{1,3},{2,0},{3,1},{4,6},{5,7},{6,4},{7,5},{8,10},{9,11},{10,... | collective-permute-start | bytes 712712 | tf_op jit(solution)/shard_map/ppermute | solution.py:22
  17.3 1.5 %collective-permute-start.5 = (f32[2,232,128]{2,1,0:T(8,128)S(1)}, f32[2,232,128]{2,1,0:T(8,128)S(1)}, u32[]{:S(2)}, u32[]{:S(2)}) collective-permute-start(f32[2,232,128]{2,1,0:T(8,128)S(1)} %shard_map.49.refs_7_), channel_id=1, source_target_pairs={{0,4},{1,5},{2,6},{3,7},{4,0},{5,1},{6,2},{7,3},{8,12},{9,13},{10,... | collective-permute-start | bytes 712712 | tf_op jit(solution)/shard_map/ppermute | solution.py:22
  19.6 4.8 %collective-permute-done.4.refs_0_.refs_2_ = f32[2,232,128]{2,1,0:T(8,128)S(1)} collective-permute-done((f32[2,232,128]{2,1,0:T(8,128)S(1)}, f32[2,232,128]{2,1,0:T(8,128)S(1)}, u32[]{:S(2)}, u32[]{:S(2)}) %collective-permute-start.4) | collective-permute-done | bytes 237600 | tf_op jit(solution)/shard_map/ppermute | solution.py:22
  24.4 1.6 %collective-permute-start.9 = (f32[2,232,128]{2,1,0:T(8,128)S(1)}, f32[2,232,128]{2,1,0:T(8,128)S(1)}, u32[]{:S(2)}, u32[]{:S(2)}) collective-permute-start(f32[2,232,128]{2,1,0:T(8,128)S(1)} %shard_map.52.refs_5_), channel_id=1, source_target_pairs={{0,2},{1,3},{2,0},{3,1},{4,6},{5,7},{6,4},{7,5},{8,10},{9,11},{10,... | collective-permute-start | bytes 712712 | tf_op jit(solution)/shard_map/ppermute | solution.py:22
  26.0 1.6 %collective-permute-start.11 = (f32[2,232,128]{2,1,0:T(8,128)S(1)}, f32[2,232,128]{2,1,0:T(8,128)S(1)}, u32[]{:S(2)}, u32[]{:S(2)}) collective-permute-start(f32[2,232,128]{2,1,0:T(8,128)S(1)} %shard_map.53.refs_6_), channel_id=1, source_target_pairs={{0,4},{1,5},{2,6},{3,7},{4,0},{5,1},{6,2},{7,3},{8,12},{9,13},{10,... | collective-permute-start | bytes 712712 | tf_op jit(solution)/shard_map/ppermute | solution.py:22
  27.6 2.5 %collective-permute-done.5.refs_0_.refs_3_ = f32[2,232,128]{2,1,0:T(8,128)S(1)} collective-permute-done((f32[2,232,128]{2,1,0:T(8,128)S(1)}, f32[2,232,128]{2,1,0:T(8,128)S(1)}, u32[]{:S(2)}, u32[]{:S(2)}) %collective-permute-start.5) | collective-permute-done | bytes 237600 | tf_op jit(solution)/shard_map/ppermute | solution.py:22
  30.1 1.6 %collective-permute-start.12 = (f32[2,232,128]{2,1,0:T(8,128)S(1)}, f32[2,232,128]{2,1,0:T(8,128)S(1)}, u32[]{:S(2)}, u32[]{:S(2)}) collective-permute-start(f32[2,232,128]{2,1,0:T(8,128)S(1)} %shard_map.54.refs_7_), channel_id=1, source_target_pairs={{0,6},{1,7},{2,4},{3,5},{4,2},{5,3},{6,0},{7,1},{8,14},{9,15},{10,... | collective-permute-start | bytes 712712 | tf_op jit(solution)/shard_map/ppermute | solution.py:22
  32.2 1.9 %collective-permute-start.8 = (f32[2,3,2,32,128]{4,3,2,1,0:T(8,128)S(1)}, f32[2,3,2,32,128]{4,3,2,1,0:T(8,128)S(1)}, u32[]{:S(2)}, u32[]{:S(2)}) collective-permute-start(f32[2,3,2,32,128]{4,3,2,1,0:T(8,128)S(1)} %pad_maximum_fusion), channel_id=1, source_target_pairs={{0,8},{8,0},{16,24},{24,16},{1,9},{9,1},{17,25},{25,17},{2,10},{10... | collective-permute-start | bytes 589832 | tf_op jit(solution)/shard_map/ppermute | solution.py:22
  34.7 1.9 %collective-permute-start.14 = (f32[2,232,128]{2,1,0:T(8,128)S(1)}, f32[2,232,128]{2,1,0:T(8,128)S(1)}, u32[]{:S(2)}, u32[]{:S(2)}) collective-permute-start(f32[2,232,128]{2,1,0:T(8,128)S(1)} %shard_map.56.refs_2_.refs_5_), channel_id=1, source_target_pairs={{0,2},{1,3},{2,0},{3,1},{4,6},{5,7},{6,4},{7,5},{8,10},{9,11},{10,... | collective-permute-start | bytes 712712 | tf_op jit(solution)/shard_map/ppermute | solution.py:22
  36.6 1.2 %collective-permute-start.16 = (f32[2,232,128]{2,1,0:T(8,128)S(1)}, f32[2,232,128]{2,1,0:T(8,128)S(1)}, u32[]{:S(2)}, u32[]{:S(2)}) collective-permute-start(f32[2,232,128]{2,1,0:T(8,128)S(1)} %shard_map.57.refs_3_.refs_6_), channel_id=1, source_target_pairs={{0,4},{1,5},{2,6},{3,7},{4,0},{5,1},{6,2},{7,3},{8,12},{9,13},{10,... | collective-permute-start | bytes 712712 | tf_op jit(solution)/shard_map/ppermute | solution.py:22
  38.0 2.9 %collective-permute-start.10 = (f32[1,3,2,32,128]{4,3,2,1,0:T(8,128)S(1)}, f32[1,3,2,32,128]{4,3,2,1,0:T(8,128)S(1)}, u32[]{:S(2)}, u32[]{:S(2)}) collective-permute-start(f32[1,3,2,32,128]{4,3,2,1,0:T(8,128)S(1)} %bitcast.32), channel_id=1, source_target_pairs={{0,16},{8,24},{16,0},{24,8},{1,17},{9,25},{17,1},{25,9},{2,18},{10... | collective-permute-start | bytes 294920 | tf_op jit(solution)/shard_map/ppermute | solution.py:22
  40.9 1.4 %collective-permute-start.17 = (f32[2,232,128]{2,1,0:T(8,128)S(1)}, f32[2,232,128]{2,1,0:T(8,128)S(1)}, u32[]{:S(2)}, u32[]{:S(2)}) collective-permute-start(f32[2,232,128]{2,1,0:T(8,128)S(1)} %shard_map.59.refs_7_), channel_id=1, source_target_pairs={{0,6},{1,7},{2,4},{3,5},{4,2},{5,3},{6,0},{7,1},{8,14},{9,15},{10,... | collective-permute-start | bytes 712712 | tf_op jit(solution)/shard_map/ppermute | solution.py:22
  42.8 1.4 %collective-permute-start.13 = (f32[2,3,2,32,128]{4,3,2,1,0:T(8,128)S(1)}, f32[2,3,2,32,128]{4,3,2,1,0:T(8,128)S(1)}, u32[]{:S(2)}, u32[]{:S(2)}) collective-permute-start(f32[2,3,2,32,128]{4,3,2,1,0:T(8,128)S(1)} %pad_maximum_fusion.1), channel_id=1, source_target_pairs={{0,8},{8,0},{16,24},{24,16},{1,9},{9,1},{17,25},{25,17},{2,10},{10... | collective-permute-start | bytes 589832 | tf_op jit(solution)/shard_map/ppermute | solution.py:22
  44.3 1.6 %collective-permute-done.14.refs_0_.refs_2_ = f32[2,232,128]{2,1,0:T(8,128)S(1)} collective-permute-done((f32[2,232,128]{2,1,0:T(8,128)S(1)}, f32[2,232,128]{2,1,0:T(8,128)S(1)}, u32[]{:S(2)}, u32[]{:S(2)}) %collective-permute-start.14) | collective-permute-done | bytes 237600 | tf_op jit(solution)/shard_map/ppermute | solution.py:22
  46.8 1.3 %collective-permute-start.21 = (f32[2,232,128]{2,1,0:T(8,128)S(1)}, f32[2,232,128]{2,1,0:T(8,128)S(1)}, u32[]{:S(2)}, u32[]{:S(2)}) collective-permute-start(f32[2,232,128]{2,1,0:T(8,128)S(1)} %shard_map.62.refs_3_.refs_6_), channel_id=1, source_target_pairs={{0,4},{1,5},{2,6},{3,7},{4,0},{5,1},{6,2},{7,3},{8,12},{9,13},{10,... | collective-permute-start | bytes 712712 | tf_op jit(solution)/shard_map/ppermute | solution.py:22
  48.0 2.2 %collective-permute-done.16.refs_0_.refs_3_ = f32[2,232,128]{2,1,0:T(8,128)S(1)} collective-permute-done((f32[2,232,128]{2,1,0:T(8,128)S(1)}, f32[2,232,128]{2,1,0:T(8,128)S(1)}, u32[]{:S(2)}, u32[]{:S(2)}) %collective-permute-start.16) | collective-permute-done | bytes 237600 | tf_op jit(solution)/shard_map/ppermute | solution.py:22
  50.3 1.5 %collective-permute-start.22 = (f32[2,232,128]{2,1,0:T(8,128)S(1)}, f32[2,232,128]{2,1,0:T(8,128)S(1)}, u32[]{:S(2)}, u32[]{:S(2)}) collective-permute-start(f32[2,232,128]{2,1,0:T(8,128)S(1)} %shard_map.64.refs_7_), channel_id=1, source_target_pairs={{0,6},{1,7},{2,4},{3,5},{4,2},{5,3},{6,0},{7,1},{8,14},{9,15},{10,... | collective-permute-start | bytes 712712 | tf_op jit(solution)/shard_map/ppermute | solution.py:22
  52.3 1.9 %collective-permute-start.18 = (f32[2,3,2,32,128]{4,3,2,1,0:T(8,128)S(1)}, f32[2,3,2,32,128]{4,3,2,1,0:T(8,128)S(1)}, u32[]{:S(2)}, u32[]{:S(2)}) collective-permute-start(f32[2,3,2,32,128]{4,3,2,1,0:T(8,128)S(1)} %pad_maximum_fusion.2), channel_id=1, source_target_pairs={{0,8},{8,0},{16,24},{24,16},{1,9},{9,1},{17,25},{25,17},{2,10},{10... | collective-permute-start | bytes 589832 | tf_op jit(solution)/shard_map/ppermute | solution.py:22
  54.2 1.8 %collective-permute-start.15 = (f32[1,3,2,32,128]{4,3,2,1,0:T(8,128)S(1)}, f32[1,3,2,32,128]{4,3,2,1,0:T(8,128)S(1)}, u32[]{:S(2)}, u32[]{:S(2)}) collective-permute-start(f32[1,3,2,32,128]{4,3,2,1,0:T(8,128)S(1)} %bitcast.31), channel_id=1, source_target_pairs={{0,16},{8,24},{16,0},{24,8},{1,17},{9,25},{17,1},{25,9},{2,18},{10... | collective-permute-start | bytes 294920 | tf_op jit(solution)/shard_map/ppermute | solution.py:22
  56.0 2.8 %collective-permute-done.18.refs_1_ = f32[2,3,2,32,128]{4,3,2,1,0:T(8,128)S(1)} collective-permute-done((f32[2,3,2,32,128]{4,3,2,1,0:T(8,128)S(1)}, f32[2,3,2,32,128]{4,3,2,1,0:T(8,128)S(1)}, u32[]{:S(2)}, u32[]{:S(2)}) %collective-permute-start.18) | collective-permute-done | bytes 196640 | tf_op jit(solution)/shard_map/ppermute | solution.py:22
  58.8 2.9 %collective-permute-start.19 = (f32[1,3,2,32,128]{4,3,2,1,0:T(8,128)S(1)}, f32[1,3,2,32,128]{4,3,2,1,0:T(8,128)S(1)}, u32[]{:S(2)}, u32[]{:S(2)}) collective-permute-start(f32[1,3,2,32,128]{4,3,2,1,0:T(8,128)S(1)} %bitcast.24), channel_id=1, source_target_pairs={{0,16},{8,24},{16,0},{24,8},{1,17},{9,25},{17,1},{25,9},{2,18},{10... | collective-permute-start | bytes 294920 | tf_op jit(solution)/shard_map/ppermute | solution.py:22
  62.2 0.9 %collective-permute-start.23 = (f32[3,2,32,128]{3,2,1,0:T(8,128)S(1)}, f32[3,2,32,128]{3,2,1,0:T(8,128)S(1)}, u32[]{:S(2)}, u32[]{:S(2)}) collective-permute-start(f32[3,2,32,128]{3,2,1,0:T(8,128)S(1)} %get-tuple-element.44), channel_id=1, source_target_pairs={{0,8},{8,0},{16,24},{24,16},{1,9},{9,1},{17,25},{25,17},{2,10},{10... | collective-permute-start | bytes 294920 | tf_op jit(solution)/shard_map/ppermute | solution.py:22
  63.0 1.7 %collective-permute-start.24 = (f32[3,2,32,128]{3,2,1,0:T(8,128)S(1)}, f32[3,2,32,128]{3,2,1,0:T(8,128)S(1)}, u32[]{:S(2)}, u32[]{:S(2)}) collective-permute-start(f32[3,2,32,128]{3,2,1,0:T(8,128)S(1)} %get-tuple-element.45), channel_id=1, source_target_pairs={{0,16},{8,24},{16,0},{24,8},{1,17},{9,25},{17,1},{25,9},{2,18},{10... | collective-permute-start | bytes 294920 | tf_op jit(solution)/shard_map/ppermute | solution.py:22
  64.7 1.9 %collective-permute-start.25 = (f32[3,2,32,128]{3,2,1,0:T(8,128)S(1)}, f32[3,2,32,128]{3,2,1,0:T(8,128)S(1)}, u32[]{:S(2)}, u32[]{:S(2)}) collective-permute-start(f32[3,2,32,128]{3,2,1,0:T(8,128)S(1)} %get-tuple-element.46), channel_id=1, source_target_pairs={{0,24},{8,16},{16,8},{24,0},{1,25},{9,17},{17,9},{25,1},{2,26},{10... | collective-permute-start | bytes 294920 | tf_op jit(solution)/shard_map/ppermute | solution.py:22
  66.7 1.4 %collective-permute-done.23.refs_10_ = f32[3,2,32,128]{3,2,1,0:T(8,128)S(1)} collective-permute-done((f32[3,2,32,128]{3,2,1,0:T(8,128)S(1)}, f32[3,2,32,128]{3,2,1,0:T(8,128)S(1)}, u32[]{:S(2)}, u32[]{:S(2)}) %collective-permute-start.23) | collective-permute-done | bytes 98336 | tf_op jit(solution)/shard_map/ppermute | solution.py:22
  68.1 5.6 %collective-permute-done.24.refs_11_ = f32[3,2,32,128]{3,2,1,0:T(8,128)S(1)} collective-permute-done((f32[3,2,32,128]{3,2,1,0:T(8,128)S(1)}, f32[3,2,32,128]{3,2,1,0:T(8,128)S(1)}, u32[]{:S(2)}, u32[]{:S(2)}) %collective-permute-start.24) | collective-permute-done | bytes 98336 | tf_op jit(solution)/shard_map/ppermute | solution.py:22
  (57 shorter events, 5.9 us)
Async XLA Ops:
  0.0 11.4 %collective-permute-start = (s32[1,1,8]{2,1,0:T(1,128)}, s32[1,1,8]{2,1,0:T(1,128)S(1)}, u32[]{:S(2)}, u32[]{:S(2)}) collective-permute-start(s32[1,1,8]{2,1,0:T(1,128)} %map_any.1), channel_id=1, source_target_pairs={{0,8},{8,0},{16,24},{24,16},{1,9},{9,1},{17,25},{25,17},{2,10},{10... | collective-permute-start | bytes 104 | tf_op jit(solution)/shard_map/ppermute | solution.py:22
  3.0 8.4 %collective-permute-start.2 = (s32[1,1,8]{2,1,0:T(1,128)}, s32[1,1,8]{2,1,0:T(1,128)S(1)}, u32[]{:S(2)}, u32[]{:S(2)}) collective-permute-start(s32[1,1,8]{2,1,0:T(1,128)} %map_any.1), channel_id=1, source_target_pairs={{0,24},{8,16},{16,8},{24,0},{1,25},{9,17},{17,9},{25,1},{2,26},{10... | collective-permute-start | bytes 104 | tf_op jit(solution)/shard_map/ppermute | solution.py:22
  5.5 5.9 %collective-permute-start.1 = (s32[1,1,8]{2,1,0:T(1,128)}, s32[1,1,8]{2,1,0:T(1,128)S(1)}, u32[]{:S(2)}, u32[]{:S(2)}) collective-permute-start(s32[1,1,8]{2,1,0:T(1,128)} %map_any.1), channel_id=1, source_target_pairs={{0,16},{8,24},{16,0},{24,8},{1,17},{9,25},{17,1},{25,9},{2,18},{10... | collective-permute-start | bytes 104 | tf_op jit(solution)/shard_map/ppermute | solution.py:22
  12.4 1.9 %collective-permute-start.3 = (f32[4,232,128]{2,1,0:T(8,128)S(1)}, f32[4,232,128]{2,1,0:T(8,128)S(1)}, u32[]{:S(2)}, u32[]{:S(2)}) collective-permute-start(f32[4,232,128]{2,1,0:T(8,128)S(1)} %get-tuple-element.60), channel_id=1, source_target_pairs={{0,1},{1,0},{2,3},{3,2},{4,5},{5,4},{6,7},{7,6},{8,9},{9,8},{10,11... | collective-permute-start | bytes 1425416 | tf_op jit(solution)/shard_map/ppermute | solution.py:22
  15.5 3.9 %collective-permute-start.7 = (f32[4,696,128]{2,1,0:T(8,128)S(1)}, f32[4,696,128]{2,1,0:T(8,128)S(1)}, u32[]{:S(2)}, u32[]{:S(2)}) collective-permute-start(f32[4,696,128]{2,1,0:T(8,128)S(1)} %slice.96), channel_id=1, source_target_pairs={{0,1},{1,0},{2,3},{3,2},{4,5},{5,4},{6,7},{7,6},{8,9},{9,8},{10,11... | collective-permute-start | bytes 4276232 | tf_op jit(solution)/shard_map/ppermute | solution.py:22
  15.7 8.7 %collective-permute-start.4 = (f32[2,232,128]{2,1,0:T(8,128)S(1)}, f32[2,232,128]{2,1,0:T(8,128)S(1)}, u32[]{:S(2)}, u32[]{:S(2)}) collective-permute-start(f32[2,232,128]{2,1,0:T(8,128)S(1)} %shard_map.48.refs_6_), channel_id=1, source_target_pairs={{0,2},{1,3},{2,0},{3,1},{4,6},{5,7},{6,4},{7,5},{8,10},{9,11},{10,... | collective-permute-start | bytes 712712 | tf_op jit(solution)/shard_map/ppermute | solution.py:22
  17.3 12.8 %collective-permute-start.5 = (f32[2,232,128]{2,1,0:T(8,128)S(1)}, f32[2,232,128]{2,1,0:T(8,128)S(1)}, u32[]{:S(2)}, u32[]{:S(2)}) collective-permute-start(f32[2,232,128]{2,1,0:T(8,128)S(1)} %shard_map.49.refs_7_), channel_id=1, source_target_pairs={{0,4},{1,5},{2,6},{3,7},{4,0},{5,1},{6,2},{7,3},{8,12},{9,13},{10,... | collective-permute-start | bytes 712712 | tf_op jit(solution)/shard_map/ppermute | solution.py:22
  18.8 12.9 %collective-permute-start.6 = (f32[2,232,128]{2,1,0:T(8,128)S(1)}, f32[2,232,128]{2,1,0:T(8,128)S(1)}, u32[]{:S(2)}, u32[]{:S(2)}) collective-permute-start(f32[2,232,128]{2,1,0:T(8,128)S(1)} %shard_map.50.refs_8_), channel_id=1, source_target_pairs={{0,6},{1,7},{2,4},{3,5},{4,2},{5,3},{6,0},{7,1},{8,14},{9,15},{10,... | collective-permute-start | bytes 712712 | tf_op jit(solution)/shard_map/ppermute | solution.py:22
  24.4 10.2 %collective-permute-start.9 = (f32[2,232,128]{2,1,0:T(8,128)S(1)}, f32[2,232,128]{2,1,0:T(8,128)S(1)}, u32[]{:S(2)}, u32[]{:S(2)}) collective-permute-start(f32[2,232,128]{2,1,0:T(8,128)S(1)} %shard_map.52.refs_5_), channel_id=1, source_target_pairs={{0,2},{1,3},{2,0},{3,1},{4,6},{5,7},{6,4},{7,5},{8,10},{9,11},{10,... | collective-permute-start | bytes 712712 | tf_op jit(solution)/shard_map/ppermute | solution.py:22
  26.0 14.9 %collective-permute-start.11 = (f32[2,232,128]{2,1,0:T(8,128)S(1)}, f32[2,232,128]{2,1,0:T(8,128)S(1)}, u32[]{:S(2)}, u32[]{:S(2)}) collective-permute-start(f32[2,232,128]{2,1,0:T(8,128)S(1)} %shard_map.53.refs_6_), channel_id=1, source_target_pairs={{0,4},{1,5},{2,6},{3,7},{4,0},{5,1},{6,2},{7,3},{8,12},{9,13},{10,... | collective-permute-start | bytes 712712 | tf_op jit(solution)/shard_map/ppermute | solution.py:22
  30.1 12.2 %collective-permute-start.12 = (f32[2,232,128]{2,1,0:T(8,128)S(1)}, f32[2,232,128]{2,1,0:T(8,128)S(1)}, u32[]{:S(2)}, u32[]{:S(2)}) collective-permute-start(f32[2,232,128]{2,1,0:T(8,128)S(1)} %shard_map.54.refs_7_), channel_id=1, source_target_pairs={{0,6},{1,7},{2,4},{3,5},{4,2},{5,3},{6,0},{7,1},{8,14},{9,15},{10,... | collective-permute-start | bytes 712712 | tf_op jit(solution)/shard_map/ppermute | solution.py:22
  32.2 5.7 %collective-permute-start.8 = (f32[2,3,2,32,128]{4,3,2,1,0:T(8,128)S(1)}, f32[2,3,2,32,128]{4,3,2,1,0:T(8,128)S(1)}, u32[]{:S(2)}, u32[]{:S(2)}) collective-permute-start(f32[2,3,2,32,128]{4,3,2,1,0:T(8,128)S(1)} %pad_maximum_fusion), channel_id=1, source_target_pairs={{0,8},{8,0},{16,24},{24,16},{1,9},{9,1},{17,25},{25,17},{2,10},{10... | collective-permute-start | bytes 589832 | tf_op jit(solution)/shard_map/ppermute | solution.py:22
  34.7 11.2 %collective-permute-start.14 = (f32[2,232,128]{2,1,0:T(8,128)S(1)}, f32[2,232,128]{2,1,0:T(8,128)S(1)}, u32[]{:S(2)}, u32[]{:S(2)}) collective-permute-start(f32[2,232,128]{2,1,0:T(8,128)S(1)} %shard_map.56.refs_2_.refs_5_), channel_id=1, source_target_pairs={{0,2},{1,3},{2,0},{3,1},{4,6},{5,7},{6,4},{7,5},{8,10},{9,11},{10,... | collective-permute-start | bytes 712712 | tf_op jit(solution)/shard_map/ppermute | solution.py:22
  36.6 13.7 %collective-permute-start.16 = (f32[2,232,128]{2,1,0:T(8,128)S(1)}, f32[2,232,128]{2,1,0:T(8,128)S(1)}, u32[]{:S(2)}, u32[]{:S(2)}) collective-permute-start(f32[2,232,128]{2,1,0:T(8,128)S(1)} %shard_map.57.refs_3_.refs_6_), channel_id=1, source_target_pairs={{0,4},{1,5},{2,6},{3,7},{4,0},{5,1},{6,2},{7,3},{8,12},{9,13},{10,... | collective-permute-start | bytes 712712 | tf_op jit(solution)/shard_map/ppermute | solution.py:22
  38.0 8.8 %collective-permute-start.10 = (f32[1,3,2,32,128]{4,3,2,1,0:T(8,128)S(1)}, f32[1,3,2,32,128]{4,3,2,1,0:T(8,128)S(1)}, u32[]{:S(2)}, u32[]{:S(2)}) collective-permute-start(f32[1,3,2,32,128]{4,3,2,1,0:T(8,128)S(1)} %bitcast.32), channel_id=1, source_target_pairs={{0,16},{8,24},{16,0},{24,8},{1,17},{9,25},{17,1},{25,9},{2,18},{10... | collective-permute-start | bytes 294920 | tf_op jit(solution)/shard_map/ppermute | solution.py:22
  40.9 10.9 %collective-permute-start.17 = (f32[2,232,128]{2,1,0:T(8,128)S(1)}, f32[2,232,128]{2,1,0:T(8,128)S(1)}, u32[]{:S(2)}, u32[]{:S(2)}) collective-permute-start(f32[2,232,128]{2,1,0:T(8,128)S(1)} %shard_map.59.refs_7_), channel_id=1, source_target_pairs={{0,6},{1,7},{2,4},{3,5},{4,2},{5,3},{6,0},{7,1},{8,14},{9,15},{10,... | collective-permute-start | bytes 712712 | tf_op jit(solution)/shard_map/ppermute | solution.py:22
  42.8 11.4 %collective-permute-start.13 = (f32[2,3,2,32,128]{4,3,2,1,0:T(8,128)S(1)}, f32[2,3,2,32,128]{4,3,2,1,0:T(8,128)S(1)}, u32[]{:S(2)}, u32[]{:S(2)}) collective-permute-start(f32[2,3,2,32,128]{4,3,2,1,0:T(8,128)S(1)} %pad_maximum_fusion.1), channel_id=1, source_target_pairs={{0,8},{8,0},{16,24},{24,16},{1,9},{9,1},{17,25},{25,17},{2,10},{10... | collective-permute-start | bytes 589832 | tf_op jit(solution)/shard_map/ppermute | solution.py:22
  45.9 15.8 %collective-permute-start.20 = (f32[2,232,128]{2,1,0:T(8,128)S(1)}, f32[2,232,128]{2,1,0:T(8,128)S(1)}, u32[]{:S(2)}, u32[]{:S(2)}) collective-permute-start(f32[2,232,128]{2,1,0:T(8,128)S(1)} %shard_map.61.refs_2_.refs_5_), channel_id=1, source_target_pairs={{0,2},{1,3},{2,0},{3,1},{4,6},{5,7},{6,4},{7,5},{8,10},{9,11},{10,... | collective-permute-start | bytes 712712 | tf_op jit(solution)/shard_map/ppermute | solution.py:22
  46.8 14.9 %collective-permute-start.21 = (f32[2,232,128]{2,1,0:T(8,128)S(1)}, f32[2,232,128]{2,1,0:T(8,128)S(1)}, u32[]{:S(2)}, u32[]{:S(2)}) collective-permute-start(f32[2,232,128]{2,1,0:T(8,128)S(1)} %shard_map.62.refs_3_.refs_6_), channel_id=1, source_target_pairs={{0,4},{1,5},{2,6},{3,7},{4,0},{5,1},{6,2},{7,3},{8,12},{9,13},{10,... | collective-permute-start | bytes 712712 | tf_op jit(solution)/shard_map/ppermute | solution.py:22
  50.3 11.4 %collective-permute-start.22 = (f32[2,232,128]{2,1,0:T(8,128)S(1)}, f32[2,232,128]{2,1,0:T(8,128)S(1)}, u32[]{:S(2)}, u32[]{:S(2)}) collective-permute-start(f32[2,232,128]{2,1,0:T(8,128)S(1)} %shard_map.64.refs_7_), channel_id=1, source_target_pairs={{0,6},{1,7},{2,4},{3,5},{4,2},{5,3},{6,0},{7,1},{8,14},{9,15},{10,... | collective-permute-start | bytes 712712 | tf_op jit(solution)/shard_map/ppermute | solution.py:22
  52.3 6.5 %collective-permute-start.18 = (f32[2,3,2,32,128]{4,3,2,1,0:T(8,128)S(1)}, f32[2,3,2,32,128]{4,3,2,1,0:T(8,128)S(1)}, u32[]{:S(2)}, u32[]{:S(2)}) collective-permute-start(f32[2,3,2,32,128]{4,3,2,1,0:T(8,128)S(1)} %pad_maximum_fusion.2), channel_id=1, source_target_pairs={{0,8},{8,0},{16,24},{24,16},{1,9},{9,1},{17,25},{25,17},{2,10},{10... | collective-permute-start | bytes 589832 | tf_op jit(solution)/shard_map/ppermute | solution.py:22
  54.2 12.4 %collective-permute-start.15 = (f32[1,3,2,32,128]{4,3,2,1,0:T(8,128)S(1)}, f32[1,3,2,32,128]{4,3,2,1,0:T(8,128)S(1)}, u32[]{:S(2)}, u32[]{:S(2)}) collective-permute-start(f32[1,3,2,32,128]{4,3,2,1,0:T(8,128)S(1)} %bitcast.31), channel_id=1, source_target_pairs={{0,16},{8,24},{16,0},{24,8},{1,17},{9,25},{17,1},{25,9},{2,18},{10... | collective-permute-start | bytes 294920 | tf_op jit(solution)/shard_map/ppermute | solution.py:22
  58.8 7.8 %collective-permute-start.19 = (f32[1,3,2,32,128]{4,3,2,1,0:T(8,128)S(1)}, f32[1,3,2,32,128]{4,3,2,1,0:T(8,128)S(1)}, u32[]{:S(2)}, u32[]{:S(2)}) collective-permute-start(f32[1,3,2,32,128]{4,3,2,1,0:T(8,128)S(1)} %bitcast.24), channel_id=1, source_target_pairs={{0,16},{8,24},{16,0},{24,8},{1,17},{9,25},{17,1},{25,9},{2,18},{10... | collective-permute-start | bytes 294920 | tf_op jit(solution)/shard_map/ppermute | solution.py:22
  62.2 5.9 %collective-permute-start.23 = (f32[3,2,32,128]{3,2,1,0:T(8,128)S(1)}, f32[3,2,32,128]{3,2,1,0:T(8,128)S(1)}, u32[]{:S(2)}, u32[]{:S(2)}) collective-permute-start(f32[3,2,32,128]{3,2,1,0:T(8,128)S(1)} %get-tuple-element.44), channel_id=1, source_target_pairs={{0,8},{8,0},{16,24},{24,16},{1,9},{9,1},{17,25},{25,17},{2,10},{10... | collective-permute-start | bytes 294920 | tf_op jit(solution)/shard_map/ppermute | solution.py:22
  63.0 10.7 %collective-permute-start.24 = (f32[3,2,32,128]{3,2,1,0:T(8,128)S(1)}, f32[3,2,32,128]{3,2,1,0:T(8,128)S(1)}, u32[]{:S(2)}, u32[]{:S(2)}) collective-permute-start(f32[3,2,32,128]{3,2,1,0:T(8,128)S(1)} %get-tuple-element.45), channel_id=1, source_target_pairs={{0,16},{8,24},{16,0},{24,8},{1,17},{9,25},{17,1},{25,9},{2,18},{10... | collective-permute-start | bytes 294920 | tf_op jit(solution)/shard_map/ppermute | solution.py:22
  64.7 9.0 %collective-permute-start.25 = (f32[3,2,32,128]{3,2,1,0:T(8,128)S(1)}, f32[3,2,32,128]{3,2,1,0:T(8,128)S(1)}, u32[]{:S(2)}, u32[]{:S(2)}) collective-permute-start(f32[3,2,32,128]{3,2,1,0:T(8,128)S(1)} %get-tuple-element.46), channel_id=1, source_target_pairs={{0,24},{8,16},{16,8},{24,0},{1,25},{9,17},{17,9},{25,1},{2,26},{10... | collective-permute-start | bytes 294920 | tf_op jit(solution)/shard_map/ppermute | solution.py:22

commit v3 on v2

--- a/solution.py
+++ b/solution.py
@@ -9,11 +9,11 @@
 
 ANC_DEV = 3
 META = 8
-CUT = 16
-CHUNK_PARTS = (2, 2, 2, 2)
+CUT = 8
+CHUNK_PARTS = (4, 4, 4, 4)
 DEPS = ((1,), (1,), (2,))
-ZWAIT = 2
 ZDEP = 2
+DIRECT = 1
 GATHER_COST = 128 * 1024 * 1024
 VMEM_LIMIT = 44 * 1024 * 1024
 
@@ -89,7 +89,7 @@
                     put(j, i, value.T)
 
 
-def route_kernel(nb, per_piece, subs, counts, extra, plan_ref, *refs):
+def route_kernel(nb, per_piece, subs, shipments, counts, extra, plan_ref, *refs):
     slot_refs = refs[: subs - 1]
     update_refs = refs[subs - 1 : subs - 1 + len(counts)]
     out_ref, goal = refs[subs - 1 + len(counts) + extra :]
@@ -99,8 +99,8 @@
     empty = plan_ref[1, 0]
     tails = []
     at = 0
-    for count in counts:
-        tails.append(at + (nb - 1) * count)
+    for shipment in shipments:
+        tails.append(at + shipment_rows(shipment, counts) - META)
         at = tails[-1] + META
     for tail in tails:
         out_ref[:, pl.ds(tail, META), :] = jnp.full((out_ref.shape[0], META, block), empty.astype(jnp.float32))
@@ -114,38 +114,71 @@
             slot = (entry - owner * ANC_DEV).astype(jnp.float32)
             for tail in tails:
                 out_ref[to, pl.ds(tail + 1 + apart, 1), :] = jnp.full((1, block), slot, jnp.float32)
-    for k in range(nb - 1):
-        place = k + (empty <= k).astype(jnp.int32)
-        apart = place // per_piece
-        for c in range(nb):
-            to = goal[apart, c]
-            for tail, count, update_ref in zip(tails, counts, update_refs):
-                out_ref[to, pl.ds(tail - (nb - 1 - k) * count, count), :] = update_ref[c, pl.ds(k * count, count), :]
-
-
-def gather_kernel(nb, per_piece, count, extra, *refs):
-    subs = nb // per_piece
-    in_refs, out_refs = refs[: len(refs) - subs - extra], refs[-subs:]
-    tail = (nb - 1) * count
+    at = 0
+    for kept, chunks in shipments:
+        for k in kept:
+            place = k + (empty <= k).astype(jnp.int32)
+            apart = place // per_piece
+            for chunk in chunks:
+                for c in range(nb):
+                    out_ref[goal[apart, c], pl.ds(at, counts[chunk]), :] = update_refs[chunk][
+                        c, pl.ds(k * counts[chunk], counts[chunk]), :
+                    ]
+                at += counts[chunk]
+        at += META
+
+
+def shipment_rows(shipment, counts):
+    kept, chunks = shipment
+    return len(kept) * sum(counts[chunk] for chunk in chunks) + META
+
+
+def places_in(kept, nb, per_piece):
+    found = {}
+    for place in range(nb):
+        if place in kept or place - 1 in kept:
+            found.setdefault(place // per_piece, []).append(place)
+    return found
+
+
+def gather_kernel(nb, per_piece, kept, count, extra, *refs):
+    found = places_in(kept, nb, per_piece)
+    in_refs, out_refs = refs[: len(refs) - len(found) - extra], refs[-len(found) :]
+    tail = len(kept) * count
     block = in_refs[0].shape[-1]
     sources = []
     for ref in in_refs:
         for index in range(ref.shape[0]):
             sources.append(ref.at[index])
-    for apart in range(subs):
-        for part in range(per_piece):
-            place = apart * per_piece + part
+    for out_ref, (apart, places) in zip(out_refs, found.items()):
+        for part, place in enumerate(places):
             sums = [jnp.zeros((count, block), jnp.float32) for _ in range(ANC_DEV)]
             for source in sources:
                 empty = source[pl.ds(tail, 1), :]
                 slot = source[pl.ds(tail + 1 + apart, 1), :]
-                low = source[pl.ds(min(place, nb - 2) * count, count), :]
-                high = source[pl.ds(max(place - 1, 0) * count, count), :]
-                value = jnp.where(empty > place, low, jnp.where(empty < place, high, 0.0))
+                value = jnp.zeros((count, block), jnp.float32)
+                if place in kept:
+                    value = jnp.where(empty > place, source[pl.ds(kept.index(place) * count, count), :], value)
+                if place - 1 in kept:
+                    value = jnp.where(empty < place, source[pl.ds(kept.index(place - 1) * count, count), :], value)
                 for index in range(ANC_DEV):
                     sums[index] += jnp.where(slot == index, value, 0.0)
             for index in range(ANC_DEV):
-                out_refs[apart][index, part] = sums[index]
+                out_ref[index, part] = sums[index]
+
+
+def pick_kernel(first, in_ref, *refs):
+    refs[-1][...] = in_ref[first:]
+
+
+def pick(params, blocks, first, earlier):
+    return pl.pallas_call(
+        functools.partial(pick_kernel, first),
+        out_shape=jax.ShapeDtypeStruct((blocks.shape[0] - first, *blocks.shape[1:]), blocks.dtype),
+        in_specs=[vmem_spec()] + [pl.BlockSpec(memory_space=pl.ANY)] * len(earlier),
+        out_specs=vmem_spec(),
+        compiler_params=params,
+    )(blocks, *earlier)
 
 
 def pack_kernel(chip, same_ref, crossed_ref, *refs):
@@ -163,14 +196,15 @@
     )(same, crossed, *earlier)
 
 
-def gather(params, nb, per_piece, count, arrived, earlier):
-    subs = nb // per_piece
+def gather(params, nb, per_piece, kept, arrived, earlier):
     block = arrived[0].shape[-1]
+    count = (arrived[0].shape[1] - META) // len(kept)
+    found = places_in(kept, nb, per_piece)
     return pl.pallas_call(
-        functools.partial(gather_kernel, nb, per_piece, count, len(earlier)),
-        out_shape=[jax.ShapeDtypeStruct((ANC_DEV, per_piece, count, block), jnp.float32)] * subs,
+        functools.partial(gather_kernel, nb, per_piece, kept, count, len(earlier)),
+        out_shape=[jax.ShapeDtypeStruct((ANC_DEV, len(places), count, block), jnp.float32) for places in found.values()],
         in_specs=[vmem_spec()] * len(arrived) + [pl.BlockSpec(memory_space=pl.ANY)] * len(earlier),
-        out_specs=[vmem_spec()] * subs,
+        out_specs=[vmem_spec()] * len(found),
         compiler_params=params,
         cost_estimate=pl.CostEstimate(flops=0, bytes_accessed=GATHER_COST, transcendentals=0),
     )(*arrived, *earlier)
@@ -203,14 +237,20 @@
         held.update(zip(kept, sums))
 
 
-def finish_kernel(chunk_rows, shares, *refs):
+def finish_kernel(chunk_rows, shares, near_ref, *refs):
     out_ref = refs[-1]
     start = at = 0
     for count, share in zip(chunk_rows, shares):
-        total = refs[at][...]
-        for part in refs[at + 1 : at + share]:
-            total += part[...]
-        out_ref[0, :, :, pl.ds(start, count), :] = total
+        rows = pl.ds(start, count)
+        for part in range(out_ref.shape[2]):
+            total = refs[at + 1][:, part]
+            for came in refs[at + 2 : at + share]:
+                total += came[:, part]
+            if part < near_ref.shape[1]:
+                total += near_ref[:, part, rows]
+            if part > 0:
+                total += refs[at][:, part - 1]
+            out_ref[0, :, part, rows, :] = total
         start += count
         at += share
 
@@ -256,59 +296,67 @@
         ),
     )(*[pltpu.with_memory_space_constraint(array, pltpu.HBM) for array in (child_map, pattern, ancestor_map, panel)])
     plan = updates[-1]
+    far = list(range(1, nb - 1))
+    shipments = [(far, [chunk]) for chunk in range(len(chunk_rows))]
+    shipments.append(([0], list(range(len(chunk_rows)))))
     laid = []
     earlier = []
-    for first, end in ((0, 1), (1, len(spans))):
-        counts = chunk_rows[first:end]
+    for group in (shipments[:1], shipments[1:]):
+        used = chunk_rows[:1] if not laid else chunk_rows
+        rows = [shipment_rows(shipment, chunk_rows) for shipment in group]
         blocks = pl.pallas_call(
-            functools.partial(route_kernel, nb, per_piece, subs, counts, len(earlier)),
-            out_shape=jax.ShapeDtypeStruct(
-                (trees, (nb - 1) * sum(counts) + META * len(counts), block), jnp.float32
-            ),
+            functools.partial(route_kernel, nb, per_piece, subs, group, used, len(earlier)),
+            out_shape=jax.ShapeDtypeStruct((trees, sum(rows), block), jnp.float32),
             in_specs=[smem_spec()] * subs
-            + [vmem_spec()] * len(counts)
+            + [vmem_spec()] * len(used)
             + [pl.BlockSpec(memory_space=pl.ANY)] * len(earlier),
             out_specs=vmem_spec(),
             scratch_shapes=[pltpu.SMEM((subs, nb), jnp.int32)],
             compiler_params=params,
-        )(plan, *slots, *updates[first:end], *earlier)
-        same, crossed = blocks[:chips], swapped(blocks[chips:], "forest", 1)
+        )(plan, *slots, *updates[: len(used)], *earlier)
+        other = blocks[chips:] if not laid else pick(params, blocks, chips, going_out)
+        same, crossed = blocks[:chips], swapped(other, "forest", 1)
         at = 0
-        for count in counts:
-            rows = (nb - 1) * count + META
-            laid.append((same[:, at : at + rows], crossed[:, at : at + rows]))
-            at += rows
-        if first == 0:
+        for count in rows:
+            laid.append((same[:, at : at + count], crossed[:, at : at + count]))
+            at += count
+        if not earlier:
             going_out = [pack(params, chip, *laid[0]) for chip in range(1, chips)]
-            earlier = going_out
+            earlier = [blocks]
 
     pieces = []
-    arrivals = []
     open_sums = None
-    for c, count in enumerate(chunk_rows):
+    for c, (kept, _) in enumerate(shipments):
         arrived = [laid[c][0][:1], laid[c][1][:1]]
         for chip in range(1, chips):
             arrived.append(swapped(going_out[chip - 1], "forest", 2 * chip))
-        arrivals.append(arrived)
+        last = c == len(shipments) - 1
+        queued = []
         waits = []
-        if c < len(chunk_rows) - 1:
-            going_out = []
-            for chip in range(1, chips):
+        for chip in range(1, chips):
+            if open_sums is not None and chip == chips - 1:
+                held, apart = open_sums[0], 1
+                settle(params, held, pieces[-1], apart, *open_sums[1:], waits)
+                waits = waits + list(held.values())[1:]
+                while 2 * apart < subs:
+                    apart *= 2
+                    settle(params, held, pieces[-1], apart, *send(held, apart), [])
+            if not last:
                 earlier = [arrived[index + 1] for index in DEPS[chip - 1]]
                 if chip == 2 and c > 1 and ZDEP:
                     earlier.append(pieces[c - 2][-1])
-                going_out.append(pack(params, chip, *laid[c + 1], *earlier))
-            waits = list(going_out)
-        if open_sums is not None:
-            held, apart = open_sums[0], 1
-            settle(params, held, pieces[-1], apart, *open_sums[1:], waits[:ZWAIT])
-            while 2 * apart < subs:
-                apart *= 2
-                settle(params, held, pieces[-1], apart, *send(held, apart), [])
-        sums = gather(params, nb, per_piece, count, arrived, waits)
+                if chip == chips - 1:
+                    earlier += waits[chip - 1 :]
+                queued.append(pack(params, chip, *laid[c + 1], *earlier))
+                waits = waits[: chip - 1] + queued[-1:] + waits[chip - 1 :]
+        going_out = queued
+        sums = gather(params, nb, per_piece, kept, arrived, waits)
+        if last:
+            near = sums[0]
+            break
         parts = [sums[0]]
         open_sums = None
-        if c == len(chunk_rows) - 1:
+        if c == len(chunk_rows) - 1 and DIRECT:
             for apart in range(1, subs):
                 parts.append(swapped(sums[apart], "subtree", apart))
         else:
@@ -318,10 +366,10 @@
     out = pl.pallas_call(
         functools.partial(finish_kernel, chunk_rows, [len(parts) for parts in pieces]),
         out_shape=jax.ShapeDtypeStruct((1, ANC_DEV, per_piece, block, block), jnp.float32),
-        in_specs=[vmem_spec()] * sum(len(parts) for parts in pieces),
+        in_specs=[vmem_spec()] * (1 + sum(len(parts) for parts in pieces)),
         out_specs=vmem_spec(),
         compiler_params=params,
-    )(*[part for parts in pieces for part in parts])
+    )(near, *[part for parts in pieces for part in parts])
     return out.reshape(1, ANC_DEV, per_piece * block, block)
 
 
@@ -403,7 +451,7 @@
     def per_device(panels, pattern, child_map, ancestor_map):
         nb = child_map.shape[2]
         subs, trees = mesh.shape["subtree"], mesh.shape["forest"]
-        if nb == trees and nb % subs == 0 and subs < META and trees % 2 == 0:
+        if nb == trees and nb % (2 * subs) == 0 and subs < META:
             return per_device_blocks(panels, pattern, child_map, ancestor_map)
         return per_device_halving(panels, pattern, child_map, ancestor_map)
 

time: 74.7 us -> 70.4 us (0.942)
  waiting for transfers between devices: 23.6 us -> 15.2 us
  starting transfers between devices: 39.5 us -> 43.4 us
    ppermute x26 -> x29, waiting for transfers between devices: 23.6 us -> 15.2 us  [swapped(): lax.ppermute(shard, axis, [(i, i ^ apart) for i in range(lax.axis_size(ax...]
    ppermute x26 -> x29, starting transfers between devices: 39.5 us -> 43.4 us  [swapped(): lax.ppermute(shard, axis, [(i, i ^ apart) for i in range(lax.axis_size(ax...]
    pallas_call x6 -> x8, Pallas kernels: 3.89 us -> 3.99 us  [the longest x2 2.01 us: per_device_blocks(): pl.pallas_call(functools.partial(route_kernel, nb, per_piece, subs, group...]
  transfers between devices with their start and end apart: 26 -> 29, of which waited for: 10 -> 9; matrix products, arithmetic and copies ran while one was open for 0% -> 0% of each run, Pallas kernels for 11% -> 13%
where the time goes in v3:
time: 70.4 us; the launch traced here: 70.1 us
  starting transfers between devices  43.4 us (62%)
  waiting for transfers between devices  15.2 us (22%)
  Pallas kernels  10.8 us (15%)
    ppermute x29, starting transfers between devices, swapped(): lax.ppermute(shard, axis, [(i, i ^ apart) for i in range(lax.axis_size(ax...  43.4 us
    ppermute x29, waiting for transfers between devices, swapped(): lax.ppermute(shard, axis, [(i, i ^ apart) for i in range(lax.axis_size(ax...  15.2 us
    pallas_call x1, Pallas kernels, per_device_blocks(): pl.pallas_call(functools.partial(multiply_kernel, nb, per_piece, spans),...  5.76 us
    pallas_call x2, Pallas kernels, per_device_blocks(): pl.pallas_call(functools.partial(route_kernel, nb, per_piece, subs, group...  2.01 us
    pallas_call x5, Pallas kernels, gather(): pl.pallas_call(functools.partial(gather_kernel, nb, per_piece, kept, coun...  1.88 us
  transfers between devices with their start and end apart: 29, of which 9 were waited for; matrix products, arithmetic and copies ran while one was open for 0% of the time, Pallas kernels for 13%

profile of v3, /device:TPU:0, one launch (start us, length us, event | category | flops | bytes accessed | tf_op | source)
XLA Modules:
  0.0 70.1 jit_solution(8995698239827284261)
XLA Ops:
  0.0 3.0 %collective-permute-start = (s32[1,1,8]{2,1,0:T(1,128)}, s32[1,1,8]{2,1,0:T(1,128)S(1)}, u32[]{:S(2)}, u32[]{:S(2)}) collective-permute-start(s32[1,1,8]{2,1,0:T(1,128)} %map_any.1), channel_id=1, source_target_pairs={{0,8},{8,0},{16,24},{24,16},{1,9},{9,1},{17,25},{25,17},{2,10},{10... | collective-permute-start | bytes 104 | tf_op jit(solution)/shard_map/ppermute | solution.py:22
  3.0 2.5 %collective-permute-start.2 = (s32[1,1,8]{2,1,0:T(1,128)}, s32[1,1,8]{2,1,0:T(1,128)S(1)}, u32[]{:S(2)}, u32[]{:S(2)}) collective-permute-start(s32[1,1,8]{2,1,0:T(1,128)} %map_any.1), channel_id=1, source_target_pairs={{0,24},{8,16},{16,8},{24,0},{1,25},{9,17},{17,9},{25,1},{2,26},{10... | collective-permute-start | bytes 104 | tf_op jit(solution)/shard_map/ppermute | solution.py:22
  5.6 5.8 %shard_map.46 = (f32[8,256,128]{2,1,0:T(8,128)S(1)}, f32[8,256,128]{2,1,0:T(8,128)S(1)}, f32[8,256,128]{2,1,0:T(8,128)S(1)}, f32[8,256,128]{2,1,0:T(8,128)S(1)}, s32[2,8]{1,0:T(2,128)S(1)}) custom-call(s32[1,1,8]{2,1,0:T(1,128)} %child_any.1, s32[1,1,8,8]{3,2,1,0:T(8,128)} %pattern_any.1, s32[1,1,8]{2,1,0:T(1,128)} %map_any.1, bf16[1024,2048]{1,0:T(8,128)(2,1)} %bitcast.34), custom_call_target="tpu_custom_call" | custom-call | flops 4294967296 | bytes 4194304 | tf_op jit(solution)/shard_map/pallas_call | solution.py:278
  11.4 0.9 %shard_map.47.refs_7_ = f32[8,200,128]{2,1,0:T(8,128)S(1)} custom-call(s32[2,8]{1,0:T(2,128)S(1)} %get-tuple-element.26.plan_ref, s32[1,1,8]{2,1,0:T(1,128)S(1)} %collective-permute-done.refs_0_, s32[1,1,8]{2,1,0:T(1,128)S(1)} %collective-permute-done.1.refs_1_, s32[1,1,8]{2,1,0:T(1,128)S(1)} %collective-permute-done.2.refs_2_, ...), custom_call_target="tpu_custom_call" | custom-call | tf_op jit(solution)/shard_map/pallas_call | solution.py:307
  12.5 1.1 %shard_map.48.in_ref = f32[8,736,128]{2,1,0:T(8,128)S(1)} custom-call(s32[2,8]{1,0:T(2,128)S(1)} %get-tuple-element.26.plan_ref, s32[1,1,8]{2,1,0:T(1,128)S(1)} %collective-permute-done.refs_0_, s32[1,1,8]{2,1,0:T(1,128)S(1)} %collective-permute-done.1.refs_1_, s32[1,1,8]{2,1,0:T(1,128)S(1)} %collective-permute-done.2.refs_2_, ...), custom_call_target="tpu_custom_call" | custom-call | tf_op jit(solution)/shard_map/pallas_call | solution.py:307
  13.6 0.6 collective-permute-done.3.crossed_ref
  14.6 1.6 %collective-permute-start.5 = (f32[2,200,128]{2,1,0:T(8,128)S(1)}, f32[2,200,128]{2,1,0:T(8,128)S(1)}, u32[]{:S(2)}, u32[]{:S(2)}) collective-permute-start(f32[2,200,128]{2,1,0:T(8,128)S(1)} %shard_map.49.refs_0_), channel_id=1, source_target_pairs={{0,2},{1,3},{2,0},{3,1},{4,6},{5,7},{6,4},{7,5},{8,10},{9,11},{10,... | collective-permute-start | bytes 614408 | tf_op jit(solution)/shard_map/ppermute | solution.py:22
  16.2 1.5 %collective-permute-start.11 = (f32[2,200,128]{2,1,0:T(8,128)S(1)}, f32[2,200,128]{2,1,0:T(8,128)S(1)}, u32[]{:S(2)}, u32[]{:S(2)}) collective-permute-start(f32[2,200,128]{2,1,0:T(8,128)S(1)} %shard_map.50.refs_1_), channel_id=1, source_target_pairs={{0,4},{1,5},{2,6},{3,7},{4,0},{5,1},{6,2},{7,3},{8,12},{9,13},{10,... | collective-permute-start | bytes 614408 | tf_op jit(solution)/shard_map/ppermute | solution.py:22
  18.3 4.3 %collective-permute-done.5.refs_0_.refs_2_ = f32[2,200,128]{2,1,0:T(8,128)S(1)} collective-permute-done((f32[2,200,128]{2,1,0:T(8,128)S(1)}, f32[2,200,128]{2,1,0:T(8,128)S(1)}, u32[]{:S(2)}, u32[]{:S(2)}) %collective-permute-start.5) | collective-permute-done | bytes 204832 | tf_op jit(solution)/shard_map/ppermute | solution.py:22
  22.6 1.6 %collective-permute-start.6 = (f32[2,200,128]{2,1,0:T(8,128)S(1)}, f32[2,200,128]{2,1,0:T(8,128)S(1)}, u32[]{:S(2)}, u32[]{:S(2)}) collective-permute-start(f32[2,200,128]{2,1,0:T(8,128)S(1)} %shard_map.53.refs_5_), channel_id=1, source_target_pairs={{0,2},{1,3},{2,0},{3,1},{4,6},{5,7},{6,4},{7,5},{8,10},{9,11},{10,... | collective-permute-start | bytes 614408 | tf_op jit(solution)/shard_map/ppermute | solution.py:22
  24.3 1.6 %collective-permute-start.10 = (f32[2,200,128]{2,1,0:T(8,128)S(1)}, f32[2,200,128]{2,1,0:T(8,128)S(1)}, u32[]{:S(2)}, u32[]{:S(2)}) collective-permute-start(f32[2,200,128]{2,1,0:T(8,128)S(1)} %shard_map.57.refs_6_), channel_id=1, source_target_pairs={{0,4},{1,5},{2,6},{3,7},{4,0},{5,1},{6,2},{7,3},{8,12},{9,13},{10,... | collective-permute-start | bytes 614408 | tf_op jit(solution)/shard_map/ppermute | solution.py:22
  25.9 1.7 %collective-permute-done.11.refs_0_.refs_3_ = f32[2,200,128]{2,1,0:T(8,128)S(1)} collective-permute-done((f32[2,200,128]{2,1,0:T(8,128)S(1)}, f32[2,200,128]{2,1,0:T(8,128)S(1)}, u32[]{:S(2)}, u32[]{:S(2)}) %collective-permute-start.11) | collective-permute-done | bytes 204832 | tf_op jit(solution)/shard_map/ppermute | solution.py:22
  27.6 1.6 %collective-permute-start.12 = (f32[2,200,128]{2,1,0:T(8,128)S(1)}, f32[2,200,128]{2,1,0:T(8,128)S(1)}, u32[]{:S(2)}, u32[]{:S(2)}) collective-permute-start(f32[2,200,128]{2,1,0:T(8,128)S(1)} %shard_map.58.refs_7_), channel_id=1, source_target_pairs={{0,6},{1,7},{2,4},{3,5},{4,2},{5,3},{6,0},{7,1},{8,14},{9,15},{10,... | collective-permute-start | bytes 614408 | tf_op jit(solution)/shard_map/ppermute | solution.py:22
  29.7 1.9 %collective-permute-start.14 = (f32[2,3,2,32,128]{4,3,2,1,0:T(8,128)S(1)}, f32[2,3,2,32,128]{4,3,2,1,0:T(8,128)S(1)}, u32[]{:S(2)}, u32[]{:S(2)}) collective-permute-start(f32[2,3,2,32,128]{4,3,2,1,0:T(8,128)S(1)} %pad_maximum_fusion), channel_id=1, source_target_pairs={{0,8},{8,0},{16,24},{24,16},{1,9},{9,1},{17,25},{25,17},{2,10},{10... | collective-permute-start | bytes 589832 | tf_op jit(solution)/shard_map/ppermute | solution.py:22
  31.6 2.4 %collective-permute-start.7 = (f32[2,200,128]{2,1,0:T(8,128)S(1)}, f32[2,200,128]{2,1,0:T(8,128)S(1)}, u32[]{:S(2)}, u32[]{:S(2)}) collective-permute-start(f32[2,200,128]{2,1,0:T(8,128)S(1)} %shard_map.54.refs_2_.refs_5_), channel_id=1, source_target_pairs={{0,2},{1,3},{2,0},{3,1},{4,6},{5,7},{6,4},{7,5},{8,10},{9,11},{10,... | collective-permute-start | bytes 614408 | tf_op jit(solution)/shard_map/ppermute | solution.py:22
  34.1 0.6 collective-permute-start.20
  34.7 0.7 %collective-permute-done.14.refs_1_ = f32[2,3,2,32,128]{4,3,2,1,0:T(8,128)S(1)} collective-permute-done((f32[2,3,2,32,128]{4,3,2,1,0:T(8,128)S(1)}, f32[2,3,2,32,128]{4,3,2,1,0:T(8,128)S(1)}, u32[]{:S(2)}, u32[]{:S(2)}) %collective-permute-start.14) | collective-permute-done | bytes 196640 | tf_op jit(solution)/shard_map/ppermute | solution.py:22
  35.4 2.9 %collective-permute-start.16 = (f32[1,3,2,32,128]{4,3,2,1,0:T(8,128)S(1)}, f32[1,3,2,32,128]{4,3,2,1,0:T(8,128)S(1)}, u32[]{:S(2)}, u32[]{:S(2)}) collective-permute-start(f32[1,3,2,32,128]{4,3,2,1,0:T(8,128)S(1)} %bitcast.20), channel_id=1, source_target_pairs={{0,16},{8,24},{16,0},{24,8},{1,17},{9,25},{17,1},{25,9},{2,18},{10... | collective-permute-start | bytes 294920 | tf_op jit(solution)/shard_map/ppermute | solution.py:22
  38.3 1.8 %collective-permute-start.21 = (f32[2,200,128]{2,1,0:T(8,128)S(1)}, f32[2,200,128]{2,1,0:T(8,128)S(1)}, u32[]{:S(2)}, u32[]{:S(2)}) collective-permute-start(f32[2,200,128]{2,1,0:T(8,128)S(1)} %shard_map.62.refs_7_), channel_id=1, source_target_pairs={{0,6},{1,7},{2,4},{3,5},{4,2},{5,3},{6,0},{7,1},{8,14},{9,15},{10,... | collective-permute-start | bytes 614408 | tf_op jit(solution)/shard_map/ppermute | solution.py:22
  41.0 1.1 %collective-permute-start.8 = (f32[2,200,128]{2,1,0:T(8,128)S(1)}, f32[2,200,128]{2,1,0:T(8,128)S(1)}, u32[]{:S(2)}, u32[]{:S(2)}) collective-permute-start(f32[2,200,128]{2,1,0:T(8,128)S(1)} %shard_map.55.refs_2_.refs_5_), channel_id=1, source_target_pairs={{0,2},{1,3},{2,0},{3,1},{4,6},{5,7},{6,4},{7,5},{8,10},{9,11},{10,... | collective-permute-start | bytes 614408 | tf_op jit(solution)/shard_map/ppermute | solution.py:22
  42.1 1.5 %collective-permute-start.19 = (f32[2,200,128]{2,1,0:T(8,128)S(1)}, f32[2,200,128]{2,1,0:T(8,128)S(1)}, u32[]{:S(2)}, u32[]{:S(2)}) collective-permute-start(f32[2,200,128]{2,1,0:T(8,128)S(1)} %shard_map.64.refs_3_.refs_6_), channel_id=1, source_target_pairs={{0,4},{1,5},{2,6},{3,7},{4,0},{5,1},{6,2},{7,3},{8,12},{9,13},{10,... | collective-permute-start | bytes 614408 | tf_op jit(solution)/shard_map/ppermute | solution.py:22
  43.6 3.5 %collective-permute-done.15.refs_1_ = f32[2,3,2,32,128]{4,3,2,1,0:T(8,128)S(1)} collective-permute-done((f32[2,3,2,32,128]{4,3,2,1,0:T(8,128)S(1)}, f32[2,3,2,32,128]{4,3,2,1,0:T(8,128)S(1)}, u32[]{:S(2)}, u32[]{:S(2)}) %collective-permute-start.15) | collective-permute-done | bytes 196640 | tf_op jit(solution)/shard_map/ppermute | solution.py:22
  47.3 1.4 %collective-permute-start.25 = (f32[2,200,128]{2,1,0:T(8,128)S(1)}, f32[2,200,128]{2,1,0:T(8,128)S(1)}, u32[]{:S(2)}, u32[]{:S(2)}) collective-permute-start(f32[2,200,128]{2,1,0:T(8,128)S(1)} %shard_map.67.refs_7_), channel_id=1, source_target_pairs={{0,6},{1,7},{2,4},{3,5},{4,2},{5,3},{6,0},{7,1},{8,14},{9,15},{10,... | collective-permute-start | bytes 614408 | tf_op jit(solution)/shard_map/ppermute | solution.py:22
  49.1 1.0 %collective-permute-start.22 = (f32[2,3,2,32,128]{4,3,2,1,0:T(8,128)S(1)}, f32[2,3,2,32,128]{4,3,2,1,0:T(8,128)S(1)}, u32[]{:S(2)}, u32[]{:S(2)}) collective-permute-start(f32[2,3,2,32,128]{4,3,2,1,0:T(8,128)S(1)} %pad_maximum_fusion.2), channel_id=1, source_target_pairs={{0,8},{8,0},{16,24},{24,16},{1,9},{9,1},{17,25},{25,17},{2,10},{10... | collective-permute-start | bytes 589832 | tf_op jit(solution)/shard_map/ppermute | solution.py:22
  50.1 2.4 %collective-permute-start.9 = (f32[2,136,128]{2,1,0:T(8,128)S(1)}, f32[2,136,128]{2,1,0:T(8,128)S(1)}, u32[]{:S(2)}, u32[]{:S(2)}) collective-permute-start(f32[2,136,128]{2,1,0:T(8,128)S(1)} %shard_map.56.refs_2_.refs_5_), channel_id=1, source_target_pairs={{0,2},{1,3},{2,0},{3,1},{4,6},{5,7},{6,4},{7,5},{8,10},{9,11},{10,... | collective-permute-start | bytes 417800 | tf_op jit(solution)/shard_map/ppermute | solution.py:22
  52.5 0.8 %collective-permute-done.17 = f32[1,3,2,32,128]{4,3,2,1,0:T(8,128)S(1)} collective-permute-done((f32[1,3,2,32,128]{4,3,2,1,0:T(8,128)S(1)}, f32[1,3,2,32,128]{4,3,2,1,0:T(8,128)S(1)}, u32[]{:S(2)}, u32[]{:S(2)}) %collective-permute-start.17) | collective-permute-done | bytes 98336 | tf_op jit(solution)/shard_map/ppermute | solution.py:22
  53.3 3.1 %collective-permute-start.18 = (f32[2,136,128]{2,1,0:T(8,128)S(1)}, f32[2,136,128]{2,1,0:T(8,128)S(1)}, u32[]{:S(2)}, u32[]{:S(2)}) collective-permute-start(f32[2,136,128]{2,1,0:T(8,128)S(1)} %shard_map.66.refs_3_.refs_6_), channel_id=1, source_target_pairs={{0,4},{1,5},{2,6},{3,7},{4,0},{5,1},{6,2},{7,3},{8,12},{9,13},{10,... | collective-permute-start | bytes 417800 | tf_op jit(solution)/shard_map/ppermute | solution.py:22
  56.8 3.9 %collective-permute-start.23 = (f32[2,136,128]{2,1,0:T(8,128)S(1)}, f32[2,136,128]{2,1,0:T(8,128)S(1)}, u32[]{:S(2)}, u32[]{:S(2)}) collective-permute-start(f32[2,136,128]{2,1,0:T(8,128)S(1)} %shard_map.70.refs_7_), channel_id=1, source_target_pairs={{0,6},{1,7},{2,4},{3,5},{4,2},{5,3},{6,0},{7,1},{8,14},{9,15},{10,... | collective-permute-start | bytes 417800 | tf_op jit(solution)/shard_map/ppermute | solution.py:22
  61.3 4.3 %collective-permute-start.28 = (f32[3,2,32,128]{3,2,1,0:T(8,128)S(1)}, f32[3,2,32,128]{3,2,1,0:T(8,128)S(1)}, u32[]{:S(2)}, u32[]{:S(2)}) collective-permute-start(f32[3,2,32,128]{3,2,1,0:T(8,128)S(1)} %get-tuple-element.46), channel_id=1, source_target_pairs={{0,24},{8,16},{16,8},{24,0},{1,25},{9,17},{17,9},{25,1},{2,26},{10... | collective-permute-start | bytes 294920 | tf_op jit(solution)/shard_map/ppermute | solution.py:22
  65.8 1.3 %collective-permute-done.26.refs_10_ = f32[3,2,32,128]{3,2,1,0:T(8,128)S(1)} collective-permute-done((f32[3,2,32,128]{3,2,1,0:T(8,128)S(1)}, f32[3,2,32,128]{3,2,1,0:T(8,128)S(1)}, u32[]{:S(2)}, u32[]{:S(2)}) %collective-permute-start.26) | collective-permute-done | bytes 98336 | tf_op jit(solution)/shard_map/ppermute | solution.py:22
  67.1 2.2 %collective-permute-done.28.refs_12_ = f32[3,2,32,128]{3,2,1,0:T(8,128)S(1)} collective-permute-done((f32[3,2,32,128]{3,2,1,0:T(8,128)S(1)}, f32[3,2,32,128]{3,2,1,0:T(8,128)S(1)}, u32[]{:S(2)}, u32[]{:S(2)}) %collective-permute-start.28) | collective-permute-done | bytes 98336 | tf_op jit(solution)/shard_map/ppermute | solution.py:22
  69.3 0.8 %shard_map.73 = f32[1,3,2,128,128]{4,3,2,1,0:T(8,128)} custom-call(f32[3,2,128,128]{3,2,1,0:T(8,128)S(1)} %shard_map.71.near_ref, f32[3,1,32,128]{3,2,1,0:T(8,128)S(1)} %get-tuple-element.40.refs_0_, f32[3,2,32,128]{3,2,1,0:T(8,128)S(1)} %slice_bitcast_fusion.2.refs_1_, f32[3,2,32,128]{3,2,1,0:T(8,128)S(1)} %bitcast.24, ...), custom_call_target="tpu_custom_call" | custom-call | tf_op jit(solution)/shard_map/pallas_call | solution.py:366
  (71 shorter events, 4.7 us)
Async XLA Ops:
  0.0 11.4 %collective-permute-start = (s32[1,1,8]{2,1,0:T(1,128)}, s32[1,1,8]{2,1,0:T(1,128)S(1)}, u32[]{:S(2)}, u32[]{:S(2)}) collective-permute-start(s32[1,1,8]{2,1,0:T(1,128)} %map_any.1), channel_id=1, source_target_pairs={{0,8},{8,0},{16,24},{24,16},{1,9},{9,1},{17,25},{25,17},{2,10},{10... | collective-permute-start | bytes 104 | tf_op jit(solution)/shard_map/ppermute | solution.py:22
  3.0 8.4 %collective-permute-start.2 = (s32[1,1,8]{2,1,0:T(1,128)}, s32[1,1,8]{2,1,0:T(1,128)S(1)}, u32[]{:S(2)}, u32[]{:S(2)}) collective-permute-start(s32[1,1,8]{2,1,0:T(1,128)} %map_any.1), channel_id=1, source_target_pairs={{0,24},{8,16},{16,8},{24,0},{1,25},{9,17},{17,9},{25,1},{2,26},{10... | collective-permute-start | bytes 104 | tf_op jit(solution)/shard_map/ppermute | solution.py:22
  5.5 5.9 %collective-permute-start.1 = (s32[1,1,8]{2,1,0:T(1,128)}, s32[1,1,8]{2,1,0:T(1,128)S(1)}, u32[]{:S(2)}, u32[]{:S(2)}) collective-permute-start(s32[1,1,8]{2,1,0:T(1,128)} %map_any.1), channel_id=1, source_target_pairs={{0,16},{8,24},{16,0},{24,8},{1,17},{9,25},{17,1},{25,9},{2,18},{10... | collective-permute-start | bytes 104 | tf_op jit(solution)/shard_map/ppermute | solution.py:22
  12.4 1.8 %collective-permute-start.3 = (f32[4,200,128]{2,1,0:T(8,128)S(1)}, f32[4,200,128]{2,1,0:T(8,128)S(1)}, u32[]{:S(2)}, u32[]{:S(2)}) collective-permute-start(f32[4,200,128]{2,1,0:T(8,128)S(1)} %get-tuple-element.59), channel_id=1, source_target_pairs={{0,1},{1,0},{2,3},{3,2},{4,5},{5,4},{6,7},{7,6},{8,9},{9,8},{10,11... | collective-permute-start | bytes 1228808 | tf_op jit(solution)/shard_map/ppermute | solution.py:22
  14.4 3.9 %collective-permute-start.4 = (f32[4,736,128]{2,1,0:T(8,128)S(1)}, f32[4,736,128]{2,1,0:T(8,128)S(1)}, u32[]{:S(2)}, u32[]{:S(2)}) collective-permute-start(f32[4,736,128]{2,1,0:T(8,128)S(1)} %shard_map.52), channel_id=1, source_target_pairs={{0,1},{1,0},{2,3},{3,2},{4,5},{5,4},{6,7},{7,6},{8,9},{9,8},{10,11... | collective-permute-start | bytes 4521992 | tf_op jit(solution)/shard_map/ppermute | solution.py:22
  14.6 8.0 %collective-permute-start.5 = (f32[2,200,128]{2,1,0:T(8,128)S(1)}, f32[2,200,128]{2,1,0:T(8,128)S(1)}, u32[]{:S(2)}, u32[]{:S(2)}) collective-permute-start(f32[2,200,128]{2,1,0:T(8,128)S(1)} %shard_map.49.refs_0_), channel_id=1, source_target_pairs={{0,2},{1,3},{2,0},{3,1},{4,6},{5,7},{6,4},{7,5},{8,10},{9,11},{10,... | collective-permute-start | bytes 614408 | tf_op jit(solution)/shard_map/ppermute | solution.py:22
  16.2 11.4 %collective-permute-start.11 = (f32[2,200,128]{2,1,0:T(8,128)S(1)}, f32[2,200,128]{2,1,0:T(8,128)S(1)}, u32[]{:S(2)}, u32[]{:S(2)}) collective-permute-start(f32[2,200,128]{2,1,0:T(8,128)S(1)} %shard_map.50.refs_1_), channel_id=1, source_target_pairs={{0,4},{1,5},{2,6},{3,7},{4,0},{5,1},{6,2},{7,3},{8,12},{9,13},{10,... | collective-permute-start | bytes 614408 | tf_op jit(solution)/shard_map/ppermute | solution.py:22
  17.7 11.5 %collective-permute-start.13 = (f32[2,200,128]{2,1,0:T(8,128)S(1)}, f32[2,200,128]{2,1,0:T(8,128)S(1)}, u32[]{:S(2)}, u32[]{:S(2)}) collective-permute-start(f32[2,200,128]{2,1,0:T(8,128)S(1)} %shard_map.51.refs_2_), channel_id=1, source_target_pairs={{0,6},{1,7},{2,4},{3,5},{4,2},{5,3},{6,0},{7,1},{8,14},{9,15},{10,... | collective-permute-start | bytes 614408 | tf_op jit(solution)/shard_map/ppermute | solution.py:22
  22.6 8.9 %collective-permute-start.6 = (f32[2,200,128]{2,1,0:T(8,128)S(1)}, f32[2,200,128]{2,1,0:T(8,128)S(1)}, u32[]{:S(2)}, u32[]{:S(2)}) collective-permute-start(f32[2,200,128]{2,1,0:T(8,128)S(1)} %shard_map.53.refs_5_), channel_id=1, source_target_pairs={{0,2},{1,3},{2,0},{3,1},{4,6},{5,7},{6,4},{7,5},{8,10},{9,11},{10,... | collective-permute-start | bytes 614408 | tf_op jit(solution)/shard_map/ppermute | solution.py:22
  24.3 14.0 %collective-permute-start.10 = (f32[2,200,128]{2,1,0:T(8,128)S(1)}, f32[2,200,128]{2,1,0:T(8,128)S(1)}, u32[]{:S(2)}, u32[]{:S(2)}) collective-permute-start(f32[2,200,128]{2,1,0:T(8,128)S(1)} %shard_map.57.refs_6_), channel_id=1, source_target_pairs={{0,4},{1,5},{2,6},{3,7},{4,0},{5,1},{6,2},{7,3},{8,12},{9,13},{10,... | collective-permute-start | bytes 614408 | tf_op jit(solution)/shard_map/ppermute | solution.py:22
  27.6 12.5 %collective-permute-start.12 = (f32[2,200,128]{2,1,0:T(8,128)S(1)}, f32[2,200,128]{2,1,0:T(8,128)S(1)}, u32[]{:S(2)}, u32[]{:S(2)}) collective-permute-start(f32[2,200,128]{2,1,0:T(8,128)S(1)} %shard_map.58.refs_7_), channel_id=1, source_target_pairs={{0,6},{1,7},{2,4},{3,5},{4,2},{5,3},{6,0},{7,1},{8,14},{9,15},{10,... | collective-permute-start | bytes 614408 | tf_op jit(solution)/shard_map/ppermute | solution.py:22
  29.7 5.7 %collective-permute-start.14 = (f32[2,3,2,32,128]{4,3,2,1,0:T(8,128)S(1)}, f32[2,3,2,32,128]{4,3,2,1,0:T(8,128)S(1)}, u32[]{:S(2)}, u32[]{:S(2)}) collective-permute-start(f32[2,3,2,32,128]{4,3,2,1,0:T(8,128)S(1)} %pad_maximum_fusion), channel_id=1, source_target_pairs={{0,8},{8,0},{16,24},{24,16},{1,9},{9,1},{17,25},{25,17},{2,10},{10... | collective-permute-start | bytes 589832 | tf_op jit(solution)/shard_map/ppermute | solution.py:22
  31.6 9.4 %collective-permute-start.7 = (f32[2,200,128]{2,1,0:T(8,128)S(1)}, f32[2,200,128]{2,1,0:T(8,128)S(1)}, u32[]{:S(2)}, u32[]{:S(2)}) collective-permute-start(f32[2,200,128]{2,1,0:T(8,128)S(1)} %shard_map.54.refs_2_.refs_5_), channel_id=1, source_target_pairs={{0,2},{1,3},{2,0},{3,1},{4,6},{5,7},{6,4},{7,5},{8,10},{9,11},{10,... | collective-permute-start | bytes 614408 | tf_op jit(solution)/shard_map/ppermute | solution.py:22
  34.1 13.2 %collective-permute-start.20 = (f32[2,200,128]{2,1,0:T(8,128)S(1)}, f32[2,200,128]{2,1,0:T(8,128)S(1)}, u32[]{:S(2)}, u32[]{:S(2)}) collective-permute-start(f32[2,200,128]{2,1,0:T(8,128)S(1)} %shard_map.59.refs_3_.refs_6_), channel_id=1, source_target_pairs={{0,4},{1,5},{2,6},{3,7},{4,0},{5,1},{6,2},{7,3},{8,12},{9,13},{10,... | collective-permute-start | bytes 614408 | tf_op jit(solution)/shard_map/ppermute | solution.py:22
  35.4 6.7 %collective-permute-start.16 = (f32[1,3,2,32,128]{4,3,2,1,0:T(8,128)S(1)}, f32[1,3,2,32,128]{4,3,2,1,0:T(8,128)S(1)}, u32[]{:S(2)}, u32[]{:S(2)}) collective-permute-start(f32[1,3,2,32,128]{4,3,2,1,0:T(8,128)S(1)} %bitcast.20), channel_id=1, source_target_pairs={{0,16},{8,24},{16,0},{24,8},{1,17},{9,25},{17,1},{25,9},{2,18},{10... | collective-permute-start | bytes 294920 | tf_op jit(solution)/shard_map/ppermute | solution.py:22
  38.3 10.3 %collective-permute-start.21 = (f32[2,200,128]{2,1,0:T(8,128)S(1)}, f32[2,200,128]{2,1,0:T(8,128)S(1)}, u32[]{:S(2)}, u32[]{:S(2)}) collective-permute-start(f32[2,200,128]{2,1,0:T(8,128)S(1)} %shard_map.62.refs_7_), channel_id=1, source_target_pairs={{0,6},{1,7},{2,4},{3,5},{4,2},{5,3},{6,0},{7,1},{8,14},{9,15},{10,... | collective-permute-start | bytes 614408 | tf_op jit(solution)/shard_map/ppermute | solution.py:22
  40.5 6.6 %collective-permute-start.15 = (f32[2,3,2,32,128]{4,3,2,1,0:T(8,128)S(1)}, f32[2,3,2,32,128]{4,3,2,1,0:T(8,128)S(1)}, u32[]{:S(2)}, u32[]{:S(2)}) collective-permute-start(f32[2,3,2,32,128]{4,3,2,1,0:T(8,128)S(1)} %pad_maximum_fusion.1), channel_id=1, source_target_pairs={{0,8},{8,0},{16,24},{24,16},{1,9},{9,1},{17,25},{25,17},{2,10},{10... | collective-permute-start | bytes 589832 | tf_op jit(solution)/shard_map/ppermute | solution.py:22
  41.0 9.1 %collective-permute-start.8 = (f32[2,200,128]{2,1,0:T(8,128)S(1)}, f32[2,200,128]{2,1,0:T(8,128)S(1)}, u32[]{:S(2)}, u32[]{:S(2)}) collective-permute-start(f32[2,200,128]{2,1,0:T(8,128)S(1)} %shard_map.55.refs_2_.refs_5_), channel_id=1, source_target_pairs={{0,2},{1,3},{2,0},{3,1},{4,6},{5,7},{6,4},{7,5},{8,10},{9,11},{10,... | collective-permute-start | bytes 614408 | tf_op jit(solution)/shard_map/ppermute | solution.py:22
  42.1 14.7 %collective-permute-start.19 = (f32[2,200,128]{2,1,0:T(8,128)S(1)}, f32[2,200,128]{2,1,0:T(8,128)S(1)}, u32[]{:S(2)}, u32[]{:S(2)}) collective-permute-start(f32[2,200,128]{2,1,0:T(8,128)S(1)} %shard_map.64.refs_3_.refs_6_), channel_id=1, source_target_pairs={{0,4},{1,5},{2,6},{3,7},{4,0},{5,1},{6,2},{7,3},{8,12},{9,13},{10,... | collective-permute-start | bytes 614408 | tf_op jit(solution)/shard_map/ppermute | solution.py:22
  47.2 6.1 %collective-permute-start.17 = (f32[1,3,2,32,128]{4,3,2,1,0:T(8,128)S(1)}, f32[1,3,2,32,128]{4,3,2,1,0:T(8,128)S(1)}, u32[]{:S(2)}, u32[]{:S(2)}) collective-permute-start(f32[1,3,2,32,128]{4,3,2,1,0:T(8,128)S(1)} %bitcast.21), channel_id=1, source_target_pairs={{0,16},{8,24},{16,0},{24,8},{1,17},{9,25},{17,1},{25,9},{2,18},{10... | collective-permute-start | bytes 294920 | tf_op jit(solution)/shard_map/ppermute | solution.py:22
  47.3 13.4 %collective-permute-start.25 = (f32[2,200,128]{2,1,0:T(8,128)S(1)}, f32[2,200,128]{2,1,0:T(8,128)S(1)}, u32[]{:S(2)}, u32[]{:S(2)}) collective-permute-start(f32[2,200,128]{2,1,0:T(8,128)S(1)} %shard_map.67.refs_7_), channel_id=1, source_target_pairs={{0,6},{1,7},{2,4},{3,5},{4,2},{5,3},{6,0},{7,1},{8,14},{9,15},{10,... | collective-permute-start | bytes 614408 | tf_op jit(solution)/shard_map/ppermute | solution.py:22
  49.1 7.3 %collective-permute-start.22 = (f32[2,3,2,32,128]{4,3,2,1,0:T(8,128)S(1)}, f32[2,3,2,32,128]{4,3,2,1,0:T(8,128)S(1)}, u32[]{:S(2)}, u32[]{:S(2)}) collective-permute-start(f32[2,3,2,32,128]{4,3,2,1,0:T(8,128)S(1)} %pad_maximum_fusion.2), channel_id=1, source_target_pairs={{0,8},{8,0},{16,24},{24,16},{1,9},{9,1},{17,25},{25,17},{2,10},{10... | collective-permute-start | bytes 589832 | tf_op jit(solution)/shard_map/ppermute | solution.py:22
  50.1 11.1 %collective-permute-start.9 = (f32[2,136,128]{2,1,0:T(8,128)S(1)}, f32[2,136,128]{2,1,0:T(8,128)S(1)}, u32[]{:S(2)}, u32[]{:S(2)}) collective-permute-start(f32[2,136,128]{2,1,0:T(8,128)S(1)} %shard_map.56.refs_2_.refs_5_), channel_id=1, source_target_pairs={{0,2},{1,3},{2,0},{3,1},{4,6},{5,7},{6,4},{7,5},{8,10},{9,11},{10,... | collective-permute-start | bytes 417800 | tf_op jit(solution)/shard_map/ppermute | solution.py:22
  53.3 8.0 %collective-permute-start.18 = (f32[2,136,128]{2,1,0:T(8,128)S(1)}, f32[2,136,128]{2,1,0:T(8,128)S(1)}, u32[]{:S(2)}, u32[]{:S(2)}) collective-permute-start(f32[2,136,128]{2,1,0:T(8,128)S(1)} %shard_map.66.refs_3_.refs_6_), channel_id=1, source_target_pairs={{0,4},{1,5},{2,6},{3,7},{4,0},{5,1},{6,2},{7,3},{8,12},{9,13},{10,... | collective-permute-start | bytes 417800 | tf_op jit(solution)/shard_map/ppermute | solution.py:22
  56.4 9.4 %collective-permute-start.24 = (f32[1,3,2,32,128]{4,3,2,1,0:T(8,128)S(1)}, f32[1,3,2,32,128]{4,3,2,1,0:T(8,128)S(1)}, u32[]{:S(2)}, u32[]{:S(2)}) collective-permute-start(f32[1,3,2,32,128]{4,3,2,1,0:T(8,128)S(1)} %bitcast.22), channel_id=1, source_target_pairs={{0,16},{8,24},{16,0},{24,8},{1,17},{9,25},{17,1},{25,9},{2,18},{10... | collective-permute-start | bytes 294920 | tf_op jit(solution)/shard_map/ppermute | solution.py:22
  56.8 8.7 %collective-permute-start.23 = (f32[2,136,128]{2,1,0:T(8,128)S(1)}, f32[2,136,128]{2,1,0:T(8,128)S(1)}, u32[]{:S(2)}, u32[]{:S(2)}) collective-permute-start(f32[2,136,128]{2,1,0:T(8,128)S(1)} %shard_map.70.refs_7_), channel_id=1, source_target_pairs={{0,6},{1,7},{2,4},{3,5},{4,2},{5,3},{6,0},{7,1},{8,14},{9,15},{10,... | collective-permute-start | bytes 417800 | tf_op jit(solution)/shard_map/ppermute | solution.py:22
  61.1 6.1 %collective-permute-start.26 = (f32[3,2,32,128]{3,2,1,0:T(8,128)S(1)}, f32[3,2,32,128]{3,2,1,0:T(8,128)S(1)}, u32[]{:S(2)}, u32[]{:S(2)}) collective-permute-start(f32[3,2,32,128]{3,2,1,0:T(8,128)S(1)} %get-tuple-element.44), channel_id=1, source_target_pairs={{0,8},{8,0},{16,24},{24,16},{1,9},{9,1},{17,25},{25,17},{2,10},{10... | collective-permute-start | bytes 294920 | tf_op jit(solution)/shard_map/ppermute | solution.py:22
  61.2 6.0 %collective-permute-start.27 = (f32[3,2,32,128]{3,2,1,0:T(8,128)S(1)}, f32[3,2,32,128]{3,2,1,0:T(8,128)S(1)}, u32[]{:S(2)}, u32[]{:S(2)}) collective-permute-start(f32[3,2,32,128]{3,2,1,0:T(8,128)S(1)} %get-tuple-element.45), channel_id=1, source_target_pairs={{0,16},{8,24},{16,0},{24,8},{1,17},{9,25},{17,1},{25,9},{2,18},{10... | collective-permute-start | bytes 294920 | tf_op jit(solution)/shard_map/ppermute | solution.py:22
  61.3 8.0 %collective-permute-start.28 = (f32[3,2,32,128]{3,2,1,0:T(8,128)S(1)}, f32[3,2,32,128]{3,2,1,0:T(8,128)S(1)}, u32[]{:S(2)}, u32[]{:S(2)}) collective-permute-start(f32[3,2,32,128]{3,2,1,0:T(8,128)S(1)} %get-tuple-element.46), channel_id=1, source_target_pairs={{0,24},{8,16},{16,8},{24,0},{1,25},{9,17},{17,9},{25,1},{2,26},{10... | collective-permute-start | bytes 294920 | tf_op jit(solution)/shard_map/ppermute | solution.py:22

commit v4 on v3

--- a/solution.py
+++ b/solution.py
@@ -10,7 +10,7 @@
 ANC_DEV = 3
 META = 8
 CUT = 8
-CHUNK_PARTS = (4, 4, 4, 4)
+CHUNK_PARTS = (3, 4, 4, 5)
 DEPS = ((1,), (1,), (2,))
 ZDEP = 2
 DIRECT = 1

time: 70.4 us -> 69.7 us (0.990)
  starting transfers between devices: 43.4 us -> 41.7 us
  waiting for transfers between devices: 15.2 us -> 16 us
    ppermute x29, starting transfers between devices: 43.4 us -> 41.7 us  [swapped(): lax.ppermute(shard, axis, [(i, i ^ apart) for i in range(lax.axis_size(ax...]
    ppermute x29, waiting for transfers between devices: 15.2 us -> 16 us  [swapped(): lax.ppermute(shard, axis, [(i, i ^ apart) for i in range(lax.axis_size(ax...]
  transfers between devices with their start and end apart: 29 -> 29, of which waited for: 9 -> 9; matrix products, arithmetic and copies ran while one was open for 0% -> 1% of each run, Pallas kernels for 13% -> 13%
where the time goes in v4:
time: 69.7 us; the launch traced here: 69.3 us
  starting transfers between devices  41.7 us (60%)
  waiting for transfers between devices  16 us (23%)
  Pallas kernels  10.9 us (16%)
    ppermute x29, starting transfers between devices, swapped(): lax.ppermute(shard, axis, [(i, i ^ apart) for i in range(lax.axis_size(ax...  41.7 us
    ppermute x29, waiting for transfers between devices, swapped(): lax.ppermute(shard, axis, [(i, i ^ apart) for i in range(lax.axis_size(ax...  16 us
    pallas_call x1, Pallas kernels, per_device_blocks(): pl.pallas_call(functools.partial(multiply_kernel, nb, per_piece, spans),...  5.76 us
    pallas_call x2, Pallas kernels, per_device_blocks(): pl.pallas_call(functools.partial(route_kernel, nb, per_piece, subs, group...  2.03 us
    pallas_call x5, Pallas kernels, gather(): pl.pallas_call(functools.partial(gather_kernel, nb, per_piece, kept, coun...  1.89 us
  transfers between devices with their start and end apart: 29, of which 9 were waited for; matrix products, arithmetic and copies ran while one was open for 1% of the time, Pallas kernels for 13%

profile of v4, /device:TPU:0, one launch (start us, length us, event | category | flops | bytes accessed | tf_op | source)
XLA Modules:
  0.0 69.3 jit_solution(2722416760580245894)
XLA Ops:
  0.0 3.0 %collective-permute-start = (s32[1,1,8]{2,1,0:T(1,128)}, s32[1,1,8]{2,1,0:T(1,128)S(1)}, u32[]{:S(2)}, u32[]{:S(2)}) collective-permute-start(s32[1,1,8]{2,1,0:T(1,128)} %map_any.1), channel_id=1, source_target_pairs={{0,8},{8,0},{16,24},{24,16},{1,9},{9,1},{17,25},{25,17},{2,10},{10... | collective-permute-start | bytes 104 | tf_op jit(solution)/shard_map/ppermute | solution.py:22
  3.0 2.5 %collective-permute-start.2 = (s32[1,1,8]{2,1,0:T(1,128)}, s32[1,1,8]{2,1,0:T(1,128)S(1)}, u32[]{:S(2)}, u32[]{:S(2)}) collective-permute-start(s32[1,1,8]{2,1,0:T(1,128)} %map_any.1), channel_id=1, source_target_pairs={{0,24},{8,16},{16,8},{24,0},{1,25},{9,17},{17,9},{25,1},{2,26},{10... | collective-permute-start | bytes 104 | tf_op jit(solution)/shard_map/ppermute | solution.py:22
  5.6 5.8 %shard_map.46 = (f32[8,192,128]{2,1,0:T(8,128)S(1)}, f32[8,256,128]{2,1,0:T(8,128)S(1)}, f32[8,256,128]{2,1,0:T(8,128)S(1)}, f32[8,320,128]{2,1,0:T(8,128)S(1)}, s32[2,8]{1,0:T(2,128)S(1)}) custom-call(s32[1,1,8]{2,1,0:T(1,128)} %child_any.1, s32[1,1,8,8]{3,2,1,0:T(8,128)} %pattern_any.1, s32[1,1,8]{2,1,0:T(1,128)} %map_any.1, bf16[1024,2048]{1,0:T(8,128)(2,1)} %bitcast.34), custom_call_target="tpu_custom_call" | custom-call | flops 4294967296 | bytes 4194304 | tf_op jit(solution)/shard_map/pallas_call | solution.py:278
  11.4 0.9 %shard_map.47.refs_7_ = f32[8,152,128]{2,1,0:T(8,128)S(1)} custom-call(s32[2,8]{1,0:T(2,128)S(1)} %get-tuple-element.26.plan_ref, s32[1,1,8]{2,1,0:T(1,128)S(1)} %collective-permute-done.refs_0_, s32[1,1,8]{2,1,0:T(1,128)S(1)} %collective-permute-done.1.refs_1_, s32[1,1,8]{2,1,0:T(1,128)S(1)} %collective-permute-done.2.refs_2_, ...), custom_call_target="tpu_custom_call" | custom-call | tf_op jit(solution)/shard_map/pallas_call | solution.py:307
  12.4 1.1 %shard_map.48.in_ref = f32[8,784,128]{2,1,0:T(8,128)S(1)} custom-call(s32[2,8]{1,0:T(2,128)S(1)} %get-tuple-element.26.plan_ref, s32[1,1,8]{2,1,0:T(1,128)S(1)} %collective-permute-done.refs_0_, s32[1,1,8]{2,1,0:T(1,128)S(1)} %collective-permute-done.1.refs_1_, s32[1,1,8]{2,1,0:T(1,128)S(1)} %collective-permute-done.2.refs_2_, ...), custom_call_target="tpu_custom_call" | custom-call | tf_op jit(solution)/shard_map/pallas_call | solution.py:307
  14.5 1.6 %collective-permute-start.5 = (f32[2,152,128]{2,1,0:T(8,128)S(1)}, f32[2,152,128]{2,1,0:T(8,128)S(1)}, u32[]{:S(2)}, u32[]{:S(2)}) collective-permute-start(f32[2,152,128]{2,1,0:T(8,128)S(1)} %shard_map.49.refs_0_), channel_id=1, source_target_pairs={{0,2},{1,3},{2,0},{3,1},{4,6},{5,7},{6,4},{7,5},{8,10},{9,11},{10,... | collective-permute-start | bytes 466952 | tf_op jit(solution)/shard_map/ppermute | solution.py:22
  16.0 1.5 %collective-permute-start.11 = (f32[2,152,128]{2,1,0:T(8,128)S(1)}, f32[2,152,128]{2,1,0:T(8,128)S(1)}, u32[]{:S(2)}, u32[]{:S(2)}) collective-permute-start(f32[2,152,128]{2,1,0:T(8,128)S(1)} %shard_map.50.refs_1_), channel_id=1, source_target_pairs={{0,4},{1,5},{2,6},{3,7},{4,0},{5,1},{6,2},{7,3},{8,12},{9,13},{10,... | collective-permute-start | bytes 466952 | tf_op jit(solution)/shard_map/ppermute | solution.py:22
  18.1 3.3 %collective-permute-done.5.refs_0_.refs_2_ = f32[2,152,128]{2,1,0:T(8,128)S(1)} collective-permute-done((f32[2,152,128]{2,1,0:T(8,128)S(1)}, f32[2,152,128]{2,1,0:T(8,128)S(1)}, u32[]{:S(2)}, u32[]{:S(2)}) %collective-permute-start.5) | collective-permute-done | bytes 155680 | tf_op jit(solution)/shard_map/ppermute | solution.py:22
  21.4 1.6 %collective-permute-start.6 = (f32[2,200,128]{2,1,0:T(8,128)S(1)}, f32[2,200,128]{2,1,0:T(8,128)S(1)}, u32[]{:S(2)}, u32[]{:S(2)}) collective-permute-start(f32[2,200,128]{2,1,0:T(8,128)S(1)} %shard_map.53.refs_5_), channel_id=1, source_target_pairs={{0,2},{1,3},{2,0},{3,1},{4,6},{5,7},{6,4},{7,5},{8,10},{9,11},{10,... | collective-permute-start | bytes 614408 | tf_op jit(solution)/shard_map/ppermute | solution.py:22
  23.1 1.6 %collective-permute-start.10 = (f32[2,200,128]{2,1,0:T(8,128)S(1)}, f32[2,200,128]{2,1,0:T(8,128)S(1)}, u32[]{:S(2)}, u32[]{:S(2)}) collective-permute-start(f32[2,200,128]{2,1,0:T(8,128)S(1)} %shard_map.57.refs_6_), channel_id=1, source_target_pairs={{0,4},{1,5},{2,6},{3,7},{4,0},{5,1},{6,2},{7,3},{8,12},{9,13},{10,... | collective-permute-start | bytes 614408 | tf_op jit(solution)/shard_map/ppermute | solution.py:22
  25.2 1.7 %collective-permute-start.12 = (f32[2,200,128]{2,1,0:T(8,128)S(1)}, f32[2,200,128]{2,1,0:T(8,128)S(1)}, u32[]{:S(2)}, u32[]{:S(2)}) collective-permute-start(f32[2,200,128]{2,1,0:T(8,128)S(1)} %shard_map.58.refs_7_), channel_id=1, source_target_pairs={{0,6},{1,7},{2,4},{3,5},{4,2},{5,3},{6,0},{7,1},{8,14},{9,15},{10,... | collective-permute-start | bytes 614408 | tf_op jit(solution)/shard_map/ppermute | solution.py:22
  27.3 1.9 %collective-permute-start.14 = (f32[2,3,2,24,128]{4,3,2,1,0:T(8,128)S(1)}, f32[2,3,2,24,128]{4,3,2,1,0:T(8,128)S(1)}, u32[]{:S(2)}, u32[]{:S(2)}) collective-permute-start(f32[2,3,2,24,128]{4,3,2,1,0:T(8,128)S(1)} %pad_maximum_fusion.2), channel_id=1, source_target_pairs={{0,8},{8,0},{16,24},{24,16},{1,9},{9,1},{17,25},{25,17},{2,10},{10... | collective-permute-start | bytes 442376 | tf_op jit(solution)/shard_map/ppermute | solution.py:22
  29.2 2.2 %collective-permute-start.7 = (f32[2,200,128]{2,1,0:T(8,128)S(1)}, f32[2,200,128]{2,1,0:T(8,128)S(1)}, u32[]{:S(2)}, u32[]{:S(2)}) collective-permute-start(f32[2,200,128]{2,1,0:T(8,128)S(1)} %shard_map.54.refs_2_.refs_5_), channel_id=1, source_target_pairs={{0,2},{1,3},{2,0},{3,1},{4,6},{5,7},{6,4},{7,5},{8,10},{9,11},{10,... | collective-permute-start | bytes 614408 | tf_op jit(solution)/shard_map/ppermute | solution.py:22
  31.6 1.2 %collective-permute-start.20 = (f32[2,200,128]{2,1,0:T(8,128)S(1)}, f32[2,200,128]{2,1,0:T(8,128)S(1)}, u32[]{:S(2)}, u32[]{:S(2)}) collective-permute-start(f32[2,200,128]{2,1,0:T(8,128)S(1)} %shard_map.59.refs_3_.refs_6_), channel_id=1, source_target_pairs={{0,4},{1,5},{2,6},{3,7},{4,0},{5,1},{6,2},{7,3},{8,12},{9,13},{10,... | collective-permute-start | bytes 614408 | tf_op jit(solution)/shard_map/ppermute | solution.py:22
  32.8 2.9 %collective-permute-start.16 = (f32[1,3,2,24,128]{4,3,2,1,0:T(8,128)S(1)}, f32[1,3,2,24,128]{4,3,2,1,0:T(8,128)S(1)}, u32[]{:S(2)}, u32[]{:S(2)}) collective-permute-start(f32[1,3,2,24,128]{4,3,2,1,0:T(8,128)S(1)} %bitcast.22), channel_id=1, source_target_pairs={{0,16},{8,24},{16,0},{24,8},{1,17},{9,25},{17,1},{25,9},{2,18},{10... | collective-permute-start | bytes 221192 | tf_op jit(solution)/shard_map/ppermute | solution.py:22
  35.7 1.2 %collective-permute-start.21 = (f32[2,200,128]{2,1,0:T(8,128)S(1)}, f32[2,200,128]{2,1,0:T(8,128)S(1)}, u32[]{:S(2)}, u32[]{:S(2)}) collective-permute-start(f32[2,200,128]{2,1,0:T(8,128)S(1)} %shard_map.62.refs_7_), channel_id=1, source_target_pairs={{0,6},{1,7},{2,4},{3,5},{4,2},{5,3},{6,0},{7,1},{8,14},{9,15},{10,... | collective-permute-start | bytes 614408 | tf_op jit(solution)/shard_map/ppermute | solution.py:22
  37.9 1.0 %collective-permute-done.7.refs_0_.refs_2_ = f32[2,200,128]{2,1,0:T(8,128)S(1)} collective-permute-done((f32[2,200,128]{2,1,0:T(8,128)S(1)}, f32[2,200,128]{2,1,0:T(8,128)S(1)}, u32[]{:S(2)}, u32[]{:S(2)}) %collective-permute-start.7) | collective-permute-done | bytes 204832 | tf_op jit(solution)/shard_map/ppermute | solution.py:22
  39.0 1.0 %collective-permute-start.8 = (f32[2,248,128]{2,1,0:T(8,128)S(1)}, f32[2,248,128]{2,1,0:T(8,128)S(1)}, u32[]{:S(2)}, u32[]{:S(2)}) collective-permute-start(f32[2,248,128]{2,1,0:T(8,128)S(1)} %shard_map.55.refs_2_.refs_5_), channel_id=1, source_target_pairs={{0,2},{1,3},{2,0},{3,1},{4,6},{5,7},{6,4},{7,5},{8,10},{9,11},{10,... | collective-permute-start | bytes 761864 | tf_op jit(solution)/shard_map/ppermute | solution.py:22
  40.0 1.5 %collective-permute-start.19 = (f32[2,248,128]{2,1,0:T(8,128)S(1)}, f32[2,248,128]{2,1,0:T(8,128)S(1)}, u32[]{:S(2)}, u32[]{:S(2)}) collective-permute-start(f32[2,248,128]{2,1,0:T(8,128)S(1)} %shard_map.64.refs_3_.refs_6_), channel_id=1, source_target_pairs={{0,4},{1,5},{2,6},{3,7},{4,0},{5,1},{6,2},{7,3},{8,12},{9,13},{10,... | collective-permute-start | bytes 761864 | tf_op jit(solution)/shard_map/ppermute | solution.py:22
  41.5 1.6 %collective-permute-done.15.refs_1_ = f32[2,3,2,32,128]{4,3,2,1,0:T(8,128)S(1)} collective-permute-done((f32[2,3,2,32,128]{4,3,2,1,0:T(8,128)S(1)}, f32[2,3,2,32,128]{4,3,2,1,0:T(8,128)S(1)}, u32[]{:S(2)}, u32[]{:S(2)}) %collective-permute-start.15) | collective-permute-done | bytes 196640 | tf_op jit(solution)/shard_map/ppermute | solution.py:22
  43.1 1.3 %collective-permute-start.17 = (f32[1,3,2,32,128]{4,3,2,1,0:T(8,128)S(1)}, f32[1,3,2,32,128]{4,3,2,1,0:T(8,128)S(1)}, u32[]{:S(2)}, u32[]{:S(2)}) collective-permute-start(f32[1,3,2,32,128]{4,3,2,1,0:T(8,128)S(1)} %bitcast.20), channel_id=1, source_target_pairs={{0,16},{8,24},{16,0},{24,8},{1,17},{9,25},{17,1},{25,9},{2,18},{10... | collective-permute-start | bytes 294920 | tf_op jit(solution)/shard_map/ppermute | solution.py:22
  44.4 1.8 %collective-permute-start.25 = (f32[2,248,128]{2,1,0:T(8,128)S(1)}, f32[2,248,128]{2,1,0:T(8,128)S(1)}, u32[]{:S(2)}, u32[]{:S(2)}) collective-permute-start(f32[2,248,128]{2,1,0:T(8,128)S(1)} %shard_map.67.refs_7_), channel_id=1, source_target_pairs={{0,6},{1,7},{2,4},{3,5},{4,2},{5,3},{6,0},{7,1},{8,14},{9,15},{10,... | collective-permute-start | bytes 761864 | tf_op jit(solution)/shard_map/ppermute | solution.py:22
  47.4 1.9 %collective-permute-done.8.refs_0_.refs_2_ = f32[2,248,128]{2,1,0:T(8,128)S(1)} collective-permute-done((f32[2,248,128]{2,1,0:T(8,128)S(1)}, f32[2,248,128]{2,1,0:T(8,128)S(1)}, u32[]{:S(2)}, u32[]{:S(2)}) %collective-permute-start.8) | collective-permute-done | bytes 253984 | tf_op jit(solution)/shard_map/ppermute | solution.py:22
  49.3 1.1 %collective-permute-start.9 = (f32[2,136,128]{2,1,0:T(8,128)S(1)}, f32[2,136,128]{2,1,0:T(8,128)S(1)}, u32[]{:S(2)}, u32[]{:S(2)}) collective-permute-start(f32[2,136,128]{2,1,0:T(8,128)S(1)} %shard_map.56.refs_2_.refs_5_), channel_id=1, source_target_pairs={{0,2},{1,3},{2,0},{3,1},{4,6},{5,7},{6,4},{7,5},{8,10},{9,11},{10,... | collective-permute-start | bytes 417800 | tf_op jit(solution)/shard_map/ppermute | solution.py:22
  50.5 2.5 %collective-permute-start.18 = (f32[2,136,128]{2,1,0:T(8,128)S(1)}, f32[2,136,128]{2,1,0:T(8,128)S(1)}, u32[]{:S(2)}, u32[]{:S(2)}) collective-permute-start(f32[2,136,128]{2,1,0:T(8,128)S(1)} %shard_map.66.refs_3_.refs_6_), channel_id=1, source_target_pairs={{0,4},{1,5},{2,6},{3,7},{4,0},{5,1},{6,2},{7,3},{8,12},{9,13},{10,... | collective-permute-start | bytes 417800 | tf_op jit(solution)/shard_map/ppermute | solution.py:22
  53.0 1.3 %collective-permute-start.24 = (f32[1,3,2,32,128]{4,3,2,1,0:T(8,128)S(1)}, f32[1,3,2,32,128]{4,3,2,1,0:T(8,128)S(1)}, u32[]{:S(2)}, u32[]{:S(2)}) collective-permute-start(f32[1,3,2,32,128]{4,3,2,1,0:T(8,128)S(1)} %bitcast.21), channel_id=1, source_target_pairs={{0,16},{8,24},{16,0},{24,8},{1,17},{9,25},{17,1},{25,9},{2,18},{10... | collective-permute-start | bytes 294920 | tf_op jit(solution)/shard_map/ppermute | solution.py:22
  54.3 1.7 %collective-permute-start.23 = (f32[2,136,128]{2,1,0:T(8,128)S(1)}, f32[2,136,128]{2,1,0:T(8,128)S(1)}, u32[]{:S(2)}, u32[]{:S(2)}) collective-permute-start(f32[2,136,128]{2,1,0:T(8,128)S(1)} %shard_map.70.refs_7_), channel_id=1, source_target_pairs={{0,6},{1,7},{2,4},{3,5},{4,2},{5,3},{6,0},{7,1},{8,14},{9,15},{10,... | collective-permute-start | bytes 417800 | tf_op jit(solution)/shard_map/ppermute | solution.py:22
  57.2 2.3 %collective-permute-start.27 = (f32[3,2,40,128]{3,2,1,0:T(8,128)S(1)}, f32[3,2,40,128]{3,2,1,0:T(8,128)S(1)}, u32[]{:S(2)}, u32[]{:S(2)}) collective-permute-start(f32[3,2,40,128]{3,2,1,0:T(8,128)S(1)} %get-tuple-element.45), channel_id=1, source_target_pairs={{0,16},{8,24},{16,0},{24,8},{1,17},{9,25},{17,1},{25,9},{2,18},{10... | collective-permute-start | bytes 368648 | tf_op jit(solution)/shard_map/ppermute | solution.py:22
  59.5 1.4 %collective-permute-start.28 = (f32[3,2,40,128]{3,2,1,0:T(8,128)S(1)}, f32[3,2,40,128]{3,2,1,0:T(8,128)S(1)}, u32[]{:S(2)}, u32[]{:S(2)}) collective-permute-start(f32[3,2,40,128]{3,2,1,0:T(8,128)S(1)} %get-tuple-element.46), channel_id=1, source_target_pairs={{0,24},{8,16},{16,8},{24,0},{1,25},{9,17},{17,9},{25,1},{2,26},{10... | collective-permute-start | bytes 368648 | tf_op jit(solution)/shard_map/ppermute | solution.py:22
  61.2 1.3 %collective-permute-done.24 = f32[1,3,2,32,128]{4,3,2,1,0:T(8,128)S(1)} collective-permute-done((f32[1,3,2,32,128]{4,3,2,1,0:T(8,128)S(1)}, f32[1,3,2,32,128]{4,3,2,1,0:T(8,128)S(1)}, u32[]{:S(2)}, u32[]{:S(2)}) %collective-permute-start.24) | collective-permute-done | bytes 98336 | tf_op jit(solution)/shard_map/ppermute | solution.py:22
  62.5 1.4 %collective-permute-done.26.refs_10_ = f32[3,2,40,128]{3,2,1,0:T(8,128)S(1)} collective-permute-done((f32[3,2,40,128]{3,2,1,0:T(8,128)S(1)}, f32[3,2,40,128]{3,2,1,0:T(8,128)S(1)}, u32[]{:S(2)}, u32[]{:S(2)}) %collective-permute-start.26) | collective-permute-done | bytes 122912 | tf_op jit(solution)/shard_map/ppermute | solution.py:22
  63.9 4.6 %collective-permute-done.27.refs_11_ = f32[3,2,40,128]{3,2,1,0:T(8,128)S(1)} collective-permute-done((f32[3,2,40,128]{3,2,1,0:T(8,128)S(1)}, f32[3,2,40,128]{3,2,1,0:T(8,128)S(1)}, u32[]{:S(2)}, u32[]{:S(2)}) %collective-permute-start.27) | collective-permute-done | bytes 122912 | tf_op jit(solution)/shard_map/ppermute | solution.py:22
  (75 shorter events, 7.5 us)
Async XLA Ops:
  0.0 11.4 %collective-permute-start = (s32[1,1,8]{2,1,0:T(1,128)}, s32[1,1,8]{2,1,0:T(1,128)S(1)}, u32[]{:S(2)}, u32[]{:S(2)}) collective-permute-start(s32[1,1,8]{2,1,0:T(1,128)} %map_any.1), channel_id=1, source_target_pairs={{0,8},{8,0},{16,24},{24,16},{1,9},{9,1},{17,25},{25,17},{2,10},{10... | collective-permute-start | bytes 104 | tf_op jit(solution)/shard_map/ppermute | solution.py:22
  3.0 8.4 %collective-permute-start.2 = (s32[1,1,8]{2,1,0:T(1,128)}, s32[1,1,8]{2,1,0:T(1,128)S(1)}, u32[]{:S(2)}, u32[]{:S(2)}) collective-permute-start(s32[1,1,8]{2,1,0:T(1,128)} %map_any.1), channel_id=1, source_target_pairs={{0,24},{8,16},{16,8},{24,0},{1,25},{9,17},{17,9},{25,1},{2,26},{10... | collective-permute-start | bytes 104 | tf_op jit(solution)/shard_map/ppermute | solution.py:22
  5.5 5.9 %collective-permute-start.1 = (s32[1,1,8]{2,1,0:T(1,128)}, s32[1,1,8]{2,1,0:T(1,128)S(1)}, u32[]{:S(2)}, u32[]{:S(2)}) collective-permute-start(s32[1,1,8]{2,1,0:T(1,128)} %map_any.1), channel_id=1, source_target_pairs={{0,16},{8,24},{16,0},{24,8},{1,17},{9,25},{17,1},{25,9},{2,18},{10... | collective-permute-start | bytes 104 | tf_op jit(solution)/shard_map/ppermute | solution.py:22
  12.4 1.7 %collective-permute-start.3 = (f32[4,152,128]{2,1,0:T(8,128)S(1)}, f32[4,152,128]{2,1,0:T(8,128)S(1)}, u32[]{:S(2)}, u32[]{:S(2)}) collective-permute-start(f32[4,152,128]{2,1,0:T(8,128)S(1)} %get-tuple-element.55), channel_id=1, source_target_pairs={{0,1},{1,0},{2,3},{3,2},{4,5},{5,4},{6,7},{7,6},{8,9},{9,8},{10,11... | collective-permute-start | bytes 933896 | tf_op jit(solution)/shard_map/ppermute | solution.py:22
  14.2 3.8 %collective-permute-start.4 = (f32[4,784,128]{2,1,0:T(8,128)S(1)}, f32[4,784,128]{2,1,0:T(8,128)S(1)}, u32[]{:S(2)}, u32[]{:S(2)}) collective-permute-start(f32[4,784,128]{2,1,0:T(8,128)S(1)} %shard_map.52), channel_id=1, source_target_pairs={{0,1},{1,0},{2,3},{3,2},{4,5},{5,4},{6,7},{7,6},{8,9},{9,8},{10,11... | collective-permute-start | bytes 4816904 | tf_op jit(solution)/shard_map/ppermute | solution.py:22
  14.5 6.9 %collective-permute-start.5 = (f32[2,152,128]{2,1,0:T(8,128)S(1)}, f32[2,152,128]{2,1,0:T(8,128)S(1)}, u32[]{:S(2)}, u32[]{:S(2)}) collective-permute-start(f32[2,152,128]{2,1,0:T(8,128)S(1)} %shard_map.49.refs_0_), channel_id=1, source_target_pairs={{0,2},{1,3},{2,0},{3,1},{4,6},{5,7},{6,4},{7,5},{8,10},{9,11},{10,... | collective-permute-start | bytes 466952 | tf_op jit(solution)/shard_map/ppermute | solution.py:22
  16.0 9.2 %collective-permute-start.11 = (f32[2,152,128]{2,1,0:T(8,128)S(1)}, f32[2,152,128]{2,1,0:T(8,128)S(1)}, u32[]{:S(2)}, u32[]{:S(2)}) collective-permute-start(f32[2,152,128]{2,1,0:T(8,128)S(1)} %shard_map.50.refs_1_), channel_id=1, source_target_pairs={{0,4},{1,5},{2,6},{3,7},{4,0},{5,1},{6,2},{7,3},{8,12},{9,13},{10,... | collective-permute-start | bytes 466952 | tf_op jit(solution)/shard_map/ppermute | solution.py:22
  17.5 9.4 %collective-permute-start.13 = (f32[2,152,128]{2,1,0:T(8,128)S(1)}, f32[2,152,128]{2,1,0:T(8,128)S(1)}, u32[]{:S(2)}, u32[]{:S(2)}) collective-permute-start(f32[2,152,128]{2,1,0:T(8,128)S(1)} %shard_map.51.refs_2_), channel_id=1, source_target_pairs={{0,6},{1,7},{2,4},{3,5},{4,2},{5,3},{6,0},{7,1},{8,14},{9,15},{10,... | collective-permute-start | bytes 466952 | tf_op jit(solution)/shard_map/ppermute | solution.py:22
  21.4 7.8 %collective-permute-start.6 = (f32[2,200,128]{2,1,0:T(8,128)S(1)}, f32[2,200,128]{2,1,0:T(8,128)S(1)}, u32[]{:S(2)}, u32[]{:S(2)}) collective-permute-start(f32[2,200,128]{2,1,0:T(8,128)S(1)} %shard_map.53.refs_5_), channel_id=1, source_target_pairs={{0,2},{1,3},{2,0},{3,1},{4,6},{5,7},{6,4},{7,5},{8,10},{9,11},{10,... | collective-permute-start | bytes 614408 | tf_op jit(solution)/shard_map/ppermute | solution.py:22
  23.1 12.5 %collective-permute-start.10 = (f32[2,200,128]{2,1,0:T(8,128)S(1)}, f32[2,200,128]{2,1,0:T(8,128)S(1)}, u32[]{:S(2)}, u32[]{:S(2)}) collective-permute-start(f32[2,200,128]{2,1,0:T(8,128)S(1)} %shard_map.57.refs_6_), channel_id=1, source_target_pairs={{0,4},{1,5},{2,6},{3,7},{4,0},{5,1},{6,2},{7,3},{8,12},{9,13},{10,... | collective-permute-start | bytes 614408 | tf_op jit(solution)/shard_map/ppermute | solution.py:22
  25.2 11.7 %collective-permute-start.12 = (f32[2,200,128]{2,1,0:T(8,128)S(1)}, f32[2,200,128]{2,1,0:T(8,128)S(1)}, u32[]{:S(2)}, u32[]{:S(2)}) collective-permute-start(f32[2,200,128]{2,1,0:T(8,128)S(1)} %shard_map.58.refs_7_), channel_id=1, source_target_pairs={{0,6},{1,7},{2,4},{3,5},{4,2},{5,3},{6,0},{7,1},{8,14},{9,15},{10,... | collective-permute-start | bytes 614408 | tf_op jit(solution)/shard_map/ppermute | solution.py:22
  27.3 5.5 %collective-permute-start.14 = (f32[2,3,2,24,128]{4,3,2,1,0:T(8,128)S(1)}, f32[2,3,2,24,128]{4,3,2,1,0:T(8,128)S(1)}, u32[]{:S(2)}, u32[]{:S(2)}) collective-permute-start(f32[2,3,2,24,128]{4,3,2,1,0:T(8,128)S(1)} %pad_maximum_fusion.2), channel_id=1, source_target_pairs={{0,8},{8,0},{16,24},{24,16},{1,9},{9,1},{17,25},{25,17},{2,10},{10... | collective-permute-start | bytes 442376 | tf_op jit(solution)/shard_map/ppermute | solution.py:22
  29.2 9.8 %collective-permute-start.7 = (f32[2,200,128]{2,1,0:T(8,128)S(1)}, f32[2,200,128]{2,1,0:T(8,128)S(1)}, u32[]{:S(2)}, u32[]{:S(2)}) collective-permute-start(f32[2,200,128]{2,1,0:T(8,128)S(1)} %shard_map.54.refs_2_.refs_5_), channel_id=1, source_target_pairs={{0,2},{1,3},{2,0},{3,1},{4,6},{5,7},{6,4},{7,5},{8,10},{9,11},{10,... | collective-permute-start | bytes 614408 | tf_op jit(solution)/shard_map/ppermute | solution.py:22
  31.6 12.8 %collective-permute-start.20 = (f32[2,200,128]{2,1,0:T(8,128)S(1)}, f32[2,200,128]{2,1,0:T(8,128)S(1)}, u32[]{:S(2)}, u32[]{:S(2)}) collective-permute-start(f32[2,200,128]{2,1,0:T(8,128)S(1)} %shard_map.59.refs_3_.refs_6_), channel_id=1, source_target_pairs={{0,4},{1,5},{2,6},{3,7},{4,0},{5,1},{6,2},{7,3},{8,12},{9,13},{10,... | collective-permute-start | bytes 614408 | tf_op jit(solution)/shard_map/ppermute | solution.py:22
  32.8 7.2 %collective-permute-start.16 = (f32[1,3,2,24,128]{4,3,2,1,0:T(8,128)S(1)}, f32[1,3,2,24,128]{4,3,2,1,0:T(8,128)S(1)}, u32[]{:S(2)}, u32[]{:S(2)}) collective-permute-start(f32[1,3,2,24,128]{4,3,2,1,0:T(8,128)S(1)} %bitcast.22), channel_id=1, source_target_pairs={{0,16},{8,24},{16,0},{24,8},{1,17},{9,25},{17,1},{25,9},{2,18},{10... | collective-permute-start | bytes 221192 | tf_op jit(solution)/shard_map/ppermute | solution.py:22
  35.7 10.5 %collective-permute-start.21 = (f32[2,200,128]{2,1,0:T(8,128)S(1)}, f32[2,200,128]{2,1,0:T(8,128)S(1)}, u32[]{:S(2)}, u32[]{:S(2)}) collective-permute-start(f32[2,200,128]{2,1,0:T(8,128)S(1)} %shard_map.62.refs_7_), channel_id=1, source_target_pairs={{0,6},{1,7},{2,4},{3,5},{4,2},{5,3},{6,0},{7,1},{8,14},{9,15},{10,... | collective-permute-start | bytes 614408 | tf_op jit(solution)/shard_map/ppermute | solution.py:22
  37.3 5.7 %collective-permute-start.15 = (f32[2,3,2,32,128]{4,3,2,1,0:T(8,128)S(1)}, f32[2,3,2,32,128]{4,3,2,1,0:T(8,128)S(1)}, u32[]{:S(2)}, u32[]{:S(2)}) collective-permute-start(f32[2,3,2,32,128]{4,3,2,1,0:T(8,128)S(1)} %pad_maximum_fusion), channel_id=1, source_target_pairs={{0,8},{8,0},{16,24},{24,16},{1,9},{9,1},{17,25},{25,17},{2,10},{10... | collective-permute-start | bytes 589832 | tf_op jit(solution)/shard_map/ppermute | solution.py:22
  39.0 10.3 %collective-permute-start.8 = (f32[2,248,128]{2,1,0:T(8,128)S(1)}, f32[2,248,128]{2,1,0:T(8,128)S(1)}, u32[]{:S(2)}, u32[]{:S(2)}) collective-permute-start(f32[2,248,128]{2,1,0:T(8,128)S(1)} %shard_map.55.refs_2_.refs_5_), channel_id=1, source_target_pairs={{0,2},{1,3},{2,0},{3,1},{4,6},{5,7},{6,4},{7,5},{8,10},{9,11},{10,... | collective-permute-start | bytes 761864 | tf_op jit(solution)/shard_map/ppermute | solution.py:22
  40.0 14.3 %collective-permute-start.19 = (f32[2,248,128]{2,1,0:T(8,128)S(1)}, f32[2,248,128]{2,1,0:T(8,128)S(1)}, u32[]{:S(2)}, u32[]{:S(2)}) collective-permute-start(f32[2,248,128]{2,1,0:T(8,128)S(1)} %shard_map.64.refs_3_.refs_6_), channel_id=1, source_target_pairs={{0,4},{1,5},{2,6},{3,7},{4,0},{5,1},{6,2},{7,3},{8,12},{9,13},{10,... | collective-permute-start | bytes 761864 | tf_op jit(solution)/shard_map/ppermute | solution.py:22
  43.1 7.4 %collective-permute-start.17 = (f32[1,3,2,32,128]{4,3,2,1,0:T(8,128)S(1)}, f32[1,3,2,32,128]{4,3,2,1,0:T(8,128)S(1)}, u32[]{:S(2)}, u32[]{:S(2)}) collective-permute-start(f32[1,3,2,32,128]{4,3,2,1,0:T(8,128)S(1)} %bitcast.20), channel_id=1, source_target_pairs={{0,16},{8,24},{16,0},{24,8},{1,17},{9,25},{17,1},{25,9},{2,18},{10... | collective-permute-start | bytes 294920 | tf_op jit(solution)/shard_map/ppermute | solution.py:22
  44.4 11.6 %collective-permute-start.25 = (f32[2,248,128]{2,1,0:T(8,128)S(1)}, f32[2,248,128]{2,1,0:T(8,128)S(1)}, u32[]{:S(2)}, u32[]{:S(2)}) collective-permute-start(f32[2,248,128]{2,1,0:T(8,128)S(1)} %shard_map.67.refs_7_), channel_id=1, source_target_pairs={{0,6},{1,7},{2,4},{3,5},{4,2},{5,3},{6,0},{7,1},{8,14},{9,15},{10,... | collective-permute-start | bytes 761864 | tf_op jit(solution)/shard_map/ppermute | solution.py:22
  46.6 6.4 %collective-permute-start.22 = (f32[2,3,2,32,128]{4,3,2,1,0:T(8,128)S(1)}, f32[2,3,2,32,128]{4,3,2,1,0:T(8,128)S(1)}, u32[]{:S(2)}, u32[]{:S(2)}) collective-permute-start(f32[2,3,2,32,128]{4,3,2,1,0:T(8,128)S(1)} %pad_maximum_fusion.1), channel_id=1, source_target_pairs={{0,8},{8,0},{16,24},{24,16},{1,9},{9,1},{17,25},{25,17},{2,10},{10... | collective-permute-start | bytes 589832 | tf_op jit(solution)/shard_map/ppermute | solution.py:22
  49.3 7.9 %collective-permute-start.9 = (f32[2,136,128]{2,1,0:T(8,128)S(1)}, f32[2,136,128]{2,1,0:T(8,128)S(1)}, u32[]{:S(2)}, u32[]{:S(2)}) collective-permute-start(f32[2,136,128]{2,1,0:T(8,128)S(1)} %shard_map.56.refs_2_.refs_5_), channel_id=1, source_target_pairs={{0,2},{1,3},{2,0},{3,1},{4,6},{5,7},{6,4},{7,5},{8,10},{9,11},{10,... | collective-permute-start | bytes 417800 | tf_op jit(solution)/shard_map/ppermute | solution.py:22
  50.5 9.0 %collective-permute-start.18 = (f32[2,136,128]{2,1,0:T(8,128)S(1)}, f32[2,136,128]{2,1,0:T(8,128)S(1)}, u32[]{:S(2)}, u32[]{:S(2)}) collective-permute-start(f32[2,136,128]{2,1,0:T(8,128)S(1)} %shard_map.66.refs_3_.refs_6_), channel_id=1, source_target_pairs={{0,4},{1,5},{2,6},{3,7},{4,0},{5,1},{6,2},{7,3},{8,12},{9,13},{10,... | collective-permute-start | bytes 417800 | tf_op jit(solution)/shard_map/ppermute | solution.py:22
  53.0 9.5 %collective-permute-start.24 = (f32[1,3,2,32,128]{4,3,2,1,0:T(8,128)S(1)}, f32[1,3,2,32,128]{4,3,2,1,0:T(8,128)S(1)}, u32[]{:S(2)}, u32[]{:S(2)}) collective-permute-start(f32[1,3,2,32,128]{4,3,2,1,0:T(8,128)S(1)} %bitcast.21), channel_id=1, source_target_pairs={{0,16},{8,24},{16,0},{24,8},{1,17},{9,25},{17,1},{25,9},{2,18},{10... | collective-permute-start | bytes 294920 | tf_op jit(solution)/shard_map/ppermute | solution.py:22
  54.3 6.7 %collective-permute-start.23 = (f32[2,136,128]{2,1,0:T(8,128)S(1)}, f32[2,136,128]{2,1,0:T(8,128)S(1)}, u32[]{:S(2)}, u32[]{:S(2)}) collective-permute-start(f32[2,136,128]{2,1,0:T(8,128)S(1)} %shard_map.70.refs_7_), channel_id=1, source_target_pairs={{0,6},{1,7},{2,4},{3,5},{4,2},{5,3},{6,0},{7,1},{8,14},{9,15},{10,... | collective-permute-start | bytes 417800 | tf_op jit(solution)/shard_map/ppermute | solution.py:22
  56.5 7.4 %collective-permute-start.26 = (f32[3,2,40,128]{3,2,1,0:T(8,128)S(1)}, f32[3,2,40,128]{3,2,1,0:T(8,128)S(1)}, u32[]{:S(2)}, u32[]{:S(2)}) collective-permute-start(f32[3,2,40,128]{3,2,1,0:T(8,128)S(1)} %get-tuple-element.44), channel_id=1, source_target_pairs={{0,8},{8,0},{16,24},{24,16},{1,9},{9,1},{17,25},{25,17},{2,10},{10... | collective-permute-start | bytes 368648 | tf_op jit(solution)/shard_map/ppermute | solution.py:22
  57.2 11.3 %collective-permute-start.27 = (f32[3,2,40,128]{3,2,1,0:T(8,128)S(1)}, f32[3,2,40,128]{3,2,1,0:T(8,128)S(1)}, u32[]{:S(2)}, u32[]{:S(2)}) collective-permute-start(f32[3,2,40,128]{3,2,1,0:T(8,128)S(1)} %get-tuple-element.45), channel_id=1, source_target_pairs={{0,16},{8,24},{16,0},{24,8},{1,17},{9,25},{17,1},{25,9},{2,18},{10... | collective-permute-start | bytes 368648 | tf_op jit(solution)/shard_map/ppermute | solution.py:22
  59.5 9.0 %collective-permute-start.28 = (f32[3,2,40,128]{3,2,1,0:T(8,128)S(1)}, f32[3,2,40,128]{3,2,1,0:T(8,128)S(1)}, u32[]{:S(2)}, u32[]{:S(2)}) collective-permute-start(f32[3,2,40,128]{3,2,1,0:T(8,128)S(1)} %get-tuple-element.46), channel_id=1, source_target_pairs={{0,24},{8,16},{16,8},{24,0},{1,25},{9,17},{17,9},{25,1},{2,26},{10... | collective-permute-start | bytes 368648 | tf_op jit(solution)/shard_map/ppermute | solution.py:22

commit v5 on v4

--- a/solution.py
+++ b/solution.py
@@ -107,7 +107,7 @@
     for apart in range(subs):
         for c in range(nb):
             entry = plan_ref[0, c] if apart == 0 else slot_refs[apart - 1][0, 0, c]
-            owner = lax.div(entry, ANC_DEV)
+            owner = (entry * (65536 // ANC_DEV + 1)) >> 16
             to = owner ^ my_tree
             to = (to & 1) * half + (to >> 1)
             goal[apart, c] = to
@@ -118,7 +118,7 @@
     for kept, chunks in shipments:
         for k in kept:
             place = k + (empty <= k).astype(jnp.int32)
-            apart = place // per_piece
+            apart = lax.div(place, jnp.int32(per_piece))
             for chunk in chunks:
                 for c in range(nb):
                     out_ref[goal[apart, c], pl.ds(at, counts[chunk]), :] = update_refs[chunk][
@@ -451,7 +451,7 @@
     def per_device(panels, pattern, child_map, ancestor_map):
         nb = child_map.shape[2]
         subs, trees = mesh.shape["subtree"], mesh.shape["forest"]
-        if nb == trees and nb % (2 * subs) == 0 and subs < META:
+        if nb == trees and nb % (2 * subs) == 0 and subs < META and trees <= 4096:
             return per_device_blocks(panels, pattern, child_map, ancestor_map)
         return per_device_halving(panels, pattern, child_map, ancestor_map)
 

time: 69.7 us -> 69.6 us (level)
  no operation moved by 1% of the time
where the time goes in v5:
time: 69.6 us; the launch traced here: 69.3 us
  starting transfers between devices  41.7 us (60%)
  waiting for transfers between devices  16.1 us (23%)
  Pallas kernels  10.8 us (16%)
    ppermute x29, starting transfers between devices, swapped(): lax.ppermute(shard, axis, [(i, i ^ apart) for i in range(lax.axis_size(ax...  41.7 us
    ppermute x29, waiting for transfers between devices, swapped(): lax.ppermute(shard, axis, [(i, i ^ apart) for i in range(lax.axis_size(ax...  16.1 us
    pallas_call x1, Pallas kernels, per_device_blocks(): pl.pallas_call(functools.partial(multiply_kernel, nb, per_piece, spans),...  5.76 us
    pallas_call x2, Pallas kernels, per_device_blocks(): pl.pallas_call(functools.partial(route_kernel, nb, per_piece, subs, group...  1.94 us
    pallas_call x5, Pallas kernels, gather(): pl.pallas_call(functools.partial(gather_kernel, nb, per_piece, kept, coun...  1.89 us
  transfers between devices with their start and end apart: 29, of which 9 were waited for; matrix products, arithmetic and copies ran while one was open for 1% of the time, Pallas kernels for 13%

profile of v5, /device:TPU:0, one launch (start us, length us, event | category | flops | bytes accessed | tf_op | source)
XLA Modules:
  0.0 69.3 jit_solution(17065628584599954183)
XLA Ops:
  0.0 3.0 %collective-permute-start = (s32[1,1,8]{2,1,0:T(1,128)}, s32[1,1,8]{2,1,0:T(1,128)S(1)}, u32[]{:S(2)}, u32[]{:S(2)}) collective-permute-start(s32[1,1,8]{2,1,0:T(1,128)} %map_any.1), channel_id=1, source_target_pairs={{0,8},{8,0},{16,24},{24,16},{1,9},{9,1},{17,25},{25,17},{2,10},{10... | collective-permute-start | bytes 104 | tf_op jit(solution)/shard_map/ppermute | solution.py:22
  3.0 2.5 %collective-permute-start.2 = (s32[1,1,8]{2,1,0:T(1,128)}, s32[1,1,8]{2,1,0:T(1,128)S(1)}, u32[]{:S(2)}, u32[]{:S(2)}) collective-permute-start(s32[1,1,8]{2,1,0:T(1,128)} %map_any.1), channel_id=1, source_target_pairs={{0,24},{8,16},{16,8},{24,0},{1,25},{9,17},{17,9},{25,1},{2,26},{10... | collective-permute-start | bytes 104 | tf_op jit(solution)/shard_map/ppermute | solution.py:22
  5.6 5.8 %shard_map.46 = (f32[8,192,128]{2,1,0:T(8,128)S(1)}, f32[8,256,128]{2,1,0:T(8,128)S(1)}, f32[8,256,128]{2,1,0:T(8,128)S(1)}, f32[8,320,128]{2,1,0:T(8,128)S(1)}, s32[2,8]{1,0:T(2,128)S(1)}) custom-call(s32[1,1,8]{2,1,0:T(1,128)} %child_any.1, s32[1,1,8,8]{3,2,1,0:T(8,128)} %pattern_any.1, s32[1,1,8]{2,1,0:T(1,128)} %map_any.1, bf16[1024,2048]{1,0:T(8,128)(2,1)} %bitcast.34), custom_call_target="tpu_custom_call" | custom-call | flops 4294967296 | bytes 4194304 | tf_op jit(solution)/shard_map/pallas_call | solution.py:278
  12.4 1.1 %shard_map.48.in_ref = f32[8,784,128]{2,1,0:T(8,128)S(1)} custom-call(s32[2,8]{1,0:T(2,128)S(1)} %get-tuple-element.26.plan_ref, s32[1,1,8]{2,1,0:T(1,128)S(1)} %collective-permute-done.refs_0_, s32[1,1,8]{2,1,0:T(1,128)S(1)} %collective-permute-done.1.refs_1_, s32[1,1,8]{2,1,0:T(1,128)S(1)} %collective-permute-done.2.refs_2_, ...), custom_call_target="tpu_custom_call" | custom-call | tf_op jit(solution)/shard_map/pallas_call | solution.py:307
  14.4 1.6 %collective-permute-start.5 = (f32[2,152,128]{2,1,0:T(8,128)S(1)}, f32[2,152,128]{2,1,0:T(8,128)S(1)}, u32[]{:S(2)}, u32[]{:S(2)}) collective-permute-start(f32[2,152,128]{2,1,0:T(8,128)S(1)} %shard_map.49.refs_0_), channel_id=1, source_target_pairs={{0,2},{1,3},{2,0},{3,1},{4,6},{5,7},{6,4},{7,5},{8,10},{9,11},{10,... | collective-permute-start | bytes 466952 | tf_op jit(solution)/shard_map/ppermute | solution.py:22
  16.0 1.5 %collective-permute-start.11 = (f32[2,152,128]{2,1,0:T(8,128)S(1)}, f32[2,152,128]{2,1,0:T(8,128)S(1)}, u32[]{:S(2)}, u32[]{:S(2)}) collective-permute-start(f32[2,152,128]{2,1,0:T(8,128)S(1)} %shard_map.50.refs_1_), channel_id=1, source_target_pairs={{0,4},{1,5},{2,6},{3,7},{4,0},{5,1},{6,2},{7,3},{8,12},{9,13},{10,... | collective-permute-start | bytes 466952 | tf_op jit(solution)/shard_map/ppermute | solution.py:22
  18.0 3.3 %collective-permute-done.5.refs_0_.refs_2_ = f32[2,152,128]{2,1,0:T(8,128)S(1)} collective-permute-done((f32[2,152,128]{2,1,0:T(8,128)S(1)}, f32[2,152,128]{2,1,0:T(8,128)S(1)}, u32[]{:S(2)}, u32[]{:S(2)}) %collective-permute-start.5) | collective-permute-done | bytes 155680 | tf_op jit(solution)/shard_map/ppermute | solution.py:22
  21.4 1.6 %collective-permute-start.6 = (f32[2,200,128]{2,1,0:T(8,128)S(1)}, f32[2,200,128]{2,1,0:T(8,128)S(1)}, u32[]{:S(2)}, u32[]{:S(2)}) collective-permute-start(f32[2,200,128]{2,1,0:T(8,128)S(1)} %shard_map.53.refs_5_), channel_id=1, source_target_pairs={{0,2},{1,3},{2,0},{3,1},{4,6},{5,7},{6,4},{7,5},{8,10},{9,11},{10,... | collective-permute-start | bytes 614408 | tf_op jit(solution)/shard_map/ppermute | solution.py:22
  23.1 1.6 %collective-permute-start.10 = (f32[2,200,128]{2,1,0:T(8,128)S(1)}, f32[2,200,128]{2,1,0:T(8,128)S(1)}, u32[]{:S(2)}, u32[]{:S(2)}) collective-permute-start(f32[2,200,128]{2,1,0:T(8,128)S(1)} %shard_map.57.refs_6_), channel_id=1, source_target_pairs={{0,4},{1,5},{2,6},{3,7},{4,0},{5,1},{6,2},{7,3},{8,12},{9,13},{10,... | collective-permute-start | bytes 614408 | tf_op jit(solution)/shard_map/ppermute | solution.py:22
  25.2 1.7 %collective-permute-start.12 = (f32[2,200,128]{2,1,0:T(8,128)S(1)}, f32[2,200,128]{2,1,0:T(8,128)S(1)}, u32[]{:S(2)}, u32[]{:S(2)}) collective-permute-start(f32[2,200,128]{2,1,0:T(8,128)S(1)} %shard_map.58.refs_7_), channel_id=1, source_target_pairs={{0,6},{1,7},{2,4},{3,5},{4,2},{5,3},{6,0},{7,1},{8,14},{9,15},{10,... | collective-permute-start | bytes 614408 | tf_op jit(solution)/shard_map/ppermute | solution.py:22
  27.3 1.9 %collective-permute-start.14 = (f32[2,3,2,24,128]{4,3,2,1,0:T(8,128)S(1)}, f32[2,3,2,24,128]{4,3,2,1,0:T(8,128)S(1)}, u32[]{:S(2)}, u32[]{:S(2)}) collective-permute-start(f32[2,3,2,24,128]{4,3,2,1,0:T(8,128)S(1)} %pad_maximum_fusion.2), channel_id=1, source_target_pairs={{0,8},{8,0},{16,24},{24,16},{1,9},{9,1},{17,25},{25,17},{2,10},{10... | collective-permute-start | bytes 442376 | tf_op jit(solution)/shard_map/ppermute | solution.py:22
  29.2 2.2 %collective-permute-start.7 = (f32[2,200,128]{2,1,0:T(8,128)S(1)}, f32[2,200,128]{2,1,0:T(8,128)S(1)}, u32[]{:S(2)}, u32[]{:S(2)}) collective-permute-start(f32[2,200,128]{2,1,0:T(8,128)S(1)} %shard_map.54.refs_2_.refs_5_), channel_id=1, source_target_pairs={{0,2},{1,3},{2,0},{3,1},{4,6},{5,7},{6,4},{7,5},{8,10},{9,11},{10,... | collective-permute-start | bytes 614408 | tf_op jit(solution)/shard_map/ppermute | solution.py:22
  31.5 1.2 %collective-permute-start.20 = (f32[2,200,128]{2,1,0:T(8,128)S(1)}, f32[2,200,128]{2,1,0:T(8,128)S(1)}, u32[]{:S(2)}, u32[]{:S(2)}) collective-permute-start(f32[2,200,128]{2,1,0:T(8,128)S(1)} %shard_map.59.refs_3_.refs_6_), channel_id=1, source_target_pairs={{0,4},{1,5},{2,6},{3,7},{4,0},{5,1},{6,2},{7,3},{8,12},{9,13},{10,... | collective-permute-start | bytes 614408 | tf_op jit(solution)/shard_map/ppermute | solution.py:22
  32.8 2.9 %collective-permute-start.16 = (f32[1,3,2,24,128]{4,3,2,1,0:T(8,128)S(1)}, f32[1,3,2,24,128]{4,3,2,1,0:T(8,128)S(1)}, u32[]{:S(2)}, u32[]{:S(2)}) collective-permute-start(f32[1,3,2,24,128]{4,3,2,1,0:T(8,128)S(1)} %bitcast.22), channel_id=1, source_target_pairs={{0,16},{8,24},{16,0},{24,8},{1,17},{9,25},{17,1},{25,9},{2,18},{10... | collective-permute-start | bytes 221192 | tf_op jit(solution)/shard_map/ppermute | solution.py:22
  35.7 1.2 %collective-permute-start.21 = (f32[2,200,128]{2,1,0:T(8,128)S(1)}, f32[2,200,128]{2,1,0:T(8,128)S(1)}, u32[]{:S(2)}, u32[]{:S(2)}) collective-permute-start(f32[2,200,128]{2,1,0:T(8,128)S(1)} %shard_map.62.refs_7_), channel_id=1, source_target_pairs={{0,6},{1,7},{2,4},{3,5},{4,2},{5,3},{6,0},{7,1},{8,14},{9,15},{10,... | collective-permute-start | bytes 614408 | tf_op jit(solution)/shard_map/ppermute | solution.py:22
  37.9 1.0 %collective-permute-done.7.refs_0_.refs_2_ = f32[2,200,128]{2,1,0:T(8,128)S(1)} collective-permute-done((f32[2,200,128]{2,1,0:T(8,128)S(1)}, f32[2,200,128]{2,1,0:T(8,128)S(1)}, u32[]{:S(2)}, u32[]{:S(2)}) %collective-permute-start.7) | collective-permute-done | bytes 204832 | tf_op jit(solution)/shard_map/ppermute | solution.py:22
  39.0 1.0 %collective-permute-start.8 = (f32[2,248,128]{2,1,0:T(8,128)S(1)}, f32[2,248,128]{2,1,0:T(8,128)S(1)}, u32[]{:S(2)}, u32[]{:S(2)}) collective-permute-start(f32[2,248,128]{2,1,0:T(8,128)S(1)} %shard_map.55.refs_2_.refs_5_), channel_id=1, source_target_pairs={{0,2},{1,3},{2,0},{3,1},{4,6},{5,7},{6,4},{7,5},{8,10},{9,11},{10,... | collective-permute-start | bytes 761864 | tf_op jit(solution)/shard_map/ppermute | solution.py:22
  39.9 1.5 %collective-permute-start.19 = (f32[2,248,128]{2,1,0:T(8,128)S(1)}, f32[2,248,128]{2,1,0:T(8,128)S(1)}, u32[]{:S(2)}, u32[]{:S(2)}) collective-permute-start(f32[2,248,128]{2,1,0:T(8,128)S(1)} %shard_map.64.refs_3_.refs_6_), channel_id=1, source_target_pairs={{0,4},{1,5},{2,6},{3,7},{4,0},{5,1},{6,2},{7,3},{8,12},{9,13},{10,... | collective-permute-start | bytes 761864 | tf_op jit(solution)/shard_map/ppermute | solution.py:22
  41.5 1.6 %collective-permute-done.15.refs_1_ = f32[2,3,2,32,128]{4,3,2,1,0:T(8,128)S(1)} collective-permute-done((f32[2,3,2,32,128]{4,3,2,1,0:T(8,128)S(1)}, f32[2,3,2,32,128]{4,3,2,1,0:T(8,128)S(1)}, u32[]{:S(2)}, u32[]{:S(2)}) %collective-permute-start.15) | collective-permute-done | bytes 196640 | tf_op jit(solution)/shard_map/ppermute | solution.py:22
  43.0 1.3 %collective-permute-start.17 = (f32[1,3,2,32,128]{4,3,2,1,0:T(8,128)S(1)}, f32[1,3,2,32,128]{4,3,2,1,0:T(8,128)S(1)}, u32[]{:S(2)}, u32[]{:S(2)}) collective-permute-start(f32[1,3,2,32,128]{4,3,2,1,0:T(8,128)S(1)} %bitcast.20), channel_id=1, source_target_pairs={{0,16},{8,24},{16,0},{24,8},{1,17},{9,25},{17,1},{25,9},{2,18},{10... | collective-permute-start | bytes 294920 | tf_op jit(solution)/shard_map/ppermute | solution.py:22
  44.4 1.8 %collective-permute-start.25 = (f32[2,248,128]{2,1,0:T(8,128)S(1)}, f32[2,248,128]{2,1,0:T(8,128)S(1)}, u32[]{:S(2)}, u32[]{:S(2)}) collective-permute-start(f32[2,248,128]{2,1,0:T(8,128)S(1)} %shard_map.67.refs_7_), channel_id=1, source_target_pairs={{0,6},{1,7},{2,4},{3,5},{4,2},{5,3},{6,0},{7,1},{8,14},{9,15},{10,... | collective-permute-start | bytes 761864 | tf_op jit(solution)/shard_map/ppermute | solution.py:22
  47.4 1.9 %collective-permute-done.8.refs_0_.refs_2_ = f32[2,248,128]{2,1,0:T(8,128)S(1)} collective-permute-done((f32[2,248,128]{2,1,0:T(8,128)S(1)}, f32[2,248,128]{2,1,0:T(8,128)S(1)}, u32[]{:S(2)}, u32[]{:S(2)}) %collective-permute-start.8) | collective-permute-done | bytes 253984 | tf_op jit(solution)/shard_map/ppermute | solution.py:22
  49.3 1.1 %collective-permute-start.9 = (f32[2,136,128]{2,1,0:T(8,128)S(1)}, f32[2,136,128]{2,1,0:T(8,128)S(1)}, u32[]{:S(2)}, u32[]{:S(2)}) collective-permute-start(f32[2,136,128]{2,1,0:T(8,128)S(1)} %shard_map.56.refs_2_.refs_5_), channel_id=1, source_target_pairs={{0,2},{1,3},{2,0},{3,1},{4,6},{5,7},{6,4},{7,5},{8,10},{9,11},{10,... | collective-permute-start | bytes 417800 | tf_op jit(solution)/shard_map/ppermute | solution.py:22
  50.4 2.5 %collective-permute-start.18 = (f32[2,136,128]{2,1,0:T(8,128)S(1)}, f32[2,136,128]{2,1,0:T(8,128)S(1)}, u32[]{:S(2)}, u32[]{:S(2)}) collective-permute-start(f32[2,136,128]{2,1,0:T(8,128)S(1)} %shard_map.66.refs_3_.refs_6_), channel_id=1, source_target_pairs={{0,4},{1,5},{2,6},{3,7},{4,0},{5,1},{6,2},{7,3},{8,12},{9,13},{10,... | collective-permute-start | bytes 417800 | tf_op jit(solution)/shard_map/ppermute | solution.py:22
  53.0 1.3 %collective-permute-start.24 = (f32[1,3,2,32,128]{4,3,2,1,0:T(8,128)S(1)}, f32[1,3,2,32,128]{4,3,2,1,0:T(8,128)S(1)}, u32[]{:S(2)}, u32[]{:S(2)}) collective-permute-start(f32[1,3,2,32,128]{4,3,2,1,0:T(8,128)S(1)} %bitcast.21), channel_id=1, source_target_pairs={{0,16},{8,24},{16,0},{24,8},{1,17},{9,25},{17,1},{25,9},{2,18},{10... | collective-permute-start | bytes 294920 | tf_op jit(solution)/shard_map/ppermute | solution.py:22
  54.2 1.7 %collective-permute-start.23 = (f32[2,136,128]{2,1,0:T(8,128)S(1)}, f32[2,136,128]{2,1,0:T(8,128)S(1)}, u32[]{:S(2)}, u32[]{:S(2)}) collective-permute-start(f32[2,136,128]{2,1,0:T(8,128)S(1)} %shard_map.70.refs_7_), channel_id=1, source_target_pairs={{0,6},{1,7},{2,4},{3,5},{4,2},{5,3},{6,0},{7,1},{8,14},{9,15},{10,... | collective-permute-start | bytes 417800 | tf_op jit(solution)/shard_map/ppermute | solution.py:22
  57.2 2.3 %collective-permute-start.27 = (f32[3,2,40,128]{3,2,1,0:T(8,128)S(1)}, f32[3,2,40,128]{3,2,1,0:T(8,128)S(1)}, u32[]{:S(2)}, u32[]{:S(2)}) collective-permute-start(f32[3,2,40,128]{3,2,1,0:T(8,128)S(1)} %get-tuple-element.45), channel_id=1, source_target_pairs={{0,16},{8,24},{16,0},{24,8},{1,17},{9,25},{17,1},{25,9},{2,18},{10... | collective-permute-start | bytes 368648 | tf_op jit(solution)/shard_map/ppermute | solution.py:22
  59.5 1.4 %collective-permute-start.28 = (f32[3,2,40,128]{3,2,1,0:T(8,128)S(1)}, f32[3,2,40,128]{3,2,1,0:T(8,128)S(1)}, u32[]{:S(2)}, u32[]{:S(2)}) collective-permute-start(f32[3,2,40,128]{3,2,1,0:T(8,128)S(1)} %get-tuple-element.46), channel_id=1, source_target_pairs={{0,24},{8,16},{16,8},{24,0},{1,25},{9,17},{17,9},{25,1},{2,26},{10... | collective-permute-start | bytes 368648 | tf_op jit(solution)/shard_map/ppermute | solution.py:22
  61.2 1.3 %collective-permute-done.24 = f32[1,3,2,32,128]{4,3,2,1,0:T(8,128)S(1)} collective-permute-done((f32[1,3,2,32,128]{4,3,2,1,0:T(8,128)S(1)}, f32[1,3,2,32,128]{4,3,2,1,0:T(8,128)S(1)}, u32[]{:S(2)}, u32[]{:S(2)}) %collective-permute-start.24) | collective-permute-done | bytes 98336 | tf_op jit(solution)/shard_map/ppermute | solution.py:22
  62.5 1.4 %collective-permute-done.26.refs_10_ = f32[3,2,40,128]{3,2,1,0:T(8,128)S(1)} collective-permute-done((f32[3,2,40,128]{3,2,1,0:T(8,128)S(1)}, f32[3,2,40,128]{3,2,1,0:T(8,128)S(1)}, u32[]{:S(2)}, u32[]{:S(2)}) %collective-permute-start.26) | collective-permute-done | bytes 122912 | tf_op jit(solution)/shard_map/ppermute | solution.py:22
  63.9 4.6 %collective-permute-done.27.refs_11_ = f32[3,2,40,128]{3,2,1,0:T(8,128)S(1)} collective-permute-done((f32[3,2,40,128]{3,2,1,0:T(8,128)S(1)}, f32[3,2,40,128]{3,2,1,0:T(8,128)S(1)}, u32[]{:S(2)}, u32[]{:S(2)}) %collective-permute-start.27) | collective-permute-done | bytes 122912 | tf_op jit(solution)/shard_map/ppermute | solution.py:22
  68.4 0.8 %shard_map.73 = f32[1,3,2,128,128]{4,3,2,1,0:T(8,128)} custom-call(f32[3,2,128,128]{3,2,1,0:T(8,128)S(1)} %shard_map.71.near_ref, f32[3,1,24,128]{3,2,1,0:T(8,128)S(1)} %get-tuple-element.40.refs_0_, f32[3,2,24,128]{3,2,1,0:T(8,128)S(1)} %slice_bitcast_fusion.2.refs_1_, f32[3,2,24,128]{3,2,1,0:T(8,128)S(1)} %bitcast.26, ...), custom_call_target="tpu_custom_call" | custom-call | tf_op jit(solution)/shard_map/pallas_call | solution.py:366
  (75 shorter events, 7.5 us)
Async XLA Ops:
  0.0 11.4 %collective-permute-start = (s32[1,1,8]{2,1,0:T(1,128)}, s32[1,1,8]{2,1,0:T(1,128)S(1)}, u32[]{:S(2)}, u32[]{:S(2)}) collective-permute-start(s32[1,1,8]{2,1,0:T(1,128)} %map_any.1), channel_id=1, source_target_pairs={{0,8},{8,0},{16,24},{24,16},{1,9},{9,1},{17,25},{25,17},{2,10},{10... | collective-permute-start | bytes 104 | tf_op jit(solution)/shard_map/ppermute | solution.py:22
  3.0 8.4 %collective-permute-start.2 = (s32[1,1,8]{2,1,0:T(1,128)}, s32[1,1,8]{2,1,0:T(1,128)S(1)}, u32[]{:S(2)}, u32[]{:S(2)}) collective-permute-start(s32[1,1,8]{2,1,0:T(1,128)} %map_any.1), channel_id=1, source_target_pairs={{0,24},{8,16},{16,8},{24,0},{1,25},{9,17},{17,9},{25,1},{2,26},{10... | collective-permute-start | bytes 104 | tf_op jit(solution)/shard_map/ppermute | solution.py:22
  5.5 5.9 %collective-permute-start.1 = (s32[1,1,8]{2,1,0:T(1,128)}, s32[1,1,8]{2,1,0:T(1,128)S(1)}, u32[]{:S(2)}, u32[]{:S(2)}) collective-permute-start(s32[1,1,8]{2,1,0:T(1,128)} %map_any.1), channel_id=1, source_target_pairs={{0,16},{8,24},{16,0},{24,8},{1,17},{9,25},{17,1},{25,9},{2,18},{10... | collective-permute-start | bytes 104 | tf_op jit(solution)/shard_map/ppermute | solution.py:22
  12.3 1.7 %collective-permute-start.3 = (f32[4,152,128]{2,1,0:T(8,128)S(1)}, f32[4,152,128]{2,1,0:T(8,128)S(1)}, u32[]{:S(2)}, u32[]{:S(2)}) collective-permute-start(f32[4,152,128]{2,1,0:T(8,128)S(1)} %get-tuple-element.55), channel_id=1, source_target_pairs={{0,1},{1,0},{2,3},{3,2},{4,5},{5,4},{6,7},{7,6},{8,9},{9,8},{10,11... | collective-permute-start | bytes 933896 | tf_op jit(solution)/shard_map/ppermute | solution.py:22
  14.2 3.8 %collective-permute-start.4 = (f32[4,784,128]{2,1,0:T(8,128)S(1)}, f32[4,784,128]{2,1,0:T(8,128)S(1)}, u32[]{:S(2)}, u32[]{:S(2)}) collective-permute-start(f32[4,784,128]{2,1,0:T(8,128)S(1)} %shard_map.52), channel_id=1, source_target_pairs={{0,1},{1,0},{2,3},{3,2},{4,5},{5,4},{6,7},{7,6},{8,9},{9,8},{10,11... | collective-permute-start | bytes 4816904 | tf_op jit(solution)/shard_map/ppermute | solution.py:22
  14.4 6.9 %collective-permute-start.5 = (f32[2,152,128]{2,1,0:T(8,128)S(1)}, f32[2,152,128]{2,1,0:T(8,128)S(1)}, u32[]{:S(2)}, u32[]{:S(2)}) collective-permute-start(f32[2,152,128]{2,1,0:T(8,128)S(1)} %shard_map.49.refs_0_), channel_id=1, source_target_pairs={{0,2},{1,3},{2,0},{3,1},{4,6},{5,7},{6,4},{7,5},{8,10},{9,11},{10,... | collective-permute-start | bytes 466952 | tf_op jit(solution)/shard_map/ppermute | solution.py:22
  16.0 9.2 %collective-permute-start.11 = (f32[2,152,128]{2,1,0:T(8,128)S(1)}, f32[2,152,128]{2,1,0:T(8,128)S(1)}, u32[]{:S(2)}, u32[]{:S(2)}) collective-permute-start(f32[2,152,128]{2,1,0:T(8,128)S(1)} %shard_map.50.refs_1_), channel_id=1, source_target_pairs={{0,4},{1,5},{2,6},{3,7},{4,0},{5,1},{6,2},{7,3},{8,12},{9,13},{10,... | collective-permute-start | bytes 466952 | tf_op jit(solution)/shard_map/ppermute | solution.py:22
  17.5 9.4 %collective-permute-start.13 = (f32[2,152,128]{2,1,0:T(8,128)S(1)}, f32[2,152,128]{2,1,0:T(8,128)S(1)}, u32[]{:S(2)}, u32[]{:S(2)}) collective-permute-start(f32[2,152,128]{2,1,0:T(8,128)S(1)} %shard_map.51.refs_2_), channel_id=1, source_target_pairs={{0,6},{1,7},{2,4},{3,5},{4,2},{5,3},{6,0},{7,1},{8,14},{9,15},{10,... | collective-permute-start | bytes 466952 | tf_op jit(solution)/shard_map/ppermute | solution.py:22
  21.4 7.8 %collective-permute-start.6 = (f32[2,200,128]{2,1,0:T(8,128)S(1)}, f32[2,200,128]{2,1,0:T(8,128)S(1)}, u32[]{:S(2)}, u32[]{:S(2)}) collective-permute-start(f32[2,200,128]{2,1,0:T(8,128)S(1)} %shard_map.53.refs_5_), channel_id=1, source_target_pairs={{0,2},{1,3},{2,0},{3,1},{4,6},{5,7},{6,4},{7,5},{8,10},{9,11},{10,... | collective-permute-start | bytes 614408 | tf_op jit(solution)/shard_map/ppermute | solution.py:22
  23.1 12.5 %collective-permute-start.10 = (f32[2,200,128]{2,1,0:T(8,128)S(1)}, f32[2,200,128]{2,1,0:T(8,128)S(1)}, u32[]{:S(2)}, u32[]{:S(2)}) collective-permute-start(f32[2,200,128]{2,1,0:T(8,128)S(1)} %shard_map.57.refs_6_), channel_id=1, source_target_pairs={{0,4},{1,5},{2,6},{3,7},{4,0},{5,1},{6,2},{7,3},{8,12},{9,13},{10,... | collective-permute-start | bytes 614408 | tf_op jit(solution)/shard_map/ppermute | solution.py:22
  25.2 11.7 %collective-permute-start.12 = (f32[2,200,128]{2,1,0:T(8,128)S(1)}, f32[2,200,128]{2,1,0:T(8,128)S(1)}, u32[]{:S(2)}, u32[]{:S(2)}) collective-permute-start(f32[2,200,128]{2,1,0:T(8,128)S(1)} %shard_map.58.refs_7_), channel_id=1, source_target_pairs={{0,6},{1,7},{2,4},{3,5},{4,2},{5,3},{6,0},{7,1},{8,14},{9,15},{10,... | collective-permute-start | bytes 614408 | tf_op jit(solution)/shard_map/ppermute | solution.py:22
  27.3 5.5 %collective-permute-start.14 = (f32[2,3,2,24,128]{4,3,2,1,0:T(8,128)S(1)}, f32[2,3,2,24,128]{4,3,2,1,0:T(8,128)S(1)}, u32[]{:S(2)}, u32[]{:S(2)}) collective-permute-start(f32[2,3,2,24,128]{4,3,2,1,0:T(8,128)S(1)} %pad_maximum_fusion.2), channel_id=1, source_target_pairs={{0,8},{8,0},{16,24},{24,16},{1,9},{9,1},{17,25},{25,17},{2,10},{10... | collective-permute-start | bytes 442376 | tf_op jit(solution)/shard_map/ppermute | solution.py:22
  29.2 9.8 %collective-permute-start.7 = (f32[2,200,128]{2,1,0:T(8,128)S(1)}, f32[2,200,128]{2,1,0:T(8,128)S(1)}, u32[]{:S(2)}, u32[]{:S(2)}) collective-permute-start(f32[2,200,128]{2,1,0:T(8,128)S(1)} %shard_map.54.refs_2_.refs_5_), channel_id=1, source_target_pairs={{0,2},{1,3},{2,0},{3,1},{4,6},{5,7},{6,4},{7,5},{8,10},{9,11},{10,... | collective-permute-start | bytes 614408 | tf_op jit(solution)/shard_map/ppermute | solution.py:22
  31.5 12.8 %collective-permute-start.20 = (f32[2,200,128]{2,1,0:T(8,128)S(1)}, f32[2,200,128]{2,1,0:T(8,128)S(1)}, u32[]{:S(2)}, u32[]{:S(2)}) collective-permute-start(f32[2,200,128]{2,1,0:T(8,128)S(1)} %shard_map.59.refs_3_.refs_6_), channel_id=1, source_target_pairs={{0,4},{1,5},{2,6},{3,7},{4,0},{5,1},{6,2},{7,3},{8,12},{9,13},{10,... | collective-permute-start | bytes 614408 | tf_op jit(solution)/shard_map/ppermute | solution.py:22
  32.8 7.2 %collective-permute-start.16 = (f32[1,3,2,24,128]{4,3,2,1,0:T(8,128)S(1)}, f32[1,3,2,24,128]{4,3,2,1,0:T(8,128)S(1)}, u32[]{:S(2)}, u32[]{:S(2)}) collective-permute-start(f32[1,3,2,24,128]{4,3,2,1,0:T(8,128)S(1)} %bitcast.22), channel_id=1, source_target_pairs={{0,16},{8,24},{16,0},{24,8},{1,17},{9,25},{17,1},{25,9},{2,18},{10... | collective-permute-start | bytes 221192 | tf_op jit(solution)/shard_map/ppermute | solution.py:22
  35.7 10.5 %collective-permute-start.21 = (f32[2,200,128]{2,1,0:T(8,128)S(1)}, f32[2,200,128]{2,1,0:T(8,128)S(1)}, u32[]{:S(2)}, u32[]{:S(2)}) collective-permute-start(f32[2,200,128]{2,1,0:T(8,128)S(1)} %shard_map.62.refs_7_), channel_id=1, source_target_pairs={{0,6},{1,7},{2,4},{3,5},{4,2},{5,3},{6,0},{7,1},{8,14},{9,15},{10,... | collective-permute-start | bytes 614408 | tf_op jit(solution)/shard_map/ppermute | solution.py:22
  37.3 5.7 %collective-permute-start.15 = (f32[2,3,2,32,128]{4,3,2,1,0:T(8,128)S(1)}, f32[2,3,2,32,128]{4,3,2,1,0:T(8,128)S(1)}, u32[]{:S(2)}, u32[]{:S(2)}) collective-permute-start(f32[2,3,2,32,128]{4,3,2,1,0:T(8,128)S(1)} %pad_maximum_fusion), channel_id=1, source_target_pairs={{0,8},{8,0},{16,24},{24,16},{1,9},{9,1},{17,25},{25,17},{2,10},{10... | collective-permute-start | bytes 589832 | tf_op jit(solution)/shard_map/ppermute | solution.py:22
  39.0 10.3 %collective-permute-start.8 = (f32[2,248,128]{2,1,0:T(8,128)S(1)}, f32[2,248,128]{2,1,0:T(8,128)S(1)}, u32[]{:S(2)}, u32[]{:S(2)}) collective-permute-start(f32[2,248,128]{2,1,0:T(8,128)S(1)} %shard_map.55.refs_2_.refs_5_), channel_id=1, source_target_pairs={{0,2},{1,3},{2,0},{3,1},{4,6},{5,7},{6,4},{7,5},{8,10},{9,11},{10,... | collective-permute-start | bytes 761864 | tf_op jit(solution)/shard_map/ppermute | solution.py:22
  39.9 14.3 %collective-permute-start.19 = (f32[2,248,128]{2,1,0:T(8,128)S(1)}, f32[2,248,128]{2,1,0:T(8,128)S(1)}, u32[]{:S(2)}, u32[]{:S(2)}) collective-permute-start(f32[2,248,128]{2,1,0:T(8,128)S(1)} %shard_map.64.refs_3_.refs_6_), channel_id=1, source_target_pairs={{0,4},{1,5},{2,6},{3,7},{4,0},{5,1},{6,2},{7,3},{8,12},{9,13},{10,... | collective-permute-start | bytes 761864 | tf_op jit(solution)/shard_map/ppermute | solution.py:22
  43.0 7.4 %collective-permute-start.17 = (f32[1,3,2,32,128]{4,3,2,1,0:T(8,128)S(1)}, f32[1,3,2,32,128]{4,3,2,1,0:T(8,128)S(1)}, u32[]{:S(2)}, u32[]{:S(2)}) collective-permute-start(f32[1,3,2,32,128]{4,3,2,1,0:T(8,128)S(1)} %bitcast.20), channel_id=1, source_target_pairs={{0,16},{8,24},{16,0},{24,8},{1,17},{9,25},{17,1},{25,9},{2,18},{10... | collective-permute-start | bytes 294920 | tf_op jit(solution)/shard_map/ppermute | solution.py:22
  44.4 11.6 %collective-permute-start.25 = (f32[2,248,128]{2,1,0:T(8,128)S(1)}, f32[2,248,128]{2,1,0:T(8,128)S(1)}, u32[]{:S(2)}, u32[]{:S(2)}) collective-permute-start(f32[2,248,128]{2,1,0:T(8,128)S(1)} %shard_map.67.refs_7_), channel_id=1, source_target_pairs={{0,6},{1,7},{2,4},{3,5},{4,2},{5,3},{6,0},{7,1},{8,14},{9,15},{10,... | collective-permute-start | bytes 761864 | tf_op jit(solution)/shard_map/ppermute | solution.py:22
  46.6 6.4 %collective-permute-start.22 = (f32[2,3,2,32,128]{4,3,2,1,0:T(8,128)S(1)}, f32[2,3,2,32,128]{4,3,2,1,0:T(8,128)S(1)}, u32[]{:S(2)}, u32[]{:S(2)}) collective-permute-start(f32[2,3,2,32,128]{4,3,2,1,0:T(8,128)S(1)} %pad_maximum_fusion.1), channel_id=1, source_target_pairs={{0,8},{8,0},{16,24},{24,16},{1,9},{9,1},{17,25},{25,17},{2,10},{10... | collective-permute-start | bytes 589832 | tf_op jit(solution)/shard_map/ppermute | solution.py:22
  49.3 7.9 %collective-permute-start.9 = (f32[2,136,128]{2,1,0:T(8,128)S(1)}, f32[2,136,128]{2,1,0:T(8,128)S(1)}, u32[]{:S(2)}, u32[]{:S(2)}) collective-permute-start(f32[2,136,128]{2,1,0:T(8,128)S(1)} %shard_map.56.refs_2_.refs_5_), channel_id=1, source_target_pairs={{0,2},{1,3},{2,0},{3,1},{4,6},{5,7},{6,4},{7,5},{8,10},{9,11},{10,... | collective-permute-start | bytes 417800 | tf_op jit(solution)/shard_map/ppermute | solution.py:22
  50.4 9.0 %collective-permute-start.18 = (f32[2,136,128]{2,1,0:T(8,128)S(1)}, f32[2,136,128]{2,1,0:T(8,128)S(1)}, u32[]{:S(2)}, u32[]{:S(2)}) collective-permute-start(f32[2,136,128]{2,1,0:T(8,128)S(1)} %shard_map.66.refs_3_.refs_6_), channel_id=1, source_target_pairs={{0,4},{1,5},{2,6},{3,7},{4,0},{5,1},{6,2},{7,3},{8,12},{9,13},{10,... | collective-permute-start | bytes 417800 | tf_op jit(solution)/shard_map/ppermute | solution.py:22
  53.0 9.5 %collective-permute-start.24 = (f32[1,3,2,32,128]{4,3,2,1,0:T(8,128)S(1)}, f32[1,3,2,32,128]{4,3,2,1,0:T(8,128)S(1)}, u32[]{:S(2)}, u32[]{:S(2)}) collective-permute-start(f32[1,3,2,32,128]{4,3,2,1,0:T(8,128)S(1)} %bitcast.21), channel_id=1, source_target_pairs={{0,16},{8,24},{16,0},{24,8},{1,17},{9,25},{17,1},{25,9},{2,18},{10... | collective-permute-start | bytes 294920 | tf_op jit(solution)/shard_map/ppermute | solution.py:22
  54.2 6.7 %collective-permute-start.23 = (f32[2,136,128]{2,1,0:T(8,128)S(1)}, f32[2,136,128]{2,1,0:T(8,128)S(1)}, u32[]{:S(2)}, u32[]{:S(2)}) collective-permute-start(f32[2,136,128]{2,1,0:T(8,128)S(1)} %shard_map.70.refs_7_), channel_id=1, source_target_pairs={{0,6},{1,7},{2,4},{3,5},{4,2},{5,3},{6,0},{7,1},{8,14},{9,15},{10,... | collective-permute-start | bytes 417800 | tf_op jit(solution)/shard_map/ppermute | solution.py:22
  56.4 7.4 %collective-permute-start.26 = (f32[3,2,40,128]{3,2,1,0:T(8,128)S(1)}, f32[3,2,40,128]{3,2,1,0:T(8,128)S(1)}, u32[]{:S(2)}, u32[]{:S(2)}) collective-permute-start(f32[3,2,40,128]{3,2,1,0:T(8,128)S(1)} %get-tuple-element.44), channel_id=1, source_target_pairs={{0,8},{8,0},{16,24},{24,16},{1,9},{9,1},{17,25},{25,17},{2,10},{10... | collective-permute-start | bytes 368648 | tf_op jit(solution)/shard_map/ppermute | solution.py:22
  57.2 11.3 %collective-permute-start.27 = (f32[3,2,40,128]{3,2,1,0:T(8,128)S(1)}, f32[3,2,40,128]{3,2,1,0:T(8,128)S(1)}, u32[]{:S(2)}, u32[]{:S(2)}) collective-permute-start(f32[3,2,40,128]{3,2,1,0:T(8,128)S(1)} %get-tuple-element.45), channel_id=1, source_target_pairs={{0,16},{8,24},{16,0},{24,8},{1,17},{9,25},{17,1},{25,9},{2,18},{10... | collective-permute-start | bytes 368648 | tf_op jit(solution)/shard_map/ppermute | solution.py:22
  59.5 9.0 %collective-permute-start.28 = (f32[3,2,40,128]{3,2,1,0:T(8,128)S(1)}, f32[3,2,40,128]{3,2,1,0:T(8,128)S(1)}, u32[]{:S(2)}, u32[]{:S(2)}) collective-permute-start(f32[3,2,40,128]{3,2,1,0:T(8,128)S(1)} %get-tuple-element.46), channel_id=1, source_target_pairs={{0,24},{8,16},{16,8},{24,0},{1,25},{9,17},{17,9},{25,1},{2,26},{10... | collective-permute-start | bytes 368648 | tf_op jit(solution)/shard_map/ppermute | solution.py:22
